TPU v7x, 32 devices: a whole 2x2x4 slice. The times are simulated.
32 devices in a mesh: dp: 2 (over x), row: 4 (over z), col: 4 (over y, core).
Axes of the slice: x: 2, y: 2, z: 4, core: 2. Of those that a mesh axis runs over, the one named last changes fastest.
Arguments:
- layer_input: bfloat16 [6144, 2048], P(('dp', 'col'), 'row'), may hold values from -16 to 16
- gains: bfloat16 [4, 2048], replicated, may hold values from 0.25 to 1.75
- qkv_weight: bfloat16 [2048, 3, 2048], P('row', None, 'col'), may hold values from -0.125 to 0.125
- output_weight: bfloat16 [2048, 2048], P('col', 'row'), may hold values from -2 to 2
- router_weight: bfloat16 [2048, 32], replicated, may hold values from -0.0625 to 0.0625
- expand_weight: bfloat16 [32, 2048, 2048], P(('row', 'col')), may hold values from -0.125 to 0.125
- reduce_weight: bfloat16 [32, 1024, 2048], P(('row', 'col')), may hold values from -3 to 3
- routes: int32 [6144, 8], P(('dp', 'col')), may hold values from 0 to 31, all different within a row
- drop_order: int32 [6144], P(('dp', 'col')), may hold values from 0 to 3071
- prefix_len: int32 [2], P('dp'), may hold values from 307 to 1536
- cotangent: bfloat16 [6144, 2048], P(('dp', 'col'), 'row'), may hold values from -6 to 6
Outputs:
- layer_output: bfloat16 [6144, 2048], P(('dp', 'col'), 'row')
- input_grad: bfloat16 [6144, 2048], P(('dp', 'col'), 'row')
- gains_grad: float32 [4, 2048], replicated
- qkv_grad: float32 [4, 512, 3, 2048], P('row', 'dp', None, 'col')
- output_grad: float32 [4, 512, 2048], P('col', 'dp', 'row')
- router_grad: float32 [2048, 32], replicated
- expand_grad: float32 [32, 2048, 2048], P(('row', 'col'), 'dp')
- reduce_grad: float32 [32, 1024, 2048], P(('row', 'col'), 'dp')
Inputs may be any that keep to these rules, and one draw needn't show every extreme that they name: `routes`: each row names 8 different experts.
All inputs are finite; a program needn't handle non-finite values.
Results may differ from a plain program's by a relative error of at most 0.02.
The roundings to bfloat16 on the way count: a program that leaves them out, or rounds other values in their place, can miss the bound.
Values may be sent and summed in bfloat16 or wider, within the bound.
No kernel may reach another device: no remote copies, remote signals or barrier semaphores. Data moves between devices by JAX's collectives and lax.ppermute only.
A program may use at most 320 MiB of HBM per device.

v0:
```python
import jax
import jax.numpy as jnp
from jax import lax
from jax.sharding import PartitionSpec as P

D = 2048
HD = 128
F = 1024
TOP = 8
QBLK = 768


norm_epsilon = 1e-05
rope_base = 10000.0


def feature_sums(values):
    return lax.psum(values, "row")


def head_sums(first_half, second_half):
    return lax.psum((first_half, second_half), "col")


def gather_cols(block_rows):
    return lax.all_gather(block_rows, "col", axis=0, tiled=True)


def gather_rows(stacked):
    return lax.all_gather(stacked, "row", axis=1, tiled=True)


def reduce_rows(term_fn, rows_here):
    return lax.psum_scatter(
        term_fn(jnp.int32(0), lax.axis_size("row") * rows_here),
        "row",
        scatter_dimension=0,
        tiled=True,
    )


def reduce_cols(term_fn, rows_here):
    return lax.psum_scatter(
        term_fn(jnp.int32(0), lax.axis_size("col") * rows_here),
        "col",
        scatter_dimension=0,
        tiled=True,
    )


def to_tokens(block_rows):
    return lax.all_to_all(block_rows, "row", split_axis=0, concat_axis=1, tiled=True)


def to_features(token_rows):
    return lax.all_to_all(token_rows, "row", split_axis=1, concat_axis=0, tiled=True)


def send_slots(slots):
    return lax.all_to_all(slots, ("row", "col"), split_axis=0, concat_axis=0, tiled=True)


def return_slots(slots):
    return lax.all_to_all(slots, ("row", "col"), split_axis=0, concat_axis=0, tiled=True)


def rope_tables(positions):
    half_width = HD // 2
    frequency = rope_base ** (-2.0 * jnp.arange(half_width, dtype=jnp.float32) / HD)
    angles = positions.astype(jnp.float32)[:, None] * frequency[None, :]
    return (jnp.cos(angles)[:, None, :], jnp.sin(angles)[:, None, :])


def rotate(values, cosine, sine_part):
    half_width = values.shape[-1] // 2
    first_half = values[..., :half_width]
    second_half = values[..., half_width:]
    return jnp.concatenate(
        [
            first_half * cosine - second_half * sine_part,
            second_half * cosine + first_half * sine_part,
        ],
        axis=-1,
    )


def unrotate(gradient, cosine, sine_part):
    half_width = gradient.shape[-1] // 2
    first_half = gradient[..., :half_width]
    second_half = gradient[..., half_width:]
    return jnp.concatenate(
        [
            first_half * cosine + second_half * sine_part,
            second_half * cosine - first_half * sine_part,
        ],
        axis=-1,
    )


def norm_back(values, inverse, gain_row, upstream, dot_total):
    scaled = upstream * gain_row
    return inverse[:, None] * scaled - values * (inverse**3 * dot_total / D)[:, None]


def placed(term, offset):
    return lax.dynamic_update_slice(jnp.zeros((D,), jnp.float32), term, (offset,))


def on_device(
    layer_input,
    gains,
    qkv_weight,
    output_weight,
    router_weight,
    expand_weight,
    reduce_weight,
    routes,
    drop_order,
    prefix_len,
    cotangent,
):
    row_rank = lax.axis_index("row")
    col_rank = lax.axis_index("col")
    row_devices = lax.axis_size("row")
    col_devices = lax.axis_size("col")
    res_rows, row_width = layer_input.shape
    col_width = qkv_weight.shape[2]
    seq_len = res_rows * col_devices
    query_rows = seq_len // row_devices
    tok_rows = res_rows // row_devices
    local_heads = col_width // HD
    expert_count = router_weight.shape[1]
    local_experts = expand_weight.shape[0]
    capacity = tok_rows * TOP // expert_count
    slot_count = expert_count * capacity
    group_size = row_devices * col_devices
    per_device = local_experts * capacity
    score_scale = HD ** (-0.5)
    gain_rows = gains.astype(jnp.float32)
    gain_first = lax.dynamic_slice_in_dim(gain_rows[0], row_rank * row_width, row_width)
    gain_query = lax.dynamic_slice_in_dim(gain_rows[1], col_rank * col_width, col_width)
    gain_key = lax.dynamic_slice_in_dim(gain_rows[2], col_rank * col_width, col_width)
    gain_second = lax.dynamic_slice_in_dim(gain_rows[3], row_rank * row_width, row_width)
    inputs = layer_input.astype(jnp.float32)
    inv_first = lax.rsqrt(feature_sums(jnp.sum(inputs * inputs, axis=1)) / D + norm_epsilon)
    first_low = (inputs * inv_first[:, None] * gain_first).astype(jnp.bfloat16)
    gathered = gather_cols(first_low)
    qkv_flat = qkv_weight.reshape(row_width, 3 * col_width)

    def qkv_term(first_row, row_number):
        return jnp.dot(gathered, qkv_flat, preferred_element_type=jnp.float32)

    projected = reduce_rows(qkv_term, query_rows)
    query_raw = projected[:, :col_width]
    key_raw = projected[:, col_width : 2 * col_width]
    value_raw = projected[:, 2 * col_width :]
    sq_query, sq_key = head_sums(
        jnp.sum(query_raw * query_raw, axis=1), jnp.sum(key_raw * key_raw, axis=1)
    )
    inv_query = lax.rsqrt(sq_query / D + norm_epsilon)
    inv_key = lax.rsqrt(sq_key / D + norm_epsilon)
    cosine, sine_part = rope_tables(row_rank * query_rows + jnp.arange(query_rows))
    head_shape = (query_rows, local_heads, HD)
    query_low = rotate(
        (query_raw * inv_query[:, None] * gain_query).reshape(head_shape), cosine, sine_part
    ).astype(jnp.bfloat16)
    key_low = rotate(
        (key_raw * inv_key[:, None] * gain_key).reshape(head_shape), cosine, sine_part
    ).astype(jnp.bfloat16)
    value_low = value_raw.astype(jnp.bfloat16)
    kv_pair = jnp.stack([key_low.reshape(query_rows, col_width), value_low])
    gathered_kv = gather_rows(kv_pair)
    key_heads = gathered_kv[0].reshape(seq_len, local_heads, HD)
    value_heads = gathered_kv[1].reshape(seq_len, local_heads, HD)
    key_pos = jnp.arange(seq_len)
    block_starts = jnp.arange(query_rows // QBLK) * QBLK
    prefix = prefix_len[0]

    def block_scores(query_block, keys_here, block_start):
        query_pos = row_rank * query_rows + block_start + jnp.arange(QBLK)
        allowed = (key_pos[None, :] <= query_pos[:, None]) | (key_pos[None, :] < prefix)
        scores = (
            jnp.einsum("qhd,khd->hqk", query_block, keys_here, preferred_element_type=jnp.float32)
            * score_scale
        )
        return jnp.where(allowed[None], scores, -1e30)

    def attend(block_start):
        scores = block_scores(query_low, key_heads, block_start)
        peak = jnp.max(scores, axis=-1, keepdims=True)
        log_total = peak + jnp.log(jnp.sum(jnp.exp(scores - peak), axis=-1, keepdims=True))
        weights = jnp.exp(scores - log_total).astype(jnp.bfloat16)
        mixed_heads = jnp.einsum(
            "hqk,khd->qhd", weights, value_heads, preferred_element_type=jnp.float32
        )
        return (mixed_heads, log_total)

    mixed_blocks, log_totals = lax.map(attend, block_starts)
    attn_low = mixed_blocks.reshape(query_rows, col_width).astype(jnp.bfloat16)
    attn_all = gather_rows(attn_low[None])[0]

    def output_term(first_row, row_number):
        return jnp.dot(attn_all, output_weight, preferred_element_type=jnp.float32)

    residual = inputs + reduce_cols(output_term, res_rows)
    inv_second = lax.rsqrt(feature_sums(jnp.sum(residual * residual, axis=1)) / D + norm_epsilon)
    second_low = (residual * inv_second[:, None] * gain_second).astype(jnp.bfloat16)
    token_feats = to_tokens(second_low)
    own_routes = lax.dynamic_slice_in_dim(routes, row_rank * tok_rows, tok_rows, 0)
    drop_rank = lax.dynamic_slice_in_dim(drop_order, row_rank * tok_rows, tok_rows, 0)
    logits = jnp.dot(token_feats, router_weight, preferred_element_type=jnp.float32)
    router_probs = jax.nn.softmax(logits, axis=-1)
    chosen = own_routes[:, :, None] == jnp.arange(expert_count)[None, None, :]
    gate_vals = jnp.sum(jnp.where(chosen, router_probs[:, None, :], 0.0), axis=-1)
    routed = jnp.sum(chosen, axis=1).astype(jnp.bfloat16)
    token_index = jnp.arange(tok_rows)
    earlier = (drop_rank[None, :] < drop_rank[:, None]) | (
        drop_rank[None, :] == drop_rank[:, None]
    ) & (token_index[None, :] < token_index[:, None])
    counts = jnp.dot(earlier.astype(jnp.bfloat16), routed, preferred_element_type=jnp.float32)
    position = jnp.sum(jnp.where(chosen, counts[:, None, :], 0.0), axis=-1).astype(jnp.int32)
    kept_mask = position < capacity
    slot_index = own_routes * capacity + position
    hits = (slot_index[:, :, None] == jnp.arange(slot_count)[None, None, :]) & kept_mask[:, :, None]
    dispatch = jnp.sum(hits, axis=1).astype(jnp.bfloat16)
    gate_weight = jnp.where(kept_mask, gate_vals, 0.0)
    slot_gate = jnp.sum(jnp.where(hits, gate_weight[:, :, None], 0.0), axis=(0, 1))
    slot_buffer = jnp.einsum(
        "ts,td->sd", dispatch, token_feats, preferred_element_type=jnp.float32
    ).astype(jnp.bfloat16)
    received = send_slots(slot_buffer.reshape(group_size, per_device, D))
    slot_rows = received.reshape(group_size, local_experts, capacity, D)
    gate_up = jnp.einsum(
        "secd,edf->secf", slot_rows, expand_weight, preferred_element_type=jnp.float32
    )
    gate_pre = gate_up[..., :F]
    up_pre = gate_up[..., F:]
    hidden = (jax.nn.silu(gate_pre) * up_pre).astype(jnp.bfloat16)
    expert_out = jnp.einsum(
        "secf,efd->secd", hidden, reduce_weight, preferred_element_type=jnp.float32
    ).astype(jnp.bfloat16)
    returned = return_slots(expert_out.reshape(group_size, per_device, D)).reshape(slot_count, D)
    picked = returned[jnp.where(kept_mask, slot_index, 0)]
    moe_tokens = jnp.zeros((tok_rows, D), jnp.float32)
    for pick_index in range(TOP):
        moe_tokens = moe_tokens + gate_weight[:, pick_index, None] * picked[:, pick_index].astype(
            jnp.float32
        )
    moe_cols = to_features(moe_tokens)
    layer_output = (residual + moe_cols).astype(jnp.bfloat16)
    upstream = cotangent.astype(jnp.float32)
    grad_tokens = to_tokens(cotangent)
    grad_gate = jnp.where(
        kept_mask,
        jnp.einsum("td,tkd->tk", grad_tokens, picked, preferred_element_type=jnp.float32),
        0.0,
    )
    grad_slots = jnp.einsum("ts,td->sd", dispatch, grad_tokens, preferred_element_type=jnp.float32)
    grad_out_slots = (
        (grad_slots * slot_gate[:, None]).astype(jnp.bfloat16).reshape(group_size, per_device, D)
    )
    grad_expert = send_slots(grad_out_slots)
    grad_expert = grad_expert.reshape(group_size, local_experts, capacity, D)
    grad_hidden = jnp.einsum(
        "secd,efd->secf", grad_expert, reduce_weight, preferred_element_type=jnp.float32
    )
    sigmoid_gate = jax.nn.sigmoid(gate_pre)
    grad_gate_pre = (
        grad_hidden * up_pre * sigmoid_gate * (1.0 + gate_pre * (1.0 - sigmoid_gate))
    ).astype(jnp.bfloat16)
    grad_up_pre = (grad_hidden * jax.nn.silu(gate_pre)).astype(jnp.bfloat16)
    grad_gate_up = jnp.concatenate([grad_gate_pre, grad_up_pre], axis=-1)
    reduce_term = jnp.einsum(
        "secf,secd->efd", hidden, grad_expert, preferred_element_type=jnp.float32
    )
    expand_term = jnp.einsum(
        "secd,secf->edf", slot_rows, grad_gate_up, preferred_element_type=jnp.float32
    )
    grad_slot_in = jnp.einsum(
        "secf,edf->secd", grad_gate_up, expand_weight, preferred_element_type=jnp.float32
    ).astype(jnp.bfloat16)
    grad_back = return_slots(grad_slot_in.reshape(group_size, per_device, D)).reshape(slot_count, D)
    grad_feats = jnp.einsum("ts,sd->td", dispatch, grad_back, preferred_element_type=jnp.float32)
    grad_probs = jnp.sum(jnp.where(chosen, grad_gate[:, :, None], 0.0), axis=1)
    grad_logits = (
        router_probs * (grad_probs - jnp.sum(router_probs * grad_probs, axis=-1, keepdims=True))
    ).astype(jnp.bfloat16)
    router_term = jnp.einsum(
        "td,te->de", token_feats, grad_logits, preferred_element_type=jnp.float32
    )
    grad_feats = grad_feats + jnp.einsum(
        "te,de->td", grad_logits, router_weight, preferred_element_type=jnp.float32
    )
    grad_second = to_features(grad_feats)
    dot_second = feature_sums(jnp.sum(grad_second * gain_second * residual, axis=1))
    grad_resid = upstream + norm_back(residual, inv_second, gain_second, grad_second, dot_second)
    gain_second_term = jnp.sum(grad_second * residual * inv_second[:, None], axis=0)
    grad_branch = gather_cols(grad_resid.astype(jnp.bfloat16))
    output_term_grad = jnp.einsum(
        "sc,sr->cr", attn_all, grad_branch, preferred_element_type=jnp.float32
    )

    def head_term(first_row, row_number):
        return jnp.einsum(
            "sr,cr->sc", grad_branch, output_weight, preferred_element_type=jnp.float32
        )

    grad_attn = reduce_rows(head_term, query_rows).astype(jnp.bfloat16).reshape(head_shape)
    keys_back = gathered_kv[0].reshape(seq_len, local_heads, HD)
    values_back = gathered_kv[1].reshape(seq_len, local_heads, HD)

    def back_block(running, packed):
        grad_keys, grad_values = running
        block_start, log_total = packed
        scores = block_scores(query_low, keys_back, block_start)
        weights = jnp.exp(scores - log_total)
        grad_weights = jnp.einsum(
            "qhd,khd->hqk", grad_attn, values_back, preferred_element_type=jnp.float32
        )
        centre = jnp.sum(weights * grad_weights, axis=-1, keepdims=True)
        grad_scores = (weights * (grad_weights - centre)).astype(jnp.bfloat16)
        grad_query = (
            jnp.einsum("hqk,khd->qhd", grad_scores, keys_back, preferred_element_type=jnp.float32)
            * score_scale
        )
        grad_keys = (
            grad_keys
            + jnp.einsum("hqk,qhd->khd", grad_scores, query_low, preferred_element_type=jnp.float32)
            * score_scale
        )
        grad_values = grad_values + jnp.einsum(
            "hqk,qhd->khd",
            weights.astype(jnp.bfloat16),
            grad_attn,
            preferred_element_type=jnp.float32,
        )
        return ((grad_keys, grad_values), grad_query)

    zero_kv = jnp.zeros((seq_len, local_heads, HD), jnp.float32)
    (grad_keys_all, grad_values_all), grad_query_blocks = lax.scan(
        back_block, (zero_kv, zero_kv), (block_starts, log_totals)
    )
    grad_key_rot, grad_value = (
        lax.psum_scatter(
            grad_keys_all.reshape(seq_len, col_width), "row", scatter_dimension=0, tiled=True
        ),
        lax.psum_scatter(
            grad_values_all.reshape(seq_len, col_width), "row", scatter_dimension=0, tiled=True
        ),
    )
    grad_qnorm = unrotate(grad_query_blocks.reshape(head_shape), cosine, sine_part).reshape(
        query_rows, col_width
    )
    grad_knorm = unrotate(grad_key_rot.reshape(head_shape), cosine, sine_part).reshape(
        query_rows, col_width
    )
    dot_query, dot_key = head_sums(
        jnp.sum(grad_qnorm * gain_query * query_raw, axis=1),
        jnp.sum(grad_knorm * gain_key * key_raw, axis=1),
    )
    grad_qraw = norm_back(query_raw, inv_query, gain_query, grad_qnorm, dot_query)
    grad_kraw = norm_back(key_raw, inv_key, gain_key, grad_knorm, dot_key)
    gain_query_term = jnp.sum(grad_qnorm * query_raw * inv_query[:, None], axis=0)
    gain_key_term = jnp.sum(grad_knorm * key_raw * inv_key[:, None], axis=0)
    grad_qkv_all = gather_rows(jnp.stack([grad_qraw, grad_kraw, grad_value]).astype(jnp.bfloat16))
    qkv_term_grad = jnp.einsum(
        "sr,jsc->rjc", gathered, grad_qkv_all, preferred_element_type=jnp.float32
    )

    def feature_term(first_row, row_number):
        return jnp.einsum(
            "jsc,rjc->sr", grad_qkv_all, qkv_weight, preferred_element_type=jnp.float32
        )

    grad_first = reduce_cols(feature_term, res_rows)
    dot_first = feature_sums(jnp.sum(grad_first * gain_first * inputs, axis=1))
    input_grad = grad_resid + norm_back(inputs, inv_first, gain_first, grad_first, dot_first)
    gain_first_term = jnp.sum(grad_first * inputs * inv_first[:, None], axis=0)
    qkv_part, output_part, expand_part, reduce_part = (
        lax.psum_scatter(qkv_term_grad[None], "dp", scatter_dimension=1, tiled=True),
        lax.psum_scatter(output_term_grad[None], "dp", scatter_dimension=1, tiled=True),
        lax.psum_scatter(expand_term, "dp", scatter_dimension=1, tiled=True),
        lax.psum_scatter(reduce_term, "dp", scatter_dimension=1, tiled=True),
    )
    gain_terms = jnp.stack(
        [
            placed(gain_first_term, row_rank * row_width),
            placed(gain_query_term, col_rank * col_width),
            placed(gain_key_term, col_rank * col_width),
            placed(gain_second_term, row_rank * row_width),
        ]
    )
    gain_total, router_total = lax.psum((gain_terms, router_term), ("dp", "row", "col"))
    return (
        layer_output,
        input_grad.astype(jnp.bfloat16),
        gain_total,
        qkv_part,
        output_part,
        router_total,
        expand_part,
        reduce_part,
    )


def solution(mesh):
    return jax.shard_map(
        on_device,
        mesh=mesh,
        in_specs=(
            P(("dp", "col"), "row"),
            P(),
            P("row", None, "col"),
            P("col", "row"),
            P(),
            P(("row", "col"), None, None),
            P(("row", "col"), None, None),
            P(("dp", "col"), None),
            P(("dp", "col")),
            P("dp"),
            P(("dp", "col"), "row"),
        ),
        out_specs=(
            P(("dp", "col"), "row"),
            P(("dp", "col"), "row"),
            P(),
            P("row", "dp", None, "col"),
            P("col", "dp", "row"),
            P(),
            P(("row", "col"), "dp", None),
            P(("row", "col"), "dp", None),
        ),
        check_vma=False,
    )
```

profile of v0, /device:TPU:0, one launch (start us, length us, event | category | flops | bytes accessed | tf_op | source)
XLA Modules:
  0.0 2993.7 jit_solution(4041286990077838577)
XLA Ops:
  27.6 25.3 all-gather.6.cloned.1.call-done
  65.4 312.4 %reduce-scatter.11.cloned.1.call-done = f32[768,1536]{1,0:T(8,128)} async-done(((f32[3072,1536]{1,0:T(8,128)}), f32[768,1536]{1,0:T(8,128)}) %reduce-scatter.11.cloned.1.call-update) | async-done | bytes 4718608 | tf_op jit(solution)/shard_map/reduce_scatter | solution.py:34
  408.1 112.9 %all-gather.8.cloned.1.call-done = bf16[2,3072,512]{2,1,0:T(8,128)(2,1)} async-done(((bf16[2,768,512]{2,1,0:T(8,128)(2,1)}), bf16[2,3072,512]{2,1,0:T(8,128)(2,1)}) %all-gather.8.cloned.1.call-update) | async-done | bytes 6291472 | tf_op jit(solution)/shard_map/all_gather | solution.py:30
  591.0 61.7 %all-gather.10.cloned.1.call-done = bf16[1,3072,512]{1,2,0:T(8,128)(2,1)} async-done(((bf16[1,768,512]{1,2,0:T(8,128)(2,1)}), bf16[1,3072,512]{1,2,0:T(8,128)(2,1)}) %all-gather.10.cloned.1.call-update) | async-done | bytes 3145744 | tf_op jit(solution)/shard_map/all_gather | solution.py:30
  659.2 57.2 %reduce-scatter.13.cloned.1.call-done = f32[768,512]{1,0:T(8,128)} async-done(((f32[3072,512]{1,0:T(8,128)}), f32[768,512]{1,0:T(8,128)}) %reduce-scatter.13.cloned.1.call-update) | async-done | bytes 1572880 | tf_op jit(solution)/shard_map/reduce_scatter | solution.py:43
  766.2 140.6 %all_to_all.93 = bf16[16,96,2048]{2,1,0:T(8,128)(2,1)} all-to-all(bf16[16,96,2048]{2,1,0:T(8,128)(2,1)S(1)} %bitcast.230), channel_id=1, replica_groups=mesh['dp'=2,'row'=4,'col'=4] {'row','col'}, dimensions={0} | all-to-all | bytes 12582912 | tf_op jit(solution)/shard_map/all_to_all | solution.py:60
  972.2 101.0 %all-to-all-done.2 = bf16[16,96,2048]{2,1,0:T(8,128)(2,1)} async-done(((bf16[16,96,2048]{2,1,0:T(8,128)(2,1)}), bf16[16,96,2048]{2,1,0:T(8,128)(2,1)}, u32[]{:S(2)}, u32[]{:S(2)}) %all-to-all-start.2) | async-done | bytes 6291488 | tf_op jit(solution)/shard_map/all_to_all | solution.py:64
  1109.1 165.6 %all_to_all.94 = bf16[16,96,2048]{2,1,0:T(8,128)(2,1)} all-to-all(bf16[16,96,2048]{2,1,0:T(8,128)(2,1)S(1)} %bitcast.245), channel_id=1, replica_groups=mesh['dp'=2,'row'=4,'col'=4] {'row','col'}, dimensions={0} | all-to-all | bytes 12582912 | tf_op jit(solution)/shard_map/all_to_all | solution.py:60
  1322.7 114.1 %all-to-all-done.6 = bf16[16,96,2048]{2,1,0:T(8,128)(2,1)} async-done(((bf16[16,96,2048]{2,1,0:T(8,128)(2,1)}), bf16[16,96,2048]{2,1,0:T(8,128)(2,1)}, u32[]{:S(2)}, u32[]{:S(2)}) %all-to-all-start.6) | async-done | bytes 6291488 | tf_op jit(solution)/shard_map/all_to_all | solution.py:64
  1441.5 64.2 %all_to_all.95 = f32[192,4,512]{2,0,1:T(8,128)S(1)} all-to-all(f32[192,4,512]{2,0,1:T(8,128)S(1)} %bitcast.247), channel_id=1, replica_groups=mesh['dp'=2,'row'=4,'col'=4] {'row'}, dimensions={1} | all-to-all | bytes 3145728 | tf_op jit(solution)/shard_map/all_to_all | solution.py:56
  1519.5 27.0 all-gather.12.cloned.1.call-done
  1553.0 110.8 %reduce-scatter.15.cloned.1.call-done = f32[768,512]{1,0:T(8,128)} async-done(((f32[3072,512]{1,0:T(8,128)}), f32[768,512]{1,0:T(8,128)}) %reduce-scatter.15.cloned.1.call-update) | async-done | bytes 1572880 | tf_op jit(solution)/shard_map/reduce_scatter | solution.py:34
  1668.5 31.5 %multiply_reduce_fusion = (f32[4,768]{1,0:T(4,128)S(1)}, f32[4,768,3072]{2,1,0:T(8,128)}) fusion(f32[4,768,3072]{2,1,0:T(8,128)} %get-tuple-element.145, f32[4,768]{1,0:T(4,128)S(1)} %copy-done.26, pred[768,3072]{1,0:T(8,128)(4,1)S(1)} %copy-done.3, bf16[768,4,128]{0,2,1:T(8,128)(2,1)} %bitcast.248, bf16[3072,4,128]{2,1,0:T(4,128)(2,1)} %reshape_squeeze.8), kind=kOutput, calls=%fused_computation.2 | convolution fusion | flops 2463101952 | bytes 81813504 | tf_op jit(solution)/shard_map/while/body/eval_jaxpr/qhd,khd->hqk/dot_general | solution.py:317
  1700.0 31.4 %multiply_convert_fusion = bf16[4,768,3072]{2,1,0:T(8,128)(2,1)} fusion(f32[4,768,3072]{2,1,0:T(8,128)} %get-tuple-element.149, f32[4,768,3072]{2,1,0:T(8,128)} %get-tuple-element.145, f32[4,768]{1,0:T(4,128)S(1)} %get-tuple-element.148, f32[4,768]{1,0:T(4,128)S(1)} %copy-done.26, pred[768,3072]{1,0:T(8,128)(4,1)S(1)} %copy-done.3), kind=kLoop, calls=%fused_computation.1 | loop fusion | flops 56623104 | bytes 96755712 | tf_op jit(solution)/shard_map/while/body/eval_jaxpr/convert_element_type | solution.py:321
  1780.9 74.5 %reduce-scatter.17.cloned.1.call-done = f32[768,512]{0,1:T(8,128)} async-done(((f32[3072,512]{0,1:T(8,128)}), f32[768,512]{0,1:T(8,128)}) %reduce-scatter.17.cloned.1.call-update) | async-done | bytes 1572880 | tf_op jit(solution)/shard_map/reduce_scatter | solution.py:344
  1874.0 95.6 %reduce-scatter.19.cloned.1.call-done = f32[768,512]{1,0:T(8,128)} async-done(((f32[3072,512]{1,0:T(8,128)}), f32[768,512]{1,0:T(8,128)}) %reduce-scatter.19.cloned.1.call-update) | async-done | bytes 1572880 | tf_op jit(solution)/shard_map/reduce_scatter | solution.py:347
  1976.8 167.4 %all-gather.14.cloned.1.call-done = bf16[3,3072,512]{2,1,0:T(8,128)(2,1)} async-done(((bf16[3,768,512]{2,1,0:T(8,128)(2,1)}), bf16[3,3072,512]{2,1,0:T(8,128)(2,1)}) %all-gather.14.cloned.1.call-update) | async-done | bytes 9437200 | tf_op jit(solution)/shard_map/all_gather | solution.py:30
  2188.9 23.2 convolution_bitcast_fusion
  2212.0 31.8 %fusion.99 = (bf16[192,1,2048]{2,1,0:T(2,128)(2,1)S(1)}, bf16[192,1,2048]{2,1,0:T(2,128)(2,1)}, bf16[192,1,2048]{2,1,0:T(2,128)(2,1)}, bf16[192,1,2048]{2,1,0:T(...) fusion(bf16[192,8,2048]{2,1,0:T(8,128)(2,1)} %bitcast.229), kind=kLoop, calls=%fused_computation.197 | loop fusion | bytes 12582912 | tf_op jit(solution)/shard_map/slice | solution.py:246
  2306.9 30.4 %psum.77 = f32[768]{0:T(1024)S(1)} all-reduce(f32[768]{0:T(1024)S(1)} %get-tuple-element.70), channel_id=1, replica_groups=mesh['dp'=2,'row'=4,'col'=4] {'row'}, use_global_device_ids=true, to_apply=%region_33.34 | all-reduce | flops 768 | bytes 6144 | tf_op jit(solution)/shard_map/psum | solution.py:18
  2337.4 48.1 %psum.78 = f32[4,2048]{1,0:T(4,128)} all-reduce(f32[4,2048]{1,0:T(4,128)S(1)} %pad_maximum_fusion.7), channel_id=1, replica_groups=mesh['dp'=2,'row'=4,'col'=4] {'dp','row','col'}, use_global_device_ids=true, to_apply=%region_38.39 | all-reduce | flops 8192 | bytes 65536 | tf_op jit(solution)/shard_map/psum | solution.py:393
  2389.5 177.7 %reduce-scatter.29.cloned.1.call-done = f32[2,512,2048]{2,1,0:T(8,128)} async-done(((f32[2,1024,2048]{2,1,0:T(8,128)}), f32[2,512,2048]{2,1,0:T(8,128)}) %reduce-scatter.29.cloned.1.call-update) | async-done | bytes 8388624 | tf_op jit(solution)/shard_map/reduce_scatter | solution.py:383
  2567.2 46.1 %reduce-scatter.23.cloned.1.call-done = f32[1,256,3,512]{3,1,2,0:T(8,128)} async-done(((f32[1,512,3,512]{3,1,2,0:T(8,128)}), f32[1,256,3,512]{3,1,2,0:T(8,128)}) %reduce-scatter.23.cloned.1.call-update) | async-done | bytes 1572880 | tf_op jit(solution)/shard_map/reduce_scatter | solution.py:380
  2613.4 371.7 %reduce-scatter.27.cloned.1.call-done = f32[2,1024,2048]{2,1,0:T(8,128)} async-done(((f32[2,2048,2048]{2,1,0:T(8,128)}), f32[2,1024,2048]{2,1,0:T(8,128)}) %reduce-scatter.27.cloned.1.call-update) | async-done | bytes 16777232 | tf_op jit(solution)/shard_map/reduce_scatter | solution.py:382
  (327 shorter events, 555.5 us)
Async XLA Ops:
  7.2 645.6 %copy-start = (bf16[512,512]{1,0:T(8,128)(2,1)S(1)}, bf16[512,512]{1,0:T(8,128)(2,1)}, u32[]{:S(2)}) copy-start(bf16[512,512]{1,0:T(8,128)(2,1)} %param.14) | copy-start | bytes 1572868
  7.2 45.7 %all-gather.6.cloned.1.call-start = ((), (), s32[]{:S(2)}) async-start(), calls=%async_computation.18 | async-start | bytes 3932160 | tf_op jit(solution)/shard_map/all_gather | solution.py:26
  26.0 351.8 %reduce-scatter.11.cloned.1.call-start = ((), (), s32[]{:S(2)}) async-start(), calls=%async_computation.19 | async-start | bytes 23592960 | tf_op jit(solution)/shard_map/reduce_scatter | solution.py:34
  63.8 457.1 %all-gather.8.cloned.1.call-start = ((), (), s32[]{:S(2)}) async-start(), calls=%async_computation.20 | async-start | bytes 7864320 | tf_op jit(solution)/shard_map/all_gather | solution.py:30
  404.8 247.9 %all-gather.10.cloned.1.call-start = ((), (), s32[]{:S(2)}) async-start(), calls=%async_computation.21 | async-start | bytes 3932160 | tf_op jit(solution)/shard_map/all_gather | solution.py:30
  590.9 125.5 %reduce-scatter.13.cloned.1.call-start = ((), (), s32[]{:S(2)}) async-start(), calls=%async_computation.22 | async-start | bytes 7864320 | tf_op jit(solution)/shard_map/reduce_scatter | solution.py:43
  718.1 798.6 %copy-start.4 = (f32[768,512]{1,0:T(8,128)}, f32[768,512]{1,0:T(8,128)S(1)}, u32[]{:S(2)}) copy-start(f32[768,512]{1,0:T(8,128)S(1)} %get-tuple-element.93) | copy-start | bytes 4718596
  731.5 31.6 %all-to-all-start = ((bf16[4,192,512]{2,1,0:T(8,128)(2,1)}), bf16[4,192,512]{2,1,0:T(8,128)(2,1)}, u32[]{:S(2)}, u32[]{:S(2)}) async-start(bf16[4,192,512]{2,1,0:T(8,128)(2,1)} %bitcast.10), calls=%async_computation.2 | async-start | bytes 1572864 | tf_op jit(solution)/shard_map/all_to_all | solution.py:52
  906.8 46.4 %all-to-all-start.4 = ((bf16[4,192,512]{2,1,0:T(8,128)(2,1)}), bf16[4,192,512]{2,1,0:T(8,128)(2,1)}, u32[]{:S(2)}, u32[]{:S(2)}) async-start(bf16[4,192,512]{2,1,0:T(8,128)(2,1)} %bitcast.239), calls=%async_computation.6 | async-start | bytes 1572864 | tf_op jit(solution)/shard_map/all_to_all | solution.py:52
  953.2 120.1 %all-to-all-start.2 = ((bf16[16,96,2048]{2,1,0:T(8,128)(2,1)}), bf16[16,96,2048]{2,1,0:T(8,128)(2,1)}, u32[]{:S(2)}, u32[]{:S(2)}) async-start(bf16[16,96,2048]{2,1,0:T(8,128)(2,1)} %bitcast.233), calls=%async_computation.4 | async-start | bytes 12582912 | tf_op jit(solution)/shard_map/all_to_all | solution.py:64
  1316.9 119.9 %all-to-all-start.6 = ((bf16[16,96,2048]{2,1,0:T(8,128)(2,1)}), bf16[16,96,2048]{2,1,0:T(8,128)(2,1)}, u32[]{:S(2)}, u32[]{:S(2)}) async-start(bf16[16,96,2048]{2,1,0:T(8,128)(2,1)} %bitcast.234), calls=%async_computation.8 | async-start | bytes 12582912 | tf_op jit(solution)/shard_map/all_to_all | solution.py:64
  1322.5 223.9 %all-gather.12.cloned.1.call-start = ((), (), s32[]{:S(2)}) async-start(), calls=%async_computation.23 | async-start | bytes 3932160 | tf_op jit(solution)/shard_map/all_gather | solution.py:26
  1519.5 144.4 %reduce-scatter.15.cloned.1.call-start = ((), (), s32[]{:S(2)}) async-start(), calls=%async_computation.24 | async-start | bytes 7864320 | tf_op jit(solution)/shard_map/reduce_scatter | solution.py:34
  1553.0 302.4 %reduce-scatter.17.cloned.1.call-start = ((), (), s32[]{:S(2)}) async-start(), calls=%async_computation.25 | async-start | bytes 7864320 | tf_op jit(solution)/shard_map/reduce_scatter | solution.py:344
  1743.9 225.6 %reduce-scatter.19.cloned.1.call-start = ((), (), s32[]{:S(2)}) async-start(), calls=%async_computation.26 | async-start | bytes 7864320 | tf_op jit(solution)/shard_map/reduce_scatter | solution.py:347
  1769.9 374.4 %all-gather.14.cloned.1.call-start = ((), (), s32[]{:S(2)}) async-start(), calls=%async_computation.27 | async-start | bytes 11796480 | tf_op jit(solution)/shard_map/all_gather | solution.py:30
  1976.8 327.9 %reduce-scatter.21.cloned.1.call-start = ((), (), s32[]{:S(2)}) async-start(), calls=%async_computation.28 | async-start | bytes 7864320 | tf_op jit(solution)/shard_map/reduce_scatter | solution.py:43
  2155.4 234.1 %all-reduce.4.cloned.1.call-start = ((), (), s32[]{:S(2)}) async-start(), calls=%async_computation.31 | async-start | bytes 524288 | tf_op jit(solution)/shard_map/psum | solution.py:393
  2157.4 232.1 %reduce-scatter.25.cloned.1.call-start = ((), (), s32[]{:S(2)}) async-start(), calls=%async_computation.30 | async-start | bytes 1572864 | tf_op jit(solution)/shard_map/reduce_scatter | solution.py:381
  2164.2 403.1 %reduce-scatter.29.cloned.1.call-start = ((), (), s32[]{:S(2)}) async-start(), calls=%async_computation.33 | async-start | bytes 25165824 | tf_op jit(solution)/shard_map/reduce_scatter | solution.py:383
  2178.2 435.2 %reduce-scatter.23.cloned.1.call-start = ((), (), s32[]{:S(2)}) async-start(), calls=%async_computation.29 | async-start | bytes 4718592 | tf_op jit(solution)/shard_map/reduce_scatter | solution.py:380
  2188.8 796.2 %reduce-scatter.27.cloned.1.call-start = ((), (), s32[]{:S(2)}) async-start(), calls=%async_computation.32 | async-start | bytes 50331648 | tf_op jit(solution)/shard_map/reduce_scatter | solution.py:382
  2300.0 85.5 %all-to-all-start.3 = ((f32[192,4,512]{2,0,1:T(8,128)}), f32[192,4,512]{2,0,1:T(8,128)}, u32[]{:S(2)}, u32[]{:S(2)}) async-start(f32[192,4,512]{2,0,1:T(8,128)} %copy.158), calls=%async_computation.5 | async-start | bytes 3145728 | tf_op jit(solution)/shard_map/all_to_all | solution.py:56
  2385.6 601.1 %copy-start.1 = (bf16[512,512]{1,0:T(8,128)(2,1)S(1)}, bf16[512,512]{1,0:T(8,128)(2,1)}, u32[]{:S(2)}) copy-start(bf16[512,512]{1,0:T(8,128)(2,1)} %param.14) | copy-start | bytes 1572868
  (68 other events, 2848.6 us)
Sparse Core Ops, SparseCore 0:
  26.1 26.7 all-gather.5
  64.0 313.7 reduce-scatter.10
  404.9 115.9 all-gather.7
  591.1 61.6 all-gather.9
  659.3 57.0 reduce-scatter.12
  1519.6 26.8 all-gather.11
  1553.1 110.7 reduce-scatter.14
  1744.1 111.2 reduce-scatter.16
  1858.2 111.2 reduce-scatter.18
  1976.9 167.2 all-gather.13
  2155.5 56.5 reduce-scatter.20
  2218.9 134.1 all-reduce.3
  2356.0 19.2 reduce-scatter.24
  2378.1 189.0 reduce-scatter.28
  2570.0 43.3 reduce-scatter.22
  2616.1 368.8 reduce-scatter.26
where the time goes:
time: 3000 us; the launch traced here: 2990 us
  waiting for transfers between devices  1870 us (62%)
  blocking collectives  498 us (17%)
  matrix products  288 us (10%)
  local copies, waits for them, and re-layouts  149 us (5%)
  other arithmetic  140 us (5%)
  starting transfers between devices  34.9 us (1%)
    reduce_scatter x2, waiting for transfers between devices, reduce_rows(): lax.psum_scatter(term_fn(jnp.int32(0), lax.axis_size('row') * rows_here),...  423 us
    reduce_scatter x1, waiting for transfers between devices, on_device(): lax.psum_scatter(expand_term, 'dp', scatter_dimension=1, tiled=True)  372 us
    all_gather x3, waiting for transfers between devices, gather_rows(): return lax.all_gather(stacked, 'row', axis=1, tiled=True)  342 us
    all_to_all x2, blocking collectives, send_slots(): lax.all_to_all(slots, ('row', 'col'), split_axis=0, concat_axis=0, tiled=...  306 us
    all_to_all x2, waiting for transfers between devices, return_slots(): lax.all_to_all(slots, ('row', 'col'), split_axis=0, concat_axis=0, tiled=...  215 us
    reduce_scatter x1, waiting for transfers between devices, on_device(): lax.psum_scatter(reduce_term, 'dp', scatter_dimension=1, tiled=True)  178 us
    reduce_scatter x1, waiting for transfers between devices, on_device(): lax.psum_scatter(grad_values_all.reshape(seq_len, col_width), 'row', scat...  95.6 us
    reduce_scatter x1, waiting for transfers between devices, on_device(): lax.psum_scatter(grad_keys_all.reshape(seq_len, col_width), 'row', scatte...  74.5 us
  transfers between devices with their start and end apart: 21, of which 16 were waited for; matrix products, arithmetic and copies ran while one was open for 9% of the time, Pallas kernels for 0%

commit v1 on v0

v1 whole, which is shorter than its diff:
```python
import functools
import math

import jax
import jax.numpy as jnp
from jax import lax
from jax.experimental import pallas as pl
from jax.experimental.pallas import tpu as pltpu
from jax.sharding import PartitionSpec as P

D = 2048
HD = 128
F = 1024
TOP = 8
CORES = 2
PLANE = ("row", "col")
BLOCKS = ("col", "row")
LOG2E = math.log2(math.e)
MASKED = -1e30

norm_epsilon = 1e-05
rope_base = 10000.0
bf16 = jnp.bfloat16
f32 = jnp.float32


def dot_nt(a, b):
    return lax.dot_general(a, b, (((1,), (1,)), ((), ())), preferred_element_type=f32)


def dot_nn(a, b):
    return lax.dot_general(a, b, (((1,), (0,)), ((), ())), preferred_element_type=f32)


def key_limits(first_query, query_rows, key_rows, prefix):
    open_blocks = jnp.maximum((first_query + 1) // key_rows, prefix // key_rows)
    all_blocks = pl.cdiv(jnp.maximum(first_query + query_rows, prefix), key_rows)
    return open_blocks, all_blocks


def mask_scores(scores, first_key, first_query, prefix):
    keys = first_key + lax.broadcasted_iota(jnp.int32, scores.shape, 0)
    queries = first_query + lax.broadcasted_iota(jnp.int32, scores.shape, 1)
    return jnp.where((keys <= queries) | (keys < prefix), scores, MASKED)


def attention_kernel(scale, prefix_ref, q_ref, k_ref, v_flip_ref, out_ref, lse_ref, scores_ref):
    query_rows = q_ref.shape[0]
    key_rows = min(512, k_ref.shape[0])
    first_query = pl.program_id(0) * query_rows
    prefix = prefix_ref[0]
    q = q_ref[...]
    open_blocks, all_blocks = key_limits(first_query, query_rows, key_rows, prefix)

    def score(j, top, masked):
        start = pl.multiple_of(j * key_rows, key_rows)
        scores = dot_nt(k_ref[pl.ds(start, key_rows), :], q) * (scale * LOG2E)
        if masked:
            scores = mask_scores(scores, start, first_query, prefix)
        scores_ref[pl.ds(start, key_rows), :] = scores
        return jnp.maximum(top, jnp.max(scores.reshape(key_rows // 8, 8, query_rows), axis=0))

    top = jnp.full((8, query_rows), MASKED, f32)
    top = lax.fori_loop(0, open_blocks, lambda j, t: score(j, t, False), top)
    top = lax.fori_loop(open_blocks, all_blocks, lambda j, t: score(j, t, True), top)
    peak = jnp.max(top, axis=0, keepdims=True)

    def mix(j, carry):
        total, mixed = carry
        start = pl.multiple_of(j * key_rows, key_rows)
        weights = jnp.exp2(scores_ref[pl.ds(start, key_rows), :] - peak)
        total = total + jnp.sum(weights.reshape(key_rows // 8, 8, query_rows), axis=0)
        mixed = mixed + dot_nn(v_flip_ref[:, pl.ds(start, key_rows)], weights.astype(bf16))
        return total, mixed

    total, mixed = lax.fori_loop(
        0,
        all_blocks,
        mix,
        (jnp.zeros((8, query_rows), f32), jnp.zeros((q.shape[1], query_rows), f32)),
    )
    total = jnp.sum(total, axis=0, keepdims=True)
    out_ref[...] = (mixed / total).T.astype(out_ref.dtype)
    lse_ref[...] = peak + jnp.log2(total)


def attention(q, k, v, prefix_len, query_rows):
    length, width = q.shape
    query_block = pl.BlockSpec((query_rows, width), lambda i, p: (i, 0))
    return pl.pallas_call(
        functools.partial(attention_kernel, width**-0.5),
        grid_spec=pltpu.PrefetchScalarGridSpec(
            num_scalar_prefetch=1,
            grid=(length // query_rows,),
            in_specs=[
                query_block,
                pl.BlockSpec((length, width), lambda i, p: (0, 0)),
                pl.BlockSpec((width, length), lambda i, p: (0, 0)),
            ],
            out_specs=[query_block, pl.BlockSpec((1, query_rows), lambda i, p: (0, i))],
            scratch_shapes=[pltpu.VMEM((length, query_rows), f32)],
        ),
        out_shape=[
            jax.ShapeDtypeStruct((length, width), bf16),
            jax.ShapeDtypeStruct((1, length), f32),
        ],
        compiler_params=pltpu.CompilerParams(vmem_limit_bytes=40 * 2**20),
        cost_estimate=pl.CostEstimate(
            flops=2 * length * length * width, bytes_accessed=10 * length * width,
            transcendentals=length * length // 2,
        ),
        name="attention_forward",
    )(prefix_len, q, k, v.T)


def attention_back_kernel(
    scale, prefix_ref, q_ref, grad_ref, lse_ref, centre_ref, k_ref, k_flip_ref, v_ref,
    grad_q_ref, grad_k_ref, grad_v_ref,
):
    query_rows = q_ref.shape[0]
    key_rows = min(512, k_ref.shape[0])
    step = pl.program_id(0)
    first_query = step * query_rows
    prefix = prefix_ref[0]

    @pl.when(step == 0)
    def _():
        grad_k_ref[...] = jnp.zeros_like(grad_k_ref)
        grad_v_ref[...] = jnp.zeros_like(grad_v_ref)

    q = q_ref[...]
    grad = grad_ref[...]
    lse = lse_ref[...]
    centre = centre_ref[...]
    open_blocks, all_blocks = key_limits(first_query, query_rows, key_rows, prefix)

    def block(j, total, masked):
        start = pl.multiple_of(j * key_rows, key_rows)
        rows = pl.ds(start, key_rows)
        scores = dot_nt(k_ref[rows, :], q) * (scale * LOG2E) - lse
        if masked:
            scores = mask_scores(scores, start, first_query, prefix)
        weights = jnp.exp2(scores)
        grad_weights = dot_nt(v_ref[rows, :], grad)
        grad_scores = (weights * (grad_weights - centre)).astype(bf16)
        grad_v_ref[rows, :] += dot_nn(weights.astype(bf16), grad)
        grad_k_ref[rows, :] += dot_nn(grad_scores, q)
        return total + dot_nn(k_flip_ref[:, rows], grad_scores)

    total = jnp.zeros((q.shape[1], query_rows), f32)
    total = lax.fori_loop(0, open_blocks, lambda j, a: block(j, a, False), total)
    total = lax.fori_loop(open_blocks, all_blocks, lambda j, a: block(j, a, True), total)
    grad_q_ref[...] = total.T * scale

    @pl.when(step == pl.num_programs(0) - 1)
    def _():
        grad_k_ref[...] = grad_k_ref[...] * scale


def attention_back(q, k, v, grad, lse, centre, prefix_len, query_rows):
    length, width = q.shape
    whole = pl.BlockSpec((length, width), lambda i, p: (0, 0))
    flipped = pl.BlockSpec((width, length), lambda i, p: (0, 0))
    query_block = pl.BlockSpec((query_rows, width), lambda i, p: (i, 0))
    query_row = pl.BlockSpec((1, query_rows), lambda i, p: (0, i))
    result = jax.ShapeDtypeStruct((length, width), f32)
    return pl.pallas_call(
        functools.partial(attention_back_kernel, width**-0.5),
        grid_spec=pltpu.PrefetchScalarGridSpec(
            num_scalar_prefetch=1,
            grid=(length // query_rows,),
            in_specs=[query_block, query_block, query_row, query_row, whole, flipped, whole],
            out_specs=[query_block, whole, whole],
        ),
        out_shape=[result, result, result],
        compiler_params=pltpu.CompilerParams(vmem_limit_bytes=40 * 2**20),
        cost_estimate=pl.CostEstimate(
            flops=5 * length * length * width, bytes_accessed=22 * length * width,
            transcendentals=length * length // 2,
        ),
        name="attention_backward",
    )(prefix_len, q, grad, lse, centre, k, k.T, v)


class Ring:
    def __init__(self, rows, cols):
        self.rows, self.cols = rows, cols
        self.cores = CORES if cols % CORES == 0 else 1
        self.groups = cols // self.cores
        self.order = [
            (row, group)
            for group in range(self.groups)
            for row in (range(rows) if group % 2 == 0 else range(rows - 1, -1, -1))
        ]
        self.size = len(self.order)
        self.clockwise = self.shift(1)
        self.counter = self.shift(-1)
        self.sibling = [
            (row * cols + col, row * cols + col - col % self.cores + (col + 1) % self.cores)
            for row in range(rows)
            for col in range(cols)
        ]
        row, col = lax.axis_index("row"), lax.axis_index("col")
        group = col // self.cores
        self.core = col % self.cores
        self.place = group * rows + jnp.where(group % 2 == 0, row, rows - 1 - row)

    def shift(self, step):
        pairs = []
        for at, (row, group) in enumerate(self.order):
            to_row, to_group = self.order[(at + step) % self.size]
            for core in range(self.cores):
                pairs.append(
                    (
                        row * self.cols + group * self.cores + core,
                        to_row * self.cols + to_group * self.cores + core,
                    )
                )
        return pairs

    def chip(self, distance):
        at = (self.place + distance + self.size) % self.size
        group = at // self.rows
        along = at % self.rows
        return jnp.where(group % 2 == 0, along, self.rows - 1 - along), group

    def owners(self, distance):
        row, group = self.chip(distance)
        return [(row, group * self.cores + (self.core + k) % self.cores) for k in range(self.cores)]

    def gather(self, block, put):
        def arrived(piece, distance):
            for k, (row, col) in enumerate(self.owners(distance)):
                put(lax.ppermute(piece, PLANE, self.sibling) if k else piece, row, col)

        forth = back = block
        arrived(block, 0)
        for step in range(1, (self.size + 1) // 2):
            forth = lax.ppermute(forth, PLANE, self.clockwise)
            back = lax.ppermute(back, PLANE, self.counter)
            arrived(forth, -step)
            arrived(back, step)
        if self.size % 2 == 0:
            half = block.shape[0] // 2
            forth = lax.ppermute(forth[:half], PLANE, self.clockwise)
            back = lax.ppermute(back[half:], PLANE, self.counter)
            arrived(jnp.concatenate([forth, back], axis=0), self.size // 2)

    def scatter_sum(self, get):
        def add(one, two):
            return (one.astype(f32) + two.astype(f32)).astype(bf16)

        def chip_sum(distance):
            mine, *others = [get(row, col) for row, col in self.owners(distance)]
            for other in others:
                mine = add(mine, lax.ppermute(other, PLANE, self.sibling))
            return mine

        forth = back = None
        half = 0
        if self.size % 2 == 0:
            far = chip_sum(self.size // 2)
            half = far.shape[0] // 2
            forth = lax.ppermute(far[:half], PLANE, self.clockwise)
            back = lax.ppermute(far[half:], PLANE, self.counter)
        for step in range((self.size - 1) // 2, 0, -1):
            ahead, behind = chip_sum(step), chip_sum(-step)
            if forth is None:
                forth, back = ahead, behind
            elif forth.shape[0] == half:
                forth = jnp.concatenate([add(ahead[:half], forth), ahead[half:]], axis=0)
                back = jnp.concatenate([behind[:half], add(behind[half:], back)], axis=0)
            else:
                forth, back = add(ahead, forth), add(behind, back)
            forth = lax.ppermute(forth, PLANE, self.clockwise)
            back = lax.ppermute(back, PLANE, self.counter)
        return chip_sum(0).astype(f32) + forth.astype(f32) + back.astype(f32)

    def small_sum(self, values):
        rows, cols = self.rows, self.cols
        if rows & (rows - 1) or cols & (cols - 1):
            return lax.psum(values, PLANE)
        swaps = []
        bit = 1
        while bit < cols:
            swaps.append(lambda row, col, bit=bit: (row, col ^ bit))
            bit *= 2
        bit = 1
        while bit < rows:
            swaps.append(lambda row, col, bit=bit: (row ^ bit, col))
            bit *= 2
        for swap in swaps:
            pairs = []
            for row in range(rows):
                for col in range(cols):
                    to_row, to_col = swap(row, col)
                    pairs.append((row * cols + col, to_row * cols + to_col))
            values = values + lax.ppermute(values, PLANE, pairs)
        return values


def dp_sum(part):
    count = lax.axis_size("dp")
    rank = lax.axis_index("dp")
    if count == 1:
        return part(rank)
    onward = [(d, (d + 1) % count) for d in range(count)]
    total = part((rank + count - 1) % count)
    for step in range(1, count):
        arrived = lax.ppermute(total.astype(bf16), "dp", onward)
        total = part((rank + 2 * count - 1 - step) % count) + arrived.astype(f32)
    return total


def exchange(pieces, axes):
    return lax.all_to_all(pieces, axes, split_axis=0, concat_axis=0, tiled=True)


def rope_tables(positions):
    half_width = HD // 2
    frequency = rope_base ** (-2.0 * jnp.arange(half_width, dtype=f32) / HD)
    angles = positions.astype(f32)[:, None] * frequency[None, :]
    return jnp.cos(angles), jnp.sin(angles)


def rotate(values, cosine, sine_part):
    half_width = values.shape[-1] // 2
    first_half, second_half = values[..., :half_width], values[..., half_width:]
    return jnp.concatenate(
        [
            first_half * cosine - second_half * sine_part,
            second_half * cosine + first_half * sine_part,
        ],
        axis=-1,
    )


def unrotate(gradient, cosine, sine_part):
    return rotate(gradient, cosine, -sine_part)


def norm_back(values, inverse, gain_row, upstream, dot_total):
    scaled = upstream * gain_row
    return inverse[:, None] * scaled - values * (inverse**3 * dot_total / D)[:, None]


def dot(a, b):
    return jnp.dot(a, b, preferred_element_type=f32)


def einsum(spec, a, b):
    return jnp.einsum(spec, a, b, preferred_element_type=f32)


def on_device(
    layer_input,
    gains,
    qkv_weight,
    output_weight,
    router_weight,
    expand_weight,
    reduce_weight,
    routes,
    drop_order,
    prefix_len,
    cotangent,
):
    row_rank, col_rank = lax.axis_index("row"), lax.axis_index("col")
    rows, cols = lax.axis_size("row"), lax.axis_size("col")
    dp_count = lax.axis_size("dp")
    group = rows * cols
    res_rows, row_width = layer_input.shape
    col_width = qkv_weight.shape[2]
    seq_len = res_rows * cols
    tok_rows = res_rows // rows
    block_rank = col_rank * rows + row_rank
    expert_rank = row_rank * cols + col_rank
    expert_count = router_weight.shape[1]
    local_experts = expand_weight.shape[0]
    capacity = tok_rows * TOP // expert_count
    slots = group * capacity
    ring = Ring(rows, cols)
    gain_rows = gains.astype(f32)

    head_weight = exchange(
        qkv_weight.reshape(row_width, 3, rows, HD).transpose(2, 0, 1, 3), "row"
    ).reshape(D, 3 * HD)
    cosine, sine_part = rope_tables(jnp.arange(seq_len))
    route_rows = lax.all_gather(
        jnp.concatenate([routes, drop_order[:, None]], axis=1), "col", axis=0, tiled=True
    )
    all_routes = route_rows[:, :TOP]
    drop_rank = route_rows[:, TOP].reshape(group, tok_rows)
    own_experts = expert_rank * local_experts + jnp.arange(local_experts)
    member = jnp.any(all_routes[:, :, None] == own_experts[None, None, :], axis=1)
    member = member.reshape(group, tok_rows, local_experts).transpose(0, 2, 1)
    token_index = jnp.arange(tok_rows)
    earlier = (drop_rank[:, None, :] < drop_rank[:, :, None]) | (
        drop_rank[:, None, :] == drop_rank[:, :, None]
    ) & (token_index[None, None, :] < token_index[None, :, None])
    position = jnp.sum(
        jnp.where(earlier[:, None] & member[:, :, None, :], 1, 0), axis=-1
    )
    kept = member & (position < capacity)
    hits = kept[:, :, None, :] & (
        position[:, :, None, :] == jnp.arange(capacity)[None, None, :, None]
    )
    dispatch = hits.astype(bf16)

    x_box = [jnp.zeros((seq_len, D), bf16)]

    def put_input(block, row, col):
        x_box[0] = lax.dynamic_update_slice(x_box[0], block, (col * res_rows, row * row_width))

    ring.gather(layer_input, put_input)
    x_all = x_box[0]
    x_wide = x_all.astype(f32)
    inv_first = lax.rsqrt(jnp.sum(x_wide * x_wide, axis=1) / D + norm_epsilon)
    first_low = (x_wide * inv_first[:, None] * gain_rows[0]).astype(bf16)
    projected = dot(first_low, head_weight)
    query_raw = projected[:, :HD]
    key_raw = projected[:, HD : 2 * HD]
    value_raw = projected[:, 2 * HD :]
    squares = ring.small_sum(
        jnp.stack([jnp.sum(query_raw * query_raw, axis=1), jnp.sum(key_raw * key_raw, axis=1)])
    )
    inv_query, inv_key = lax.rsqrt(squares / D + norm_epsilon)
    head_first = block_rank * HD
    gain_query = lax.dynamic_slice_in_dim(gain_rows[1], head_first, HD)
    gain_key = lax.dynamic_slice_in_dim(gain_rows[2], head_first, HD)
    query_low = rotate(query_raw * inv_query[:, None] * gain_query, cosine, sine_part).astype(bf16)
    key_low = rotate(key_raw * inv_key[:, None] * gain_key, cosine, sine_part).astype(bf16)
    value_low = value_raw.astype(bf16)

    query_rows = max(seq_len // 6, 128)
    attn_head, lse = attention(query_low, key_low, value_low, prefix_len, query_rows)
    attn_tokens = exchange(attn_head.reshape(group, tok_rows, HD), BLOCKS)
    attn_tokens = attn_tokens.transpose(1, 0, 2).reshape(tok_rows, D)
    output_full = lax.all_gather(output_weight, BLOCKS, axis=0)
    output_full = output_full.reshape(cols, rows, col_width, row_width)
    output_full = output_full.transpose(0, 2, 1, 3).reshape(D, D)
    first_token = block_rank * tok_rows
    x_tokens = lax.dynamic_slice_in_dim(x_all, first_token, tok_rows, 0).astype(f32)
    residual = x_tokens + dot(attn_tokens, output_full)
    inv_second = lax.rsqrt(jnp.sum(residual * residual, axis=1) / D + norm_epsilon)
    second_low = (residual * inv_second[:, None] * gain_rows[3]).astype(bf16)

    upstream_all = lax.all_gather(cotangent, BLOCKS, axis=0)
    upstream_all = upstream_all.reshape(cols, rows, res_rows, row_width)
    upstream_all = upstream_all.transpose(0, 2, 1, 3).reshape(seq_len, D)
    upstream = lax.dynamic_slice_in_dim(upstream_all, first_token, tok_rows, 0).astype(f32)

    def to_slots(token_rows):
        filled = einsum("best,btd->ebsd", dispatch, token_rows.reshape(group, tok_rows, D))
        return filled.astype(bf16).reshape(local_experts, slots, D)

    def from_slots(slot_rows):
        shaped = slot_rows.reshape(local_experts, group, capacity, D)
        return einsum("best,ebsd->btd", dispatch, shaped).astype(bf16)

    upstream_slots = to_slots(upstream_all)
    grad_hidden_raw = einsum("end,efd->enf", upstream_slots, reduce_weight)

    h_box = [jnp.zeros((group, tok_rows, D), bf16)]

    def put_rows(block, row, col):
        h_box[0] = lax.dynamic_update_slice(h_box[0], block[None], (col * rows + row, 0, 0))

    ring.gather(second_low, put_rows)
    feats_all = h_box[0].reshape(seq_len, D)
    slot_rows = to_slots(feats_all)
    logits = dot(feats_all, router_weight)
    router_probs = jax.nn.softmax(logits, axis=-1)
    own_probs = lax.dynamic_slice_in_dim(
        router_probs, expert_rank * local_experts, local_experts, 1
    ).reshape(group, tok_rows, local_experts)
    slot_gate = jnp.sum(
        jnp.where(hits, own_probs.transpose(0, 2, 1)[:, :, None, :], 0.0), axis=-1
    )
    slot_gate = slot_gate.transpose(1, 0, 2).reshape(local_experts, slots)[:, :, None]
    gate_up = einsum("end,edf->enf", slot_rows, expand_weight)
    gate_pre, up_pre = gate_up[..., :F], gate_up[..., F:]
    sigmoid_gate = jax.nn.sigmoid(gate_pre)
    silu_gate = gate_pre * sigmoid_gate
    hidden = (silu_gate * up_pre).astype(bf16)
    grad_hidden = grad_hidden_raw * slot_gate
    grad_gate_pre = (
        grad_hidden * up_pre * sigmoid_gate * (1.0 + gate_pre * (1.0 - sigmoid_gate))
    ).astype(bf16)
    grad_up_pre = (grad_hidden * silu_gate).astype(bf16)
    grad_gate_up = jnp.concatenate([grad_gate_pre, grad_up_pre], axis=-1)
    grad_slot_in = einsum("enf,edf->end", grad_gate_up, expand_weight).astype(bf16)
    grad_feats_part = from_slots(grad_slot_in)

    def rows_of(parts):
        return lambda row, col: lax.dynamic_index_in_dim(parts, col * rows + row, 0, False)

    grad_feats = ring.scatter_sum(rows_of(grad_feats_part))

    expert_out = einsum("enf,efd->end", hidden, reduce_weight).astype(bf16)
    grad_gate = jnp.sum(expert_out.astype(f32) * upstream_slots.astype(f32), axis=-1)
    grad_gate = grad_gate.reshape(local_experts, group, capacity).transpose(1, 0, 2)
    gate_tokens = jnp.sum(jnp.where(hits, grad_gate[..., None], 0.0), axis=2)
    grad_probs = exchange(gate_tokens, BLOCKS).reshape(cols, rows, local_experts, tok_rows)
    grad_probs = grad_probs.transpose(3, 1, 0, 2).reshape(tok_rows, expert_count)
    probs = lax.dynamic_slice_in_dim(router_probs, first_token, tok_rows, 0)
    grad_logits = (
        probs * (grad_probs - jnp.sum(probs * grad_probs, axis=-1, keepdims=True))
    ).astype(bf16)
    router_term = einsum("td,te->de", second_low, grad_logits)

    moe_part = from_slots((expert_out.astype(f32) * slot_gate).astype(bf16))
    moe_tokens = ring.scatter_sum(rows_of(moe_part))
    layer_tokens = (residual + moe_tokens).astype(bf16)
    layer_output = lax.all_to_all(layer_tokens, "row", split_axis=1, concat_axis=0, tiled=True)

    grad_out_slots = (upstream_slots.astype(f32) * slot_gate).astype(bf16)
    reduce_rows = F // dp_count
    expand_rows = D // dp_count

    def reduce_part(rank):
        block = lax.dynamic_slice_in_dim(hidden, rank * reduce_rows, reduce_rows, 2)
        return einsum("enf,end->efd", block, grad_out_slots)

    def expand_part(rank):
        block = lax.dynamic_slice_in_dim(slot_rows, rank * expand_rows, expand_rows, 2)
        return einsum("end,enf->edf", block, grad_gate_up)

    reduce_grad = dp_sum(reduce_part)
    expand_grad = dp_sum(expand_part)

    grad_feats = grad_feats + dot(grad_logits, router_weight.T)
    dot_second = jnp.sum(grad_feats * gain_rows[3] * residual, axis=1)
    grad_resid = upstream + norm_back(residual, inv_second, gain_rows[3], grad_feats, dot_second)
    gain_second_term = jnp.sum(grad_feats * residual * inv_second[:, None], axis=0)
    grad_branch = grad_resid.astype(bf16)
    grad_attn = einsum("tr,cr->tc", grad_branch, output_full).astype(bf16)
    grad_attn = grad_attn.reshape(tok_rows, group, HD).transpose(1, 0, 2)
    grad_attn = exchange(grad_attn, BLOCKS).reshape(seq_len, HD)
    grad_block = lax.all_to_all(grad_branch, "row", split_axis=1, concat_axis=0, tiled=True)
    output_term = einsum("tc,tr->cr", attn_tokens, grad_branch).astype(bf16)
    output_term = output_term.reshape(cols, col_width, rows, row_width).transpose(0, 2, 1, 3)
    output_sum = lax.psum_scatter(
        output_term.reshape(group, col_width, row_width), BLOCKS, scatter_dimension=0, tiled=False
    )
    output_rows = col_width // dp_count
    output_grad = dp_sum(
        lambda rank: lax.dynamic_slice_in_dim(
            output_sum, rank * output_rows, output_rows, 0
        ).astype(f32)
    )

    centre = jnp.sum(attn_head.astype(f32) * grad_attn.astype(f32), axis=1)[None]
    grad_query, grad_key, grad_value = attention_back(
        query_low, key_low, value_low, grad_attn, lse, centre, prefix_len, query_rows
    )
    grad_qnorm = unrotate(grad_query, cosine, sine_part)
    grad_knorm = unrotate(grad_key, cosine, sine_part)
    dots = ring.small_sum(
        jnp.stack(
            [
                jnp.sum(grad_qnorm * gain_query * query_raw, axis=1),
                jnp.sum(grad_knorm * gain_key * key_raw, axis=1),
            ]
        )
    )
    grad_qraw = norm_back(query_raw, inv_query, gain_query, grad_qnorm, dots[0])
    grad_kraw = norm_back(key_raw, inv_key, gain_key, grad_knorm, dots[1])
    gain_query_term = jnp.sum(grad_qnorm * query_raw * inv_query[:, None], axis=0)
    gain_key_term = jnp.sum(grad_knorm * key_raw * inv_key[:, None], axis=0)
    grad_qkv = jnp.concatenate([grad_qraw, grad_kraw, grad_value], axis=1).astype(bf16)

    grad_first_part = einsum("tc,fc->tf", grad_qkv, head_weight).astype(bf16)
    grad_first = ring.scatter_sum(
        lambda row, col: lax.dynamic_slice(
            grad_first_part, (col * res_rows, row * row_width), (res_rows, row_width)
        )
    )
    dot_first = ring.small_sum(jnp.sum(grad_qkv.astype(f32) * projected, axis=1) / inv_first)
    own_first = col_rank * res_rows
    dot_first = lax.dynamic_slice_in_dim(dot_first, own_first, res_rows)
    inv_block = lax.dynamic_slice_in_dim(inv_first, own_first, res_rows)
    gain_block = lax.dynamic_slice_in_dim(gain_rows[0], row_rank * row_width, row_width)
    input_grad = grad_block.astype(f32) + norm_back(
        layer_input.astype(f32), inv_block, gain_block, grad_first, dot_first
    )

    qkv_term = einsum("tf,tc->fc", first_low, grad_qkv)
    gain_first_term = jnp.sum(qkv_term * head_weight.astype(f32), axis=1) / gain_rows[0]
    qkv_rows = row_width // dp_count
    qkv_shaped = qkv_term.reshape(rows, row_width, 3 * HD)
    qkv_sum = dp_sum(
        lambda rank: lax.dynamic_slice_in_dim(qkv_shaped, rank * qkv_rows, qkv_rows, 1)
    )
    qkv_grad = exchange(qkv_sum.astype(bf16), "row").reshape(rows, qkv_rows, 3, HD)
    qkv_grad = qkv_grad.transpose(1, 2, 0, 3).reshape(1, qkv_rows, 3, col_width).astype(f32)

    def placed(term):
        return lax.dynamic_update_slice(jnp.zeros((D,), f32), term, (head_first,))

    gain_terms = jnp.stack(
        [gain_first_term, placed(gain_query_term), placed(gain_key_term), gain_second_term]
    )
    gain_total, router_total = lax.psum((gain_terms, router_term), ("dp", "row", "col"))
    return (
        layer_output,
        input_grad.astype(bf16),
        gain_total,
        qkv_grad,
        output_grad[None],
        router_total,
        expand_grad,
        reduce_grad,
    )


def solution(mesh):
    return jax.shard_map(
        on_device,
        mesh=mesh,
        in_specs=(
            P(("dp", "col"), "row"),
            P(),
            P("row", None, "col"),
            P("col", "row"),
            P(),
            P(("row", "col"), None, None),
            P(("row", "col"), None, None),
            P(("dp", "col"), None),
            P(("dp", "col")),
            P("dp"),
            P(("dp", "col"), "row"),
        ),
        out_specs=(
            P(("dp", "col"), "row"),
            P(("dp", "col"), "row"),
            P(),
            P("row", "dp", None, "col"),
            P("col", "dp", "row"),
            P(),
            P(("row", "col"), "dp", None),
            P(("row", "col"), "dp", None),
        ),
        check_vma=False,
    )
```

time: 3000 us -> 1440 us (0.48)
  waiting for transfers between devices: 1870 us -> 539 us
  blocking collectives: 498 us -> 78.9 us
  local copies, waits for them, and re-layouts: 149 us -> 328 us
  starting transfers between devices: 34.9 us -> 119 us
  matrix products: 288 us -> 210 us
  other arithmetic: 140 us -> 102 us
  Pallas kernels: 0 us -> 34.7 us
    reduce_scatter x10 -> x1, waiting for transfers between devices: 1250 us -> 0.01 us  [on_device(): lax.psum_scatter(output_term.reshape(group, col_width, row_width), BLOCKS...]
    ppermute x0 -> x96, waiting for transfers between devices: none -> 509 us  [the longest x4 179 us: dp_sum(): arrived = lax.ppermute(total.astype(bf16), 'dp', onward)]
    all_gather x5 -> x2, waiting for transfers between devices: 394 us -> 0.02 us  [the longest x1 0.02 us: on_device(): output_full = lax.all_gather(output_weight, BLOCKS, axis=0)]
    all_to_all x3 -> x1, blocking collectives: 370 us -> 25.8 us  [exchange(): return lax.all_to_all(pieces, axes, split_axis=0, concat_axis=0, tiled=True)]
    all_to_all x5 -> x6, waiting for transfers between devices: 228 us -> 29.7 us  [the longest x4 19.4 us: exchange(): return lax.all_to_all(pieces, axes, split_axis=0, concat_axis=0, tiled=True)]
    dynamic_update_slice x4 -> x33, local copies, waits for them, and re-layouts: 0.05 us -> 156 us  [the longest x16 142 us: put_input(): lax.dynamic_update_slice(x_box[0], block, (col * res_rows, row * row_width))]
    ppermute x0 -> x96, starting transfers between devices: none -> 94.2 us  [the longest x6 18.4 us: gather(): forth = lax.ppermute(forth, PLANE, self.clockwise)]
    psum x6 -> x0, blocking collectives: 79.1 us -> none  [the longest x4 65.3 us: feature_sums(): return lax.psum(values, 'row')]
  transfers between devices with their start and end apart: 21 -> 106, of which waited for: 16 -> 43; matrix products, arithmetic and copies ran while one was open for 9% -> 34% of each run, Pallas kernels for 0% -> 2%
where the time goes in v1:
time: 1440 us; the launch traced here: 1430 us
  waiting for transfers between devices  539 us (37%)
  local copies, waits for them, and re-layouts  328 us (23%)
  matrix products  210 us (15%)
  starting transfers between devices  119 us (8%)
  other arithmetic  102 us (7%)
  blocking collectives  78.9 us (5%)
  Pallas kernels  34.7 us (2%)
  between operations  16.8 us (1%)
    dot_general x17, matrix products, einsum(): return jnp.einsum(spec, a, b, preferred_element_type=f32)  191 us
    ppermute x4, waiting for transfers between devices, dp_sum(): arrived = lax.ppermute(total.astype(bf16), 'dp', onward)  179 us
    ppermute x6, waiting for transfers between devices, gather(): forth = lax.ppermute(forth, PLANE, self.clockwise)  143 us
    dynamic_update_slice x16, local copies, waits for them, and re-layouts, put_input(): lax.dynamic_update_slice(x_box[0], block, (col * res_rows, row * row_width))  142 us
    ppermute x9, waiting for transfers between devices, scatter_sum(): forth = lax.ppermute(forth, PLANE, self.clockwise)  75.8 us
    unnamed x174, local copies, waits for them, and re-layouts  41.5 us
    psum x1, blocking collectives, on_device(): lax.psum((gain_terms, router_term), ('dp', 'row', 'col'))  39.6 us
    ppermute x12, waiting for transfers between devices, small_sum(): values = values + lax.ppermute(values, PLANE, pairs)  37.2 us
  transfers between devices with their start and end apart: 106, of which 43 were waited for; matrix products, arithmetic and copies ran while one was open for 34% of the time, Pallas kernels for 2%

profile of v1, /device:TPU:0, one launch (start us, length us, event | category | flops | bytes accessed | tf_op | source)
XLA Modules:
  0.0 1428.3 jit_solution(7637734331456404013)
XLA Ops:
  11.0 24.3 %collective-permute-done.1 = bf16[768,512]{1,0:T(8,128)(2,1)} collective-permute-done((bf16[768,512]{1,0:T(8,128)(2,1)}, bf16[768,512]{1,0:T(8,128)(2,1)}, u32[]{:S(2)}, u32[]{:S(2)}) %collective-permute-start.1) | collective-permute-done | bytes 786464 | tf_op jit(solution)/shard_map/ppermute | solution.py:239
  78.7 59.0 %collective-permute-done.9 = bf16[768,512]{1,0:T(8,128)(2,1)} collective-permute-done((bf16[768,512]{1,0:T(8,128)(2,1)}, bf16[768,512]{1,0:T(8,128)(2,1)}, u32[]{:S(2)}, u32[]{:S(2)}) %collective-permute-start.9) | collective-permute-done | bytes 786464 | tf_op jit(solution)/shard_map/ppermute | solution.py:239
  356.8 15.3 %attention_forward.1 = (bf16[3072,128]{1,0:T(8,128)(2,1)}, f32[1,3072]{1,0:T(1,128)S(1)}) custom-call(s32[1]{0:T(128)S(6)} %copy.325.prefix_ref, bf16[3072,128]{1,0:T(8,128)(2,1)S(1)} %copy.205.q_ref, bf16[3072,128]{1,0:T(8,128)(2,1)S(1)} %copy.206.k_ref, bf16[128,3072]{1,0:T(8,128)(2,1)S(1)} %copy.207.v_flip_ref), custom_call_target="tpu_custom_call" | custom-call | flops 2415919104 | bytes 3932160 | tf_op jit(solution)/shard_map/attention_forward/pallas_call | solution.py:90
  436.9 16.8 %collective-permute-done.21 = bf16[192,2048]{1,0:T(8,128)(2,1)S(1)} collective-permute-done((bf16[192,2048]{1,0:T(8,128)(2,1)S(1)}, bf16[192,2048]{1,0:T(8,128)(2,1)S(1)}, u32[]{:S(2)}, u32[]{:S(2)}) %collective-permute-start.21) | collective-permute-done | bytes 786464 | tf_op jit(solution)/shard_map/ppermute | solution.py:239
  463.2 15.8 %collective-permute-done.25 = bf16[192,2048]{1,0:T(8,128)(2,1)S(1)} collective-permute-done((bf16[192,2048]{1,0:T(8,128)(2,1)S(1)}, bf16[192,2048]{1,0:T(8,128)(2,1)S(1)}, u32[]{:S(2)}, u32[]{:S(2)}) %collective-permute-start.25) | collective-permute-done | bytes 786464 | tf_op jit(solution)/shard_map/ppermute | solution.py:239
  485.6 13.7 collective-permute-done.29
  536.5 21.1 %fusion.139 = f32[2,768,2048]{2,1,0:T(8,128)} fusion(bf16[2,768,2048]{2,1,0:T(8,128)(2,1)} %bitcast.297, bf16[2,2048,2048]{2,1,0:T(8,128)(2,1)} %param.16), kind=kOutput, calls=%fused_computation.299 | convolution fusion | flops 12884901888 | bytes 35651584 | tf_op jit(solution)/shard_map/end,edf->enf/dot_general | solution.py:352
  564.4 17.4 %copy.286 = bf16[4,4,768,512]{3,1,2,0:T(4,128)(2,1)} copy(bf16[4,4,768,512]{3,2,1,0:T(8,128)(2,1)} %bitcast.292) | data formatting | bytes 25165824 | tf_op jit(solution)/shard_map/reshape | solution.py:449
  581.7 21.0 %reshape.303 = bf16[16,192,2048,1]{2,1,0,3:T(8,128)(2,1)} reshape(bf16[4,768,4,512]{3,2,1,0:T(4,128)(2,1)} %bitcast.283) | data formatting | bytes 25165824 | tf_op jit(solution)/shard_map/reshape;reshape | solution.py:454
  611.0 14.5 %fusion.4 = (f32[2,768]{1,0:T(2,128)S(1)}, bf16[2,768,2048]{2,1,0:T(8,128)(2,1)}) fusion(bf16[2,16,48,2048]{3,2,1,0:T(8,128)(2,1)S(1)} %copy.217, bf16[2,768,1024]{2,1,0:T(8,128)(2,1)S(1)} %copy-done.34, bf16[2,1024,2048]{2,1,0:T(8,128)(2,1)} %param.17), kind=kOutput, calls=%fused_computation.12 | convolution fusion | flops 6458178048 | bytes 24123392 | tf_op jit(solution)/shard_map/enf,efd->end/dot_general | solution.py:352
  627.1 16.7 %multiply_convert_fusion.1 = (bf16[2,768,1024]{2,1,0:T(8,128)(2,1)}, bf16[2,768,1024]{2,1,0:T(8,128)(2,1)}) fusion(f32[2,768,2048]{2,1,0:T(8,128)} %fusion.139, f32[2,768]{1,0:T(2,128)S(1)} %mul.889, bf16[2,768,2048]{2,1,0:T(8,128)(2,1)} %bitcast.300, bf16[2,1024,2048]{2,1,0:T(8,128)(2,1)} %param.17), kind=kOutput, calls=%fused_computation.25 | convolution fusion | flops 6464471040 | bytes 33560576 | tf_op jit(solution)/shard_map/end,efd->enf/dot_general | solution.py:352
  643.8 19.7 %convolution_convert_fusion.4 = bf16[2,768,2048]{2,1,0:T(8,128)(2,1)} fusion(bf16[2,2048,2048]{2,1,0:T(8,128)(2,1)} %param.16, bf16[2,768,1024]{2,1,0:T(8,128)(2,1)} %get-tuple-element.68, bf16[2,768,1024]{2,1,0:T(8,128)(2,1)} %get-tuple-element.67), kind=kOutput, calls=%fused_computation.37 | convolution fusion | flops 12900630528 | bytes 29360128 | tf_op jit(solution)/shard_map/enf,edf->end/dot_general | solution.py:352
  728.0 14.9 %collective-permute-done.58 = bf16[192,2048]{1,0:T(8,128)(2,1)S(1)} collective-permute-done((bf16[192,2048]{1,0:T(8,128)(2,1)S(1)}, bf16[192,2048]{1,0:T(8,128)(2,1)S(1)}, u32[]{:S(2)}, u32[]{:S(2)}) %collective-permute-start.58) | collective-permute-done | bytes 786464 | tf_op jit(solution)/shard_map/ppermute | solution.py:275
  746.1 13.7 collective-permute-done.42
  812.2 13.7 collective-permute-done.49
  908.8 14.5 %reshape.275 = bf16[4,512,4,512]{3,2,1,0:T(4,128)(2,1)} reshape(bf16[2048,2048]{1,0:T(8,128)(2,1)} %convolution_convert_fusion.1) | data formatting | bytes 16777216 | tf_op jit(solution)/shard_map/reshape | solution.py:542
  938.5 25.8 %all_to_all.57 = bf16[16,192,128]{2,1,0:T(8,128)(2,1)S(1)} all-to-all(bf16[16,192,128]{2,1,0:T(8,128)(2,1)S(1)} %bitcast.312), channel_id=1, replica_groups=mesh['dp'=2,'row'=4,'col'=4] {'col','row'}, dimensions={0} | all-to-all | bytes 1572864 | tf_op jit(solution)/shard_map/all_to_all | solution.py:316
  965.9 19.4 %attention_backward.1 = (f32[3072,128]{1,0:T(8,128)S(1)}, f32[3072,128]{1,0:T(8,128)S(1)}, f32[3072,128]{1,0:T(8,128)S(1)}) custom-call(s32[1]{0:T(128)S(6)} %copy.325.prefix_ref, bf16[3072,128]{1,0:T(8,128)(2,1)S(1)} %copy-done.4, bf16[3072,128]{1,0:T(8,128)(2,1)S(1)} %bitcast.280, f32[1,3072]{1,0:T(1,128)S(1)} %get-tuple-element.14.lse_ref, ...), custom_call_target="tpu_custom_call" | custom-call | flops 6039797760 | bytes 8650752 | tf_op jit(solution)/shard_map/attention_backward/pallas_call | solution.py:167
  1039.8 15.0 %convolution_convert_fusion.2 = bf16[2,1024,2048]{2,1,0:T(8,128)(2,1)} fusion(bf16[2,768,2048]{2,1,0:T(8,128)(2,1)} %bitcast.298, s32[]{:T(128)S(6)} %select_n.947, bf16[2,768,1024]{2,1,0:T(8,128)(2,1)} %get-tuple-element.68, bf16[2,768,1024]{2,1,0:T(8,128)(2,1)} %get-tuple-element.67), kind=kOutput, calls=%fused_computation.34 | convolution fusion | flops 6459228160 | bytes 17825796 | tf_op jit(solution)/shard_map/end,enf->edf/dot_general | solution.py:352
  1071.3 45.3 %collective-permute-done.95 = bf16[2,512,2048]{2,1,0:T(8,128)(2,1)} collective-permute-done((bf16[2,512,2048]{2,1,0:T(8,128)(2,1)}, bf16[2,512,2048]{2,1,0:T(8,128)(2,1)}, u32[]{:S(2)}, u32[]{:S(2)}) %collective-permute-start.95) | collective-permute-done | bytes 4194336 | tf_op jit(solution)/shard_map/ppermute | solution.py:310
  1162.2 14.5 %collective-permute-done.89 = f32[3072]{0:T(1024)S(1)} collective-permute-done((f32[3072]{0:T(1024)S(1)}, f32[3072]{0:T(1024)S(1)}, u32[]{:S(2)}, u32[]{:S(2)}) %collective-permute-start.89) | collective-permute-done | bytes 12320 | tf_op jit(solution)/shard_map/ppermute | solution.py:298
  1176.7 134.1 %collective-permute-done.92 = bf16[4,256,384]{1,2,0:T(8,128)(2,1)} collective-permute-done((bf16[4,256,384]{1,2,0:T(8,128)(2,1)}, bf16[4,256,384]{1,2,0:T(8,128)(2,1)}, u32[]{:S(2)}, u32[]{:S(2)}) %collective-permute-start.92) | collective-permute-done | bytes 786464 | tf_op jit(solution)/shard_map/ppermute | solution.py:310
  1336.1 39.6 %psum.14 = f32[4,2048]{1,0:T(4,128)} all-reduce(f32[4,2048]{1,0:T(4,128)S(1)} %pad_maximum_fusion.15), channel_id=1, replica_groups=mesh['dp'=2,'row'=4,'col'=4] {'dp','row','col'}, use_global_device_ids=true, to_apply=%region_21.22 | all-reduce | flops 8192 | bytes 65536 | tf_op jit(solution)/shard_map/psum | solution.py:604
  1383.9 15.0 %convert_add_fusion = f32[2,1024,2048]{2,1,0:T(8,128)} fusion(bf16[2,1024,2048]{2,1,0:T(8,128)(2,1)} %collective-permute-done.94, bf16[2,768,2048]{2,1,0:T(8,128)(2,1)} %bitcast.299, s32[]{:T(128)S(6)} %select_n.946, bf16[2,768,1024]{2,1,0:T(8,128)(2,1)} %get-tuple-element.68, bf16[2,768,1024]{2,1,0:T(8,128)(2,1)} %get-tuple-element.67), kind=kOutput, calls=%fused_computation.7 | convolution fusion | flops 6463422464 | bytes 34603012 | tf_op jit(solution)/shard_map/end,enf->edf/dot_general | solution.py:352
  (575 shorter events, 790.7 us)
Async XLA Ops:
  7.2 383.4 %all-gather.5.cloned.1.call-start = ((), (), s32[]{:S(2)}) async-start(), calls=%async_computation.10 | async-start | bytes 8912896 | tf_op jit(solution)/shard_map/all_gather | solution.py:439
  49.3 180.0 %all-to-all-start = ((bf16[4,512,3,128]{1,3,2,0:T(8,128)(2,1)}), bf16[4,512,3,128]{1,3,2,0:T(8,128)(2,1)S(1)}, u32[]{:S(2)}, u32[]{:S(2)}) async-start(bf16[4,512,3,128]{1,3,2,0:T(8,128)(2,1)} %copy.202), calls=%async_computation | async-start | bytes 3145728 | tf_op jit(solution)/shard_map/all_to_all | solution.py:316
  54.1 510.3 %all-gather.7.cloned.1.call-start = ((), (), s32[]{:S(2)}) async-start(), calls=%async_computation.11 | async-start | bytes 13369344 | tf_op jit(solution)/shard_map/all_gather | solution.py:448
  67.1 70.5 %collective-permute-start.9 = (bf16[768,512]{1,0:T(8,128)(2,1)}, bf16[768,512]{1,0:T(8,128)(2,1)}, u32[]{:S(2)}, u32[]{:S(2)}) collective-permute-start(bf16[768,512]{1,0:T(8,128)(2,1)} %collective-permute-done.5), channel_id=1, source_target_pairs={{0,4},{1,5},{4,8},{5,9},{8,12},{9,13},{12,14},{13,15},{14,10},{15,... | collective-permute-start | bytes 2359304 | tf_op jit(solution)/shard_map/ppermute | solution.py:239
  78.1 70.6 %collective-permute-start.11 = (bf16[768,512]{1,0:T(8,128)(2,1)}, bf16[768,512]{1,0:T(8,128)(2,1)S(1)}, u32[]{:S(2)}, u32[]{:S(2)}) collective-permute-start(bf16[768,512]{1,0:T(8,128)(2,1)} %collective-permute-done.7), channel_id=1, source_target_pairs={{0,2},{1,3},{4,0},{5,1},{8,4},{9,5},{12,8},{13,9},{14,12},{15,13},... | collective-permute-start | bytes 2359304 | tf_op jit(solution)/shard_map/ppermute | solution.py:240
  78.1 78.3 %collective-permute-start = (bf16[768,512]{1,0:T(8,128)(2,1)S(1)}, bf16[768,512]{1,0:T(8,128)(2,1)S(1)}, u32[]{:S(2)}, u32[]{:S(2)}) collective-permute-start(bf16[768,512]{1,0:T(8,128)(2,1)S(1)} %copy-done.29), channel_id=1, source_target_pairs={{0,1},{1,0},{2,3},{3,2},{4,5},{5,4},{6,7},{7,6},{8,9},{9,8},{10,11... | collective-permute-start | bytes 2359304 | tf_op jit(solution)/shard_map/ppermute | solution.py:234
  78.1 78.8 %collective-permute-start.2 = (bf16[768,512]{1,0:T(8,128)(2,1)}, bf16[768,512]{1,0:T(8,128)(2,1)S(1)}, u32[]{:S(2)}, u32[]{:S(2)}) collective-permute-start(bf16[768,512]{1,0:T(8,128)(2,1)} %collective-permute-done.1), channel_id=1, source_target_pairs={{0,1},{1,0},{2,3},{3,2},{4,5},{5,4},{6,7},{7,6},{8,9},{9,8},{10,11... | collective-permute-start | bytes 2359304 | tf_op jit(solution)/shard_map/ppermute | solution.py:234
  78.6 80.8 %collective-permute-start.4 = (bf16[768,512]{1,0:T(8,128)(2,1)}, bf16[768,512]{1,0:T(8,128)(2,1)}, u32[]{:S(2)}, u32[]{:S(2)}) collective-permute-start(bf16[768,512]{1,0:T(8,128)(2,1)} %copy-done.42), channel_id=1, source_target_pairs={{0,1},{1,0},{2,3},{3,2},{4,5},{5,4},{6,7},{7,6},{8,9},{9,8},{10,11... | collective-permute-start | bytes 2359304 | tf_op jit(solution)/shard_map/ppermute | solution.py:234
  155.6 75.4 %collective-permute-start.6 = (bf16[768,512]{1,0:T(8,128)(2,1)}, bf16[768,512]{1,0:T(8,128)(2,1)}, u32[]{:S(2)}, u32[]{:S(2)}) collective-permute-start(bf16[768,512]{1,0:T(8,128)(2,1)} %collective-permute-done.5), channel_id=1, source_target_pairs={{0,1},{1,0},{2,3},{3,2},{4,5},{5,4},{6,7},{7,6},{8,9},{9,8},{10,11... | collective-permute-start | bytes 2359304 | tf_op jit(solution)/shard_map/ppermute | solution.py:234
  156.4 92.7 %collective-permute-start.8 = (bf16[768,512]{1,0:T(8,128)(2,1)}, bf16[768,512]{1,0:T(8,128)(2,1)}, u32[]{:S(2)}, u32[]{:S(2)}) collective-permute-start(bf16[768,512]{1,0:T(8,128)(2,1)} %collective-permute-done.7), channel_id=1, source_target_pairs={{0,1},{1,0},{2,3},{3,2},{4,5},{5,4},{6,7},{7,6},{8,9},{9,8},{10,11... | collective-permute-start | bytes 2359304 | tf_op jit(solution)/shard_map/ppermute | solution.py:234
  156.9 110.8 %collective-permute-start.10 = (bf16[768,512]{1,0:T(8,128)(2,1)}, bf16[768,512]{1,0:T(8,128)(2,1)}, u32[]{:S(2)}, u32[]{:S(2)}) collective-permute-start(bf16[768,512]{1,0:T(8,128)(2,1)} %collective-permute-done.9), channel_id=1, source_target_pairs={{0,1},{1,0},{2,3},{3,2},{4,5},{5,4},{6,7},{7,6},{8,9},{9,8},{10,11... | collective-permute-start | bytes 2359304 | tf_op jit(solution)/shard_map/ppermute | solution.py:234
  158.6 125.8 %collective-permute-start.12 = (bf16[768,512]{1,0:T(8,128)(2,1)S(1)}, bf16[768,512]{1,0:T(8,128)(2,1)}, u32[]{:S(2)}, u32[]{:S(2)}) collective-permute-start(bf16[768,512]{1,0:T(8,128)(2,1)S(1)} %collective-permute-done.11), channel_id=1, source_target_pairs={{0,1},{1,0},{2,3},{3,2},{4,5},{5,4},{6,7},{7,6},{8,9},{9,8},{10,11... | collective-permute-start | bytes 2359304 | tf_op jit(solution)/shard_map/ppermute | solution.py:234
  159.4 142.2 %collective-permute-start.15 = (bf16[768,512]{1,0:T(8,128)(2,1)}, bf16[768,512]{1,0:T(8,128)(2,1)}, u32[]{:S(2)}, u32[]{:S(2)}) collective-permute-start(bf16[768,512]{1,0:T(8,128)(2,1)} %constant_dynamic-update-slice_fusion.2), channel_id=1, source_target_pairs={{0,1},{1,0},{2,3},{3,2},{4,5},{5,4},{6,7},{7,6},{8,9},{9,8},{10,11... | collective-permute-start | bytes 2359304 | tf_op jit(solution)/shard_map/ppermute | solution.py:234
  833.9 566.9 %reduce-scatter.2.cloned.1.call-start = ((), (), s32[]{:S(2)}) async-start(), calls=%async_computation.8 | async-start | bytes 8912896 | tf_op jit(solution)/shard_map/reduce_scatter | solution.py:543
  931.9 486.8 %all-reduce.2.cloned.1.call-start = ((), (), s32[]{:S(2)}) async-start(), calls=%async_computation.9 | async-start | bytes 524288 | tf_op jit(solution)/shard_map/psum | solution.py:604
  1021.6 95.0 %collective-permute-start.95 = (bf16[2,512,2048]{2,1,0:T(8,128)(2,1)}, bf16[2,512,2048]{2,1,0:T(8,128)(2,1)}, u32[]{:S(2)}, u32[]{:S(2)}) collective-permute-start(bf16[2,512,2048]{2,1,0:T(8,128)(2,1)} %fusion.23), channel_id=1, source_target_pairs={{0,16},{16,0},{1,17},{17,1},{2,18},{18,2},{3,19},{19,3},{4,20},{20... | collective-permute-start | bytes 12582920 | tf_op jit(solution)/shard_map/ppermute | solution.py:310
  1054.9 329.0 %collective-permute-start.94 = (bf16[2,1024,2048]{2,1,0:T(8,128)(2,1)}, bf16[2,1024,2048]{2,1,0:T(8,128)(2,1)}, u32[]{:S(2)}, u32[]{:S(2)}) collective-permute-start(bf16[2,1024,2048]{2,1,0:T(8,128)(2,1)} %convolution_convert_fusion.2), channel_id=1, source_target_pairs={{0,16},{16,0},{1,17},{17,1},{2,18},{18,2},{3,19},{19,3},{4,20},{20... | collective-permute-start | bytes 25165832 | tf_op jit(solution)/shard_map/ppermute | solution.py:310
  1063.2 64.3 %all-to-all-start.2 = ((bf16[192,4,512]{2,0,1:T(8,128)(2,1)}), bf16[192,4,512]{2,0,1:T(8,128)(2,1)S(1)}, u32[]{:S(2)}, u32[]{:S(2)}) async-start(bf16[192,4,512]{2,0,1:T(8,128)(2,1)} %bitcast.277), calls=%async_computation.2 | async-start | bytes 1572864 | tf_op jit(solution)/shard_map/all_to_all | solution.py:515
  1148.8 168.2 %collective-permute-start.82 = (bf16[768,512]{1,0:T(8,128)(2,1)}, bf16[768,512]{1,0:T(8,128)(2,1)}, u32[]{:S(2)}, u32[]{:S(2)}) collective-permute-start(bf16[768,512]{1,0:T(8,128)(2,1)} %get-tuple-element.71), channel_id=1, source_target_pairs={{0,1},{1,0},{2,3},{3,2},{4,5},{5,4},{6,7},{7,6},{8,9},{9,8},{10,11... | collective-permute-start | bytes 2359304 | tf_op jit(solution)/shard_map/ppermute | solution.py:256
  1148.8 162.0 %collective-permute-start.92 = (bf16[4,256,384]{1,2,0:T(8,128)(2,1)}, bf16[4,256,384]{1,2,0:T(8,128)(2,1)}, u32[]{:S(2)}, u32[]{:S(2)}) collective-permute-start(bf16[4,256,384]{1,2,0:T(8,128)(2,1)} %copy.247), channel_id=1, source_target_pairs={{0,16},{16,0},{1,17},{17,1},{2,18},{18,2},{3,19},{19,3},{4,20},{20... | collective-permute-start | bytes 2359304 | tf_op jit(solution)/shard_map/ppermute | solution.py:310
  1158.6 160.4 %collective-permute-start.85 = (bf16[768,512]{1,0:T(8,128)(2,1)}, bf16[768,512]{1,0:T(8,128)(2,1)}, u32[]{:S(2)}, u32[]{:S(2)}) collective-permute-start(bf16[768,512]{1,0:T(8,128)(2,1)} %pad_maximum_fusion.14), channel_id=1, source_target_pairs={{0,2},{1,3},{4,0},{5,1},{8,4},{9,5},{12,8},{13,9},{14,12},{15,13},... | collective-permute-start | bytes 2359304 | tf_op jit(solution)/shard_map/ppermute | solution.py:276
  1176.6 200.0 %collective-permute-start.81 = (bf16[768,512]{1,0:T(8,128)(2,1)}, bf16[768,512]{1,0:T(8,128)(2,1)S(1)}, u32[]{:S(2)}, u32[]{:S(2)}) collective-permute-start(bf16[768,512]{1,0:T(8,128)(2,1)} %get-tuple-element.72), channel_id=1, source_target_pairs={{0,1},{1,0},{2,3},{3,2},{4,5},{5,4},{6,7},{7,6},{8,9},{9,8},{10,11... | collective-permute-start | bytes 2359304 | tf_op jit(solution)/shard_map/ppermute | solution.py:256
  1310.8 103.5 %collective-permute-start.72 = (bf16[768,512]{1,0:T(8,128)(2,1)}, bf16[768,512]{1,0:T(8,128)(2,1)}, u32[]{:S(2)}, u32[]{:S(2)}) collective-permute-start(bf16[768,512]{1,0:T(8,128)(2,1)} %get-tuple-element.69), channel_id=1, source_target_pairs={{0,1},{1,0},{2,3},{3,2},{4,5},{5,4},{6,7},{7,6},{8,9},{9,8},{10,11... | collective-permute-start | bytes 2359304 | tf_op jit(solution)/shard_map/ppermute | solution.py:256
  1313.0 67.4 %all-to-all-start.6 = ((bf16[4,256,384]{1,2,0:T(8,128)(2,1)}), bf16[4,256,384]{1,2,0:T(8,128)(2,1)S(1)}, u32[]{:S(2)}, u32[]{:S(2)}) async-start(bf16[4,256,384]{1,2,0:T(8,128)(2,1)} %add_convert_fusion), calls=%async_computation.6 | async-start | bytes 1572864 | tf_op jit(solution)/shard_map/all_to_all | solution.py:316
  (163 other events, 4226.7 us)
Sparse Core Ops, SparseCore 0:
  10.2 122.6 all-gather.4
  329.7 123.5 all-gather.6
  932.0 104.0 reduce-scatter.1
  1062.4 129.7 all-reduce.1

commit v2 on v1

v2 whole, which is shorter than its diff:
```python
import functools
import math

import jax
import jax.numpy as jnp
from jax import lax
from jax.experimental import pallas as pl
from jax.experimental.pallas import tpu as pltpu
from jax.sharding import PartitionSpec as P

D = 2048
HD = 128
F = 1024
TOP = 8
CORES = 2
PLANE = ("row", "col")
BLOCKS = ("col", "row")
LOG2E = math.log2(math.e)
MASKED = -1e30

norm_epsilon = 1e-05
rope_base = 10000.0
bf16 = jnp.bfloat16
f32 = jnp.float32


def dot_nt(a, b):
    return lax.dot_general(a, b, (((1,), (1,)), ((), ())), preferred_element_type=f32)


def dot_nn(a, b):
    return lax.dot_general(a, b, (((1,), (0,)), ((), ())), preferred_element_type=f32)


def cost(microseconds):
    return pl.CostEstimate(flops=int(microseconds * 1.1e9), bytes_accessed=0, transcendentals=0)


def as_row(column):
    return jnp.broadcast_to(column, (column.shape[0], 128)).T[:1]


def as_column(row):
    return jnp.broadcast_to(row, (8, row.shape[1])).T[:, :1]


def key_limits(first_query, query_rows, key_rows, prefix):
    open_blocks = jnp.maximum((first_query + 1) // key_rows, prefix // key_rows)
    all_blocks = pl.cdiv(jnp.maximum(first_query + query_rows, prefix), key_rows)
    return open_blocks, all_blocks


def mask_scores(scores, first_key, first_query, prefix):
    keys = first_key + lax.broadcasted_iota(jnp.int32, scores.shape, 0)
    queries = first_query + lax.broadcasted_iota(jnp.int32, scores.shape, 1)
    return jnp.where((keys <= queries) | (keys < prefix), scores, MASKED)


def attention_kernel(scale, prefix_ref, q_ref, k_ref, v_flip_ref, out_ref, lse_ref, scores_ref):
    query_rows = q_ref.shape[0]
    key_rows = min(512, k_ref.shape[0])
    first_query = pl.program_id(0) * query_rows
    prefix = prefix_ref[0]
    q = q_ref[...]
    open_blocks, all_blocks = key_limits(first_query, query_rows, key_rows, prefix)

    def score(j, top, masked):
        start = pl.multiple_of(j * key_rows, key_rows)
        scores = dot_nt(k_ref[pl.ds(start, key_rows), :], q) * (scale * LOG2E)
        if masked:
            scores = mask_scores(scores, start, first_query, prefix)
        scores_ref[pl.ds(start, key_rows), :] = scores
        return jnp.maximum(top, jnp.max(scores.reshape(key_rows // 8, 8, query_rows), axis=0))

    top = jnp.full((8, query_rows), MASKED, f32)
    top = lax.fori_loop(0, open_blocks, lambda j, t: score(j, t, False), top)
    top = lax.fori_loop(open_blocks, all_blocks, lambda j, t: score(j, t, True), top)
    peak = jnp.max(top, axis=0, keepdims=True)

    def mix(j, carry):
        total, mixed = carry
        start = pl.multiple_of(j * key_rows, key_rows)
        weights = jnp.exp2(scores_ref[pl.ds(start, key_rows), :] - peak)
        total = total + jnp.sum(weights.reshape(key_rows // 8, 8, query_rows), axis=0)
        mixed = mixed + dot_nn(v_flip_ref[:, pl.ds(start, key_rows)], weights.astype(bf16))
        return total, mixed

    total, mixed = lax.fori_loop(
        0,
        all_blocks,
        mix,
        (jnp.zeros((8, query_rows), f32), jnp.zeros((q.shape[1], query_rows), f32)),
    )
    total = jnp.sum(total, axis=0, keepdims=True)
    out_ref[...] = (mixed / total).T.astype(out_ref.dtype)
    lse_ref[...] = peak + jnp.log2(total)


def attention(q, k, v_flip, prefix_len, query_rows):
    length, width = q.shape
    query_block = pl.BlockSpec((query_rows, width), lambda i, p: (i, 0))
    return pl.pallas_call(
        functools.partial(attention_kernel, width**-0.5),
        grid_spec=pltpu.PrefetchScalarGridSpec(
            num_scalar_prefetch=1,
            grid=(length // query_rows,),
            in_specs=[
                query_block,
                pl.BlockSpec((length, width), lambda i, p: (0, 0)),
                pl.BlockSpec((width, length), lambda i, p: (0, 0)),
            ],
            out_specs=[query_block, pl.BlockSpec((1, query_rows), lambda i, p: (0, i))],
            scratch_shapes=[pltpu.VMEM((length, query_rows), f32)],
        ),
        out_shape=[
            jax.ShapeDtypeStruct((length, width), bf16),
            jax.ShapeDtypeStruct((1, length), f32),
        ],
        compiler_params=pltpu.CompilerParams(vmem_limit_bytes=40 * 2**20),
        cost_estimate=cost(17),
        name="attention_forward",
    )(prefix_len, q, k, v_flip)


def attention_back_kernel(
    scale, prefix_ref, q_ref, grad_ref, lse_ref, centre_ref, k_ref, k_flip_ref, v_ref,
    grad_q_ref, grad_k_ref, grad_v_ref, dot_q_ref, dot_k_ref, dot_v_ref,
):
    query_rows = q_ref.shape[0]
    key_rows = min(512, k_ref.shape[0])
    step = pl.program_id(0)
    first_query = step * query_rows
    prefix = prefix_ref[0]

    @pl.when(step == 0)
    def _():
        grad_k_ref[...] = jnp.zeros_like(grad_k_ref)
        grad_v_ref[...] = jnp.zeros_like(grad_v_ref)

    q = q_ref[...]
    grad = grad_ref[...]
    lse = lse_ref[...]
    centre = centre_ref[...]
    open_blocks, all_blocks = key_limits(first_query, query_rows, key_rows, prefix)

    def block(j, total, masked):
        start = pl.multiple_of(j * key_rows, key_rows)
        rows = pl.ds(start, key_rows)
        scores = dot_nt(k_ref[rows, :], q) * (scale * LOG2E) - lse
        if masked:
            scores = mask_scores(scores, start, first_query, prefix)
        weights = jnp.exp2(scores)
        grad_weights = dot_nt(v_ref[rows, :], grad)
        grad_scores = (weights * (grad_weights - centre)).astype(bf16)
        grad_v_ref[rows, :] += dot_nn(weights.astype(bf16), grad)
        grad_k_ref[rows, :] += dot_nn(grad_scores, q)
        return total + dot_nn(k_flip_ref[:, rows], grad_scores)

    total = jnp.zeros((q.shape[1], query_rows), f32)
    total = lax.fori_loop(0, open_blocks, lambda j, a: block(j, a, False), total)
    total = lax.fori_loop(open_blocks, all_blocks, lambda j, a: block(j, a, True), total)
    grad_q = total.T * scale
    grad_q_ref[...] = grad_q
    dot_q_ref[...] = as_row(jnp.sum(grad_q * q.astype(f32), axis=1, keepdims=True))

    @pl.when(step == pl.num_programs(0) - 1)
    def _():
        for start in range(0, k_ref.shape[0], key_rows):
            rows = pl.ds(start, key_rows)
            grad_k = grad_k_ref[rows, :] * scale
            grad_k_ref[rows, :] = grad_k
            dot_k_ref[:, rows] = as_row(
                jnp.sum(grad_k * k_ref[rows, :].astype(f32), axis=1, keepdims=True)
            )
            dot_v_ref[:, rows] = as_row(
                jnp.sum(grad_v_ref[rows, :] * v_ref[rows, :].astype(f32), axis=1, keepdims=True)
            )


def attention_back(q, k, k_flip, v, grad, lse, centre, prefix_len, query_rows):
    length, width = q.shape
    whole = pl.BlockSpec((length, width), lambda i, p: (0, 0))
    flipped = pl.BlockSpec((width, length), lambda i, p: (0, 0))
    query_block = pl.BlockSpec((query_rows, width), lambda i, p: (i, 0))
    query_row = pl.BlockSpec((1, query_rows), lambda i, p: (0, i))
    result = jax.ShapeDtypeStruct((length, width), f32)
    return pl.pallas_call(
        functools.partial(attention_back_kernel, width**-0.5),
        grid_spec=pltpu.PrefetchScalarGridSpec(
            num_scalar_prefetch=1,
            grid=(length // query_rows,),
            in_specs=[query_block, query_block, query_row, query_row, whole, flipped, whole],
            out_specs=[query_block, whole, whole, query_row] + [pl.BlockSpec((1, length), lambda i, p: (0, 0))] * 2,
        ),
        out_shape=[result, result, result] + [jax.ShapeDtypeStruct((1, length), f32)] * 3,
        compiler_params=pltpu.CompilerParams(vmem_limit_bytes=40 * 2**20),
        cost_estimate=cost(24),
        name="attention_backward",
    )(prefix_len, q, grad, lse, centre, k, k_flip, v)


def unwritten(shape, dtype):
    return pl.pallas_call(
        lambda out_ref: None,
        out_specs=pl.BlockSpec(memory_space=pl.ANY),
        out_shape=jax.ShapeDtypeStruct(shape, dtype),
        name="buffer",
    )()


def add_low(one, two):
    return (one.astype(f32) + two.astype(f32)).astype(bf16)


def after(value, earlier):
    return lax.optimization_barrier((value, earlier))[0]


def together(*values):
    return lax.optimization_barrier(values)


class Ring:
    def __init__(self, rows, cols):
        self.rows, self.cols = rows, cols
        self.cores = CORES if cols % CORES == 0 else 1
        self.groups = cols // self.cores
        self.order = [
            (row, group)
            for group in range(self.groups)
            for row in (range(rows) if group % 2 == 0 else range(rows - 1, -1, -1))
        ]
        self.size = len(self.order)
        self.clockwise = self.shift(1)
        self.counter = self.shift(-1)
        self.sibling = [
            (row * cols + col, row * cols + col - col % self.cores + (col + 1) % self.cores)
            for row in range(rows)
            for col in range(cols)
        ]
        row, col = lax.axis_index("row"), lax.axis_index("col")
        group = col // self.cores
        self.core = col % self.cores
        self.place = group * rows + jnp.where(group % 2 == 0, row, rows - 1 - row)

    def shift(self, step):
        pairs = []
        for at, (row, group) in enumerate(self.order):
            to_row, to_group = self.order[(at + step) % self.size]
            for core in range(self.cores):
                pairs.append(
                    (
                        row * self.cols + group * self.cores + core,
                        to_row * self.cols + to_group * self.cores + core,
                    )
                )
        return pairs

    def chip(self, distance):
        at = (self.place + distance + self.size) % self.size
        group = at // self.rows
        along = at % self.rows
        return jnp.where(group % 2 == 0, along, self.rows - 1 - along), group

    def owners(self, distance):
        row, group = self.chip(distance)
        return [(row, group * self.cores + (self.core + k) % self.cores) for k in range(self.cores)]

    def block_ids(self, distance):
        return [col * self.rows + row for row, col in self.owners(distance)]

    def from_siblings(self, block):
        return [block] + [lax.ppermute(block, PLANE, self.sibling)] * (self.cores - 1)

    def gather_steps(self, block):
        forth = back = block
        yield [(block, 0)]
        for step in range(1, (self.size + 1) // 2):
            forth = lax.ppermute(forth, PLANE, self.clockwise)
            back = lax.ppermute(back, PLANE, self.counter)
            sent = yield [(forth, -step), (back, step)]
            if sent is not None:
                forth, back = sent
        if self.size % 2 == 0:
            half = block.shape[0] // 2
            forth = lax.ppermute(forth[:half], PLANE, self.clockwise)
            back = lax.ppermute(back[half:], PLANE, self.counter)
            yield [(jnp.concatenate([forth, back], axis=0), self.size // 2)]

    def with_siblings(self, arrival):
        return [
            pair
            for piece, distance in arrival
            for pair in zip(self.from_siblings(piece), self.block_ids(distance))
        ]

    def place_blocks(self, box, pairs):
        for piece, ident in pairs:
            start = (ident,) + (0,) * piece.ndim
            box = lax.dynamic_update_slice(box, piece[None], start)
        return box

    def gather_array(self, block):
        box = unwritten((self.rows * self.cols,) + block.shape, block.dtype)
        for arrival in self.gather_steps(block):
            box = self.place_blocks(box, self.with_siblings(arrival))
        return box

    def chip_sum(self, mine, *others):
        for other in others:
            mine = add_low(mine, lax.ppermute(other, PLANE, self.sibling))
        return mine

    def scatter_steps(self, parts):
        forth = back = None
        half = 0
        if self.size % 2 == 0:
            far = parts(self.size // 2)
            half = far.shape[0] // 2
            forth = lax.ppermute(far[:half], PLANE, self.clockwise)
            back = lax.ppermute(far[half:], PLANE, self.counter)
            forth, back = yield forth, back
        for step in range((self.size - 1) // 2, 0, -1):
            ahead, behind = parts(step), parts(-step)
            if forth is None:
                forth, back = ahead, behind
            elif forth.shape[0] == half:
                forth = jnp.concatenate([add_low(ahead[:half], forth), ahead[half:]], axis=0)
                back = jnp.concatenate([behind[:half], add_low(behind[half:], back)], axis=0)
            else:
                forth, back = add_low(ahead, forth), add_low(behind, back)
            forth = lax.ppermute(forth, PLANE, self.clockwise)
            back = lax.ppermute(back, PLANE, self.counter)
            forth, back = yield forth, back
        yield parts(0), forth, back

    def scatter_parts(self, parts):
        steps = self.scatter_steps(parts)
        terms = next(steps)
        while len(terms) == 2:
            terms = steps.send(terms)
        return terms

    def distances(self):
        half = (self.size - 1) // 2
        far = [self.size // 2] if self.size % 2 == 0 else []
        return [0] + [d for step in range(1, half + 1) for d in (-step, step)] + far

    def sum_steps(self, values):
        rows, cols = self.rows, self.cols
        if rows & (rows - 1) or cols & (cols - 1):
            yield lax.psum(values, PLANE)
            return
        swaps = []
        bit = 1
        while bit < cols:
            swaps.append(lambda row, col, bit=bit: (row, col ^ bit))
            bit *= 2
        bit = 1
        while bit < rows:
            swaps.append(lambda row, col, bit=bit: (row ^ bit, col))
            bit *= 2
        for swap in swaps:
            pairs = []
            for row in range(rows):
                for col in range(cols):
                    to_row, to_col = swap(row, col)
                    pairs.append((row * cols + col, to_row * cols + to_col))
            values = values + lax.ppermute(values, PLANE, pairs)
            sent = yield values
            values = values if sent is None else sent

    def small_sum(self, values):
        *_, last = self.sum_steps(values)
        return last


def dp_sum(part):
    count = lax.axis_size("dp")
    rank = lax.axis_index("dp")
    if count == 1:
        return part(rank)
    onward = [(d, (d + 1) % count) for d in range(count)]
    total = part((rank + count - 1) % count)
    for step in range(1, count):
        arrived = lax.ppermute(total.astype(bf16), "dp", onward)
        total = part((rank + 2 * count - 1 - step) % count) + arrived.astype(f32)
    return total


def dp_all_sum(values):
    count = lax.axis_size("dp")
    if count & (count - 1):
        return lax.psum(values, "dp")
    bit = 1
    while bit < count:
        values = values + lax.ppermute(values, "dp", [(d, d ^ bit) for d in range(count)])
        bit *= 2
    return values


def exchange_rows(pieces):
    rows = pieces.shape[0]
    row = lax.axis_index("row")
    start = lambda at: (at,) + (0,) * (pieces.ndim - 1)
    taken = unwritten(pieces.shape, pieces.dtype)
    own = lax.dynamic_index_in_dim(pieces, row, 0, True)
    taken = lax.dynamic_update_slice(taken, own, start(row))
    for step in range(1, rows):
        sent = lax.dynamic_index_in_dim(pieces, (row + step) % rows, 0, True)
        sent = lax.ppermute(sent, "row", [(r, (r + step) % rows) for r in range(rows)])
        taken = lax.dynamic_update_slice(taken, sent, start((row + rows - step) % rows))
    return taken


def exchange(pieces, axes):
    return lax.all_to_all(pieces, axes, split_axis=0, concat_axis=0, tiled=True)


def project_kernel(x_ref, gain_ref, weight_ref, out_ref, inverse_ref, squares_ref, low_ref):
    blocks, _, width = x_ref.shape
    total = 0.0
    for block in range(blocks):
        part = x_ref[block].astype(f32)
        total = total + jnp.sum(part * part, axis=1, keepdims=True)
    inverse = lax.rsqrt(total / D + norm_epsilon)
    for block in range(blocks):
        at = pl.ds(block * width, width)
        low_ref[:, at] = (x_ref[block].astype(f32) * inverse * gain_ref[:, at]).astype(bf16)
    out = dot_nn(low_ref[...], weight_ref[...])
    out_ref[...] = out
    inverse_ref[...] = as_row(inverse)
    for j in range(2):
        part = out[:, j * HD : (j + 1) * HD]
        squares_ref[pl.ds(j, 1), :] = as_row(jnp.sum(part * part, axis=1, keepdims=True))


def project(x_blocks, gain_row, weight, rows):
    count, block_rows, width = x_blocks.shape
    cols = count // rows
    tile = block_rows
    per = block_rows // tile
    length = cols * block_rows
    return pl.pallas_call(
        project_kernel,
        grid=(cols * per,),
        in_specs=[
            pl.BlockSpec((rows, tile, width), lambda i: (i // per, i % per, 0)),
            pl.BlockSpec((1, D), lambda i: (0, 0)),
            pl.BlockSpec(weight.shape, lambda i: (0, 0)),
        ],
        out_specs=[
            pl.BlockSpec((tile, 3 * HD), lambda i: (i, 0)),
            pl.BlockSpec((1, tile), lambda i: (0, i)),
            pl.BlockSpec((2, tile), lambda i: (0, i)),
        ],
        scratch_shapes=[pltpu.VMEM((tile, D), bf16)],
        out_shape=[
            jax.ShapeDtypeStruct((length, 3 * HD), f32),
            jax.ShapeDtypeStruct((1, length), f32),
            jax.ShapeDtypeStruct((2, length), f32),
        ],
        compiler_params=pltpu.CompilerParams(vmem_limit_bytes=52 * 2**20),
        cost_estimate=cost(14),
        name="norm_and_project",
    )(x_blocks, gain_row, weight)


def project_weight_kernel(x_ref, gain_ref, inverse_ref, grad_ref, out_ref, low_ref):
    blocks, _, width = x_ref.shape
    inverse = as_column(inverse_ref[...])

    @pl.when(pl.program_id(0) == 0)
    def _():
        out_ref[...] = jnp.zeros_like(out_ref)

    for block in range(blocks):
        at = pl.ds(block * width, width)
        low_ref[:, at] = (x_ref[block].astype(f32) * inverse * gain_ref[:, at]).astype(bf16)
    for block in range(blocks):
        at = pl.ds(block * width, width)
        out_ref[at, :] += dot_nn(low_ref[:, at].T, grad_ref[...])


def project_weight(x_blocks, gain_row, inverse, grads, rows):
    count, block_rows, width = x_blocks.shape
    cols = count // rows
    tile = block_rows // 3 if block_rows % 384 == 0 else block_rows
    per = block_rows // tile
    return pl.pallas_call(
        project_weight_kernel,
        grid=(cols * per,),
        in_specs=[
            pl.BlockSpec((rows, tile, width), lambda i: (i // per, i % per, 0)),
            pl.BlockSpec((1, D), lambda i: (0, 0)),
            pl.BlockSpec((1, tile), lambda i: (0, i)),
            pl.BlockSpec((tile, 3 * HD), lambda i: (i, 0)),
        ],
        out_specs=pl.BlockSpec((D, 3 * HD), lambda i: (0, 0)),
        scratch_shapes=[pltpu.VMEM((tile, D), bf16)],
        out_shape=jax.ShapeDtypeStruct((D, 3 * HD), f32),
        compiler_params=pltpu.CompilerParams(vmem_limit_bytes=40 * 2**20),
        cost_estimate=cost(15),
        name="projection_weight_gradient",
    )(x_blocks, gain_row, inverse, grads)


def turn_kernel(raw_ref, squares_ref, gain_ref, cosine_ref, sine_ref, q_ref, k_ref, v_ref, k_flip_ref, v_flip_ref):
    inverse = lax.rsqrt(squares_ref[...] / D + norm_epsilon)
    for j, out_ref in ((0, q_ref), (1, k_ref)):
        normed = raw_ref[:, j * HD : (j + 1) * HD] * as_column(inverse[j : j + 1]) * gain_ref[j : j + 1, :]
        turned = normed * cosine_ref[...] + jnp.roll(normed, HD // 2, axis=1) * sine_ref[...]
        out_ref[...] = turned.astype(bf16)
        if j == 1:
            k_flip_ref[...] = turned.T.astype(bf16)
    v = raw_ref[:, 2 * HD :]
    v_ref[...] = v.astype(bf16)
    v_flip_ref[...] = v.T.astype(bf16)


def turn(raw, squares, gain_pair, cosine, sine_part):
    length = raw.shape[0]
    tile = min(1024, length)
    tall = pl.BlockSpec((tile, HD), lambda i: (i, 0))
    wide = pl.BlockSpec((HD, tile), lambda i: (0, i))
    tall_shape = jax.ShapeDtypeStruct((length, HD), bf16)
    wide_shape = jax.ShapeDtypeStruct((HD, length), bf16)
    return pl.pallas_call(
        turn_kernel,
        grid=(length // tile,),
        in_specs=[
            pl.BlockSpec((tile, 3 * HD), lambda i: (i, 0)),
            pl.BlockSpec((2, tile), lambda i: (0, i)),
            pl.BlockSpec((2, HD), lambda i: (0, 0)),
            tall,
            tall,
        ],
        out_specs=[tall, tall, tall, wide, wide],
        out_shape=[tall_shape, tall_shape, tall_shape, wide_shape, wide_shape],
        cost_estimate=cost(7.4),
        name="query_key_value",
    )(raw, squares, gain_pair, cosine, sine_part)


def branch_kernel(
    groups, sets, at_ref, heads_ref, x_ref, gain_ref, *refs
):
    weights, (residual_ref, low_ref) = refs[: groups * sets], refs[groups * sets :]
    step = pl.program_id(0)
    rows, width = x_ref.shape[0], x_ref.shape[2]
    height = weights[0].shape[1]
    per = height // HD
    branch = x_ref[pl.ds(step, 1)][0].astype(f32)
    for group in range(groups):
        for k in range(sets):
            first = at_ref[2 + group * sets + k]
            heads = jnp.concatenate([heads_ref[first + j] for j in range(per)], axis=1)
            branch = branch + dot_nn(heads, weights[group * sets + k][0])
    residual_ref[:, pl.ds(pl.multiple_of(step * width, width), width)] = branch

    @pl.when(step == rows - 1)
    def _():
        total = residual_ref[...]
        inverse = lax.rsqrt(jnp.sum(total * total, axis=1, keepdims=True) / D + norm_epsilon)
        low_ref[...] = (total * inverse * gain_ref[...]).astype(bf16)


def output_branch(at, table, heads, weight_sets, x_blocks, gain_row, rows, groups):
    tok_rows = heads.shape[1]
    sets = len(weight_sets)
    _, height, width = weight_sets[0].shape
    fixed = lambda shape: pl.BlockSpec(shape, lambda i, a, t: (0,) * len(shape))
    return pl.pallas_call(
        lambda at_ref, table_ref, *refs: branch_kernel(groups, sets, at_ref, *refs),
        grid_spec=pltpu.PrefetchScalarGridSpec(
            num_scalar_prefetch=2,
            grid=(rows,),
            in_specs=[
                fixed(heads.shape),
                pl.BlockSpec((rows, tok_rows, width), lambda i, a, t: (a[0], a[1], 0)),
                fixed((1, D)),
            ]
            + [
                pl.BlockSpec(
                    (1, height, width), lambda i, a, t, g=g, k=k: (t[(k * groups + g) * rows + i], 0, 0)
                )
                for g in range(groups)
                for k in range(sets)
            ],
            out_specs=[fixed((tok_rows, D)), fixed((tok_rows, D))],
        ),
        out_shape=[
            jax.ShapeDtypeStruct((tok_rows, D), f32),
            jax.ShapeDtypeStruct((tok_rows, D), bf16),
        ],
        compiler_params=pltpu.CompilerParams(vmem_limit_bytes=40 * 2**20),
        cost_estimate=cost(6),
        name="output_projection",
    )(at, table, heads, x_blocks, gain_row, *[w for _ in range(groups) for w in weight_sets])


def resid_kernel(
    at_ref, own_ref, forth_ref, back_ref, logit_ref, router_ref, residual_ref, up_ref, gain_ref,
    grad_low_ref, gain_term_ref,
):
    rows, width = up_ref.shape[0], up_ref.shape[2]
    grad = own_ref[...].astype(f32) + forth_ref[...].astype(f32) + back_ref[...].astype(f32)
    grad = grad + dot_nn(logit_ref[...], router_ref[...])
    residual = residual_ref[...]
    inverse = lax.rsqrt(jnp.sum(residual * residual, axis=1, keepdims=True) / D + norm_epsilon)
    scaled = grad * gain_ref[...]
    total = jnp.sum(scaled * residual, axis=1, keepdims=True)
    gain_term_ref[...] = jnp.sum(grad * residual * inverse, axis=0, keepdims=True)
    back = inverse * scaled - residual * (inverse * inverse * inverse * total / D)
    for row in range(rows):
        at = pl.ds(row * width, width)
        grad_low_ref[:, at] = (
            up_ref[row].astype(f32) + back[:, row * width : (row + 1) * width]
        ).astype(bf16)


def residual_back(at, terms, grad_logits, router_flip, residual, up_blocks, gain_row, rows):
    tok_rows = residual.shape[0]
    width = up_blocks.shape[2]
    fixed = lambda shape: pl.BlockSpec(shape, lambda i, a: (0,) * len(shape))
    whole, line = fixed((tok_rows, D)), fixed((1, D))
    return pl.pallas_call(
        resid_kernel,
        grid_spec=pltpu.PrefetchScalarGridSpec(
            num_scalar_prefetch=1,
            grid=(1,),
            in_specs=[
                whole,
                whole,
                whole,
                fixed(grad_logits.shape),
                fixed(router_flip.shape),
                whole,
                pl.BlockSpec((rows, tok_rows, width), lambda i, a: (a[0], a[1], 0)),
                line,
            ],
            out_specs=[whole, line],
        ),
        out_shape=[
            jax.ShapeDtypeStruct((tok_rows, D), bf16),
            jax.ShapeDtypeStruct((1, D), f32),
        ],
        compiler_params=pltpu.CompilerParams(vmem_limit_bytes=40 * 2**20),
        cost_estimate=cost(3),
        name="residual_backward",
    )(at, *terms, grad_logits, router_flip, residual, up_blocks, gain_row)


def dispatch_kernel(hits_ref, x_ref, out_ref):
    experts, _, capacity, _ = out_ref.shape
    width = x_ref.shape[2]
    for block in range(x_ref.shape[0]):
        picked = dot_nn(hits_ref[0], x_ref[block]).astype(bf16)
        for e in range(experts):
            out_ref[e, 0, :, pl.ds(block * width, width)] = picked[e * capacity : (e + 1) * capacity]


def dispatch_blocks(hits, x_blocks, rows, experts):
    group, slot_rows, tok_rows = hits.shape
    width = x_blocks.shape[2]
    capacity = slot_rows // experts
    return pl.pallas_call(
        dispatch_kernel,
        grid=(group,),
        in_specs=[
            pl.BlockSpec((1, slot_rows, tok_rows), lambda b: (b, 0, 0)),
            pl.BlockSpec((rows, tok_rows, width), lambda b: (b // rows, b % rows, 0)),
        ],
        out_specs=pl.BlockSpec((experts, 1, capacity, D), lambda b: (0, b, 0, 0)),
        out_shape=jax.ShapeDtypeStruct((experts, group, capacity, D), bf16),
        cost_estimate=cost(14),
        name="cotangent_to_slots",
    )(hits, x_blocks)


def experts_kernel(count, first, ids_ref, *refs):
    feats = refs[:count]
    raws = refs[count : 2 * count]
    hits_ref, flip_ref, router_ref, gate_w_ref, up_w_ref = refs[2 * count : 2 * count + 5]
    rest = refs[2 * count + 5 :]
    if not first:
        rest = rest[5:]
    slot_ref, hidden_ref, grad_gate_ref, grad_up_ref, scale_ref = rest[:5]
    feat_sums = rest[5 : 5 + count]
    probs_ref, in_acc, in_all = rest[5 + count :]
    e, f = pl.program_id(0), pl.program_id(1)
    last_expert = e == pl.num_programs(0) - 1
    last_tile = f == pl.num_programs(1) - 1
    capacity = raws[0].shape[2]
    chosen = ids_ref[count] + e
    own_slots = pl.ds(pl.multiple_of(e * capacity, 16), capacity)

    @pl.when((e == 0) & (f == 0))
    def _():
        for k in range(count):
            logits = dot_nt(router_ref[...], feats[k][...])
            raised = jnp.exp(logits - jnp.max(logits, axis=0, keepdims=True))
            probs_ref[k] = raised / jnp.sum(raised, axis=0, keepdims=True)

    @pl.when(f == 0)
    def _():
        for k in range(count):
            at = pl.ds(k * capacity, capacity)
            hits = hits_ref[ids_ref[k], own_slots, :]
            slot_ref[0, at, :] = dot_nn(hits, feats[k][...]).astype(bf16)
            probs = probs_ref[k]
            rank = lax.broadcasted_iota(jnp.int32, probs.shape, 0)
            gate = jnp.sum(jnp.where(rank == chosen, probs, 0.0), axis=0, keepdims=True)
            scale_ref[0, at, :] = jnp.sum(hits.astype(f32) * gate, axis=1, keepdims=True)

    slots = slot_ref[0]
    gate_w, up_w = gate_w_ref[0], up_w_ref[0]
    gate_pre = dot_nn(slots, gate_w)
    up_pre = dot_nn(slots, up_w)
    sigmoid = 1.0 / (1.0 + jnp.exp(-gate_pre))
    silu = gate_pre * sigmoid
    hidden_ref[0] = (silu * up_pre).astype(bf16)
    grad_hidden = jnp.concatenate([raw[0, 0] for raw in raws], axis=0) * scale_ref[0]
    grad_gate = (grad_hidden * up_pre * sigmoid * (1.0 + gate_pre * (1.0 - sigmoid))).astype(bf16)
    grad_up = (grad_hidden * silu).astype(bf16)
    grad_gate_ref[0] = grad_gate
    grad_up_ref[0] = grad_up
    in_term = dot_nt(grad_gate, gate_w) + dot_nt(grad_up, up_w)

    @pl.when(f == 0)
    def _():
        in_acc[...] = in_term

    @pl.when(f > 0)
    def _():
        in_acc[...] += in_term

    @pl.when(last_tile)
    def _():
        for k in range(count):
            in_all[k, own_slots, :] = in_acc[pl.ds(k * capacity, capacity), :].astype(bf16)

    @pl.when(last_tile & last_expert)
    def _():
        for k in range(count):
            feat_sums[k][...] = dot_nn(flip_ref[ids_ref[k]], in_all[k]).astype(bf16)


def run_experts(feats, ids, first_expert, grad_raw, hits, flip, router_flip, expand_weight, carried, place):
    count = len(feats)
    experts, group, capacity, _ = grad_raw.shape
    tok_rows = feats[0].shape[0]
    rows = count * capacity
    tile = F // 2
    tiles = F // tile
    first = carried is None
    whole = lambda shape: pl.BlockSpec(shape, lambda e, f, ids: (0,) * len(shape))
    in_specs = [whole((tok_rows, D))] * count
    in_specs += [
        pl.BlockSpec((1, 1, capacity, tile), lambda e, f, ids, k=k: (e, ids[k], 0, f))
        for k in range(count)
    ]
    in_specs += [
        whole(hits.shape),
        whole(flip.shape),
        whole(router_flip.shape),
        pl.BlockSpec((1, D, tile), lambda e, f, ids: (e, 0, f)),
        pl.BlockSpec((1, D, tile), lambda e, f, ids: (e, 0, f + tiles)),
    ]
    operands = [*feats, *[grad_raw] * count, hits, flip, router_flip, expand_weight, expand_weight]
    aliases = {}
    if not first:
        in_specs += [pl.BlockSpec(memory_space=pl.ANY)] * 5
        operands += carried
        aliases = {1 + len(operands) - 5 + k: k for k in range(5)}
    wide = pl.BlockSpec((1, rows, D), lambda e, f, ids: (e, place, 0))
    narrow = pl.BlockSpec((1, rows, tile), lambda e, f, ids: (e, place, f))
    thin = pl.BlockSpec((1, rows, 1), lambda e, f, ids: (e, place, 0))
    narrow_shape = jax.ShapeDtypeStruct((experts, group * capacity, F), bf16)
    out = pl.pallas_call(
        functools.partial(experts_kernel, count, first),
        grid_spec=pltpu.PrefetchScalarGridSpec(
            num_scalar_prefetch=1,
            grid=(experts, tiles),
            in_specs=in_specs,
            out_specs=[wide, narrow, narrow, narrow, thin] + [whole((tok_rows, D))] * count,
            scratch_shapes=[
                pltpu.VMEM((count, router_flip.shape[0], tok_rows), f32),
                pltpu.VMEM((rows, D), f32),
                pltpu.VMEM((count, experts * capacity, D), bf16),
            ],
        ),
        out_shape=[jax.ShapeDtypeStruct((experts, group * capacity, D), bf16)]
        + [narrow_shape] * 3
        + [jax.ShapeDtypeStruct((experts, group * capacity, 1), f32)]
        + [jax.ShapeDtypeStruct((tok_rows, D), bf16)] * count,
        input_output_aliases=aliases,
        compiler_params=pltpu.CompilerParams(vmem_limit_bytes=56 * 2**20),
        cost_estimate=cost(13 + 2 * count),
        name="experts",
    )(jnp.stack([*ids, first_expert]).astype(jnp.int32), *operands)
    return out[:5], out[5:]


def combine_kernel(ids_ref, out_ref, up_ref, hits_ref, flip_ref, scale_ref, gates_ref, grad_out_ref, moe_ref):
    experts, _, capacity, _ = out_ref.shape
    scaled = []
    for e in range(experts):
        expert_out = out_ref[e, 0].astype(f32)
        upstream = up_ref[e, 0].astype(f32)
        scale = scale_ref[e, 0]
        dots = jnp.sum(expert_out * upstream, axis=1, keepdims=True)
        hits = hits_ref[0, e * capacity : (e + 1) * capacity, :].astype(f32)
        gates_ref[0, pl.ds(e, 1), :] = jnp.sum(hits * dots, axis=0, keepdims=True)
        grad_out_ref[e, 0] = (upstream * scale).astype(bf16)
        scaled.append((expert_out * scale).astype(bf16))
    moe_ref[0] = dot_nn(flip_ref[0], jnp.concatenate(scaled, axis=0)).astype(bf16)


def combine_experts(ids, expert_out, upstream_slots, hits, flip, scale):
    experts, group, capacity, _ = upstream_slots.shape
    tok_rows = hits.shape[2]
    by_place = pl.BlockSpec((experts, 1, capacity, D), lambda j, ids: (0, j, 0, 0))
    by_id = lambda shape: pl.BlockSpec((1,) + shape, lambda j, ids: (ids[j], 0, 0))
    return pl.pallas_call(
        combine_kernel,
        grid_spec=pltpu.PrefetchScalarGridSpec(
            num_scalar_prefetch=1,
            grid=(group,),
            in_specs=[
                by_place,
                pl.BlockSpec((experts, 1, capacity, D), lambda j, ids: (0, ids[j], 0, 0)),
                by_id(hits.shape[1:]),
                by_id(flip.shape[1:]),
                pl.BlockSpec((experts, 1, capacity, 1), lambda j, ids: (0, j, 0, 0)),
            ],
            out_specs=[by_id((experts, tok_rows)), by_place, by_id((tok_rows, D))],
        ),
        out_shape=[
            jax.ShapeDtypeStruct((group, experts, tok_rows), f32),
            jax.ShapeDtypeStruct((experts, group, capacity, D), bf16),
            jax.ShapeDtypeStruct((group, tok_rows, D), bf16),
        ],
        compiler_params=pltpu.CompilerParams(vmem_limit_bytes=40 * 2**20),
        cost_estimate=cost(18),
        name="experts_combine",
    )(
        ids,
        expert_out.reshape(experts, group, capacity, D),
        upstream_slots,
        hits,
        flip,
        scale.reshape(experts, group, capacity, 1),
    )


def weight_grad_kernel(sides, added, pieces, rank_ref, left_ref, *refs):
    rights, refs = refs[:sides], refs[sides:]
    more, refs = refs[:added], refs[added:]
    outs, flip_ref = refs[:-1], refs[-1]
    e, m, n = pl.program_id(0), pl.program_id(1), pl.program_id(2)

    @pl.when(n == 0)
    def _():
        flip_ref[...] = left_ref[0].T

    for side in range(sides):

        @pl.when(n == side)
        def _():
            total = dot_nn(flip_ref[...], rights[side][0])
            if not added and not pieces:
                outs[0][0] = total
            for k in range(side, max(added, len(outs) if pieces else 0), sides):

                @pl.when(e * pl.num_programs(1) + m == k // sides)
                def _():
                    grown = total + more[k][...].astype(f32) if added else total
                    if pieces:
                        outs[k][...] = grown.astype(bf16)
                    else:
                        outs[0][0] = grown


def weight_grad(left, rights, rank, rows, first=0, experts=None, more=(), pieces=False):
    experts = left.shape[0] if experts is None else experts
    slots = left.shape[1]
    tile = min(512, rows)
    per = rows // tile
    width = F
    shares = [(right, j) for right in rights for j in range(right.shape[2] // width)]
    sides = len(shares)
    piece = pl.BlockSpec((tile, width), lambda e, m, n, p: (0, 0))
    if pieces:
        out_specs = [piece] * (experts * per * sides)
        out_shape = [jax.ShapeDtypeStruct((tile, width), bf16)] * (experts * per * sides)
    else:
        out_specs = [pl.BlockSpec((1, tile, width), lambda e, m, n, p: (e, m, n))]
        out_shape = [jax.ShapeDtypeStruct((experts, rows, sides * width), f32)]
    out = pl.pallas_call(
        functools.partial(weight_grad_kernel, sides, len(more), pieces),
        grid_spec=pltpu.PrefetchScalarGridSpec(
            num_scalar_prefetch=1,
            grid=(experts, per, sides),
            in_specs=[
                pl.BlockSpec((1, slots, tile), lambda e, m, n, p: (e + first, 0, p[0] * per + m))
            ]
            + [
                pl.BlockSpec((1, slots, width), lambda e, m, n, p, j=j: (e + first, 0, j))
                for _, j in shares
            ]
            + [piece] * len(more),
            out_specs=out_specs,
            scratch_shapes=[pltpu.VMEM((tile, slots), bf16)],
        ),
        out_shape=out_shape,
        compiler_params=pltpu.CompilerParams(vmem_limit_bytes=48 * 2**20),
        cost_estimate=cost(experts * rows * sides / 560 * (2 if more else 1.7)),
        name="weight_gradient",
    )(rank.reshape(1).astype(jnp.int32), left, *[right for right, _ in shares], *more)
    return out if pieces else out[0]


def weight_grad_sends(left, rights, rows):
    count = lax.axis_size("dp")
    rank = lax.axis_index("dp")
    onward = [(d, (d + 1) % count) for d in range(count)]
    sent, arrived = [], []
    for e in range(left.shape[0]):
        more = []
        for step in range(1, count):
            parts = weight_grad(left, rights, (rank + count - step) % count, rows, e, 1, more, True)
            more = [lax.ppermute(part, "dp", onward) for part in parts]
        sent += parts if more else []
        arrived += more
    return sent, arrived


def unturn(grad, cosine, sine_part):
    return grad * cosine - jnp.roll(grad, HD // 2, axis=1) * sine_part


def unproject_kernel(
    grad_q_ref, grad_k_ref, grad_v_ref, raw_ref, squares_ref, dots_ref, gain_ref, cosine_ref, sine_ref,
    weight_ref, grad_ref, gain_terms_ref, out_ref,
):
    rows, _, width = out_ref.shape
    inverse = lax.rsqrt(squares_ref[...] / D + norm_epsilon)
    inner = inverse * inverse * dots_ref[:2] / D

    @pl.when(pl.program_id(0) == 0)
    def _():
        gain_terms_ref[...] = jnp.zeros_like(gain_terms_ref)

    for j, part_ref in ((0, grad_q_ref), (1, grad_k_ref)):
        grad = unturn(part_ref[...], cosine_ref[...], sine_ref[...])
        column = as_column(inverse[j : j + 1])
        raw = raw_ref[:, j * HD : (j + 1) * HD]
        gain_terms_ref[pl.ds(j, 1), :] += jnp.sum(grad * raw * column, axis=0, keepdims=True)
        back = column * grad * gain_ref[j : j + 1, :] - raw * as_column(inner[j : j + 1])
        grad_ref[:, pl.ds(j * HD, HD)] = back.astype(bf16)
    grad_ref[:, pl.ds(2 * HD, HD)] = grad_v_ref[...].astype(bf16)
    for row in range(rows):
        at = pl.ds(row * width, width)
        out_ref[row] = dot_nn(grad_ref[...], weight_ref[:, at]).astype(bf16)


def unproject(grads, raw, squares, dots, gain_pair, cosine, sine_part, weight_flip, rows, cols):
    length = raw.shape[0]
    block_rows, width = length // cols, D // rows
    tile = block_rows
    tall = pl.BlockSpec((tile, HD), lambda i: (i, 0))
    three = pl.BlockSpec((tile, 3 * HD), lambda i: (i, 0))
    pair = pl.BlockSpec((2, tile), lambda i: (0, i))
    trio = pl.BlockSpec((3, tile), lambda i: (0, i))
    fixed = pl.BlockSpec((2, HD), lambda i: (0, 0))
    return pl.pallas_call(
        unproject_kernel,
        grid=(length // tile,),
        in_specs=[
            tall, tall, tall, three, pair, trio, fixed, tall, tall,
            pl.BlockSpec(weight_flip.shape, lambda i: (0, 0)),
        ],
        out_specs=[
            three, fixed, pl.BlockSpec((rows, tile, width), lambda i: (i, 0, 0)),
        ],
        out_shape=[
            jax.ShapeDtypeStruct((length, 3 * HD), bf16),
            jax.ShapeDtypeStruct((2, HD), f32),
            jax.ShapeDtypeStruct((rows * cols, block_rows, width), bf16),
        ],
        compiler_params=pltpu.CompilerParams(vmem_limit_bytes=52 * 2**20),
        cost_estimate=cost(15.5),
        name="projection_backward",
    )(*grads, raw, squares, dots, gain_pair, cosine, sine_part, weight_flip)


def norm_back(values, inverse, gain_row, upstream, dot_total):
    scaled = upstream * gain_row
    return inverse[:, None] * scaled - values * (inverse**3 * dot_total / D)[:, None]


def dot(a, b):
    return jnp.dot(a, b, preferred_element_type=f32)


def einsum(spec, a, b):
    return jnp.einsum(spec, a, b, preferred_element_type=f32)


def on_device(
    layer_input,
    gains,
    qkv_weight,
    output_weight,
    router_weight,
    expand_weight,
    reduce_weight,
    routes,
    drop_order,
    prefix_len,
    cotangent,
):
    row_rank, col_rank = lax.axis_index("row"), lax.axis_index("col")
    rows, cols = lax.axis_size("row"), lax.axis_size("col")
    dp_count = lax.axis_size("dp")
    group = rows * cols
    res_rows, row_width = layer_input.shape
    col_width = qkv_weight.shape[2]
    seq_len = res_rows * cols
    tok_rows = res_rows // rows
    block_rank = col_rank * rows + row_rank
    expert_rank = row_rank * cols + col_rank
    expert_count = router_weight.shape[1]
    local_experts = expand_weight.shape[0]
    capacity = tok_rows * TOP // expert_count
    ring = Ring(rows, cols)
    gain_rows = gains.astype(f32)
    router_flip = router_weight.T

    paired = dp_count % 2 == 0
    half_rank = lax.axis_index("dp") % 2 if paired else 0
    partner = [(d, d ^ 1) for d in range(dp_count)]
    halves = 2 if paired else 1
    half_rows = row_width // halves
    head_half = lax.dynamic_slice_in_dim(qkv_weight, half_rank * half_rows, half_rows, 0)
    head_half = head_half.reshape(half_rows, 3, rows, HD).transpose(2, 0, 1, 3)
    head_half = exchange_rows(head_half.reshape(rows, half_rows, 3 * HD))
    half_width = HD // 2
    frequency = rope_base ** (-2.0 * jnp.arange(half_width, dtype=f32) / HD)
    angles = jnp.arange(seq_len).astype(f32)[:, None] * frequency[None, :]
    cosine, sine_part = jnp.cos(angles), jnp.sin(angles)
    cosine = jnp.concatenate([cosine, cosine], axis=1)
    sine_part = jnp.concatenate([-sine_part, sine_part], axis=1)
    own_lines = jnp.concatenate([routes.T, drop_order[None, :]], axis=0)
    lines = jnp.zeros((cols,) + own_lines.shape, jnp.int32)
    lines = lax.dynamic_update_slice(lines, own_lines[None], (col_rank, 0, 0))
    for step in range(1, cols):
        arrived = lax.ppermute(own_lines, "col", [(c, (c + step) % cols) for c in range(cols)])
        lines = lax.dynamic_update_slice(
            lines, arrived[None], ((col_rank + cols - step) % cols, 0, 0)
        )
    first_expert = expert_rank * local_experts
    own_experts = first_expert + jnp.arange(local_experts)
    member = jnp.any(lines[None, :, :TOP] == own_experts[:, None, None, None], axis=2)
    member = member.reshape(local_experts, group, tok_rows).transpose(1, 0, 2)
    drop_rank = lines[:, TOP].reshape(group, tok_rows)
    token_index = jnp.arange(tok_rows)
    earlier = (drop_rank[:, None, :] < drop_rank[:, :, None]) | (
        drop_rank[:, None, :] == drop_rank[:, :, None]
    ) & (token_index[None, None, :] < token_index[None, :, None])
    position = jnp.sum(jnp.where(earlier[:, None] & member[:, :, None, :], 1, 0), axis=-1)
    kept = member & (position < capacity)
    hits = kept[:, :, None, :] & (
        position[:, :, None, :] == jnp.arange(capacity)[None, None, :, None]
    )
    hits = hits.reshape(group, local_experts * capacity, tok_rows)
    dispatch = hits.astype(bf16)
    combine = hits.transpose(0, 2, 1).astype(bf16)

    weight_half = lax.dynamic_slice_in_dim(
        output_weight, half_rank * (col_width // 2), col_width // halves, 0
    )
    weight_mine = lax.all_gather(weight_half, BLOCKS, axis=0)
    by_core = weight_mine.reshape(
        ring.groups, ring.cores, rows, weight_half.shape[0], row_width
    )
    if paired:
        own_core = lax.dynamic_index_in_dim(by_core, ring.core, 1, False)
        own_core = own_core.reshape(ring.size, weight_half.shape[0], row_width)
        weight_theirs = ring.from_siblings(lax.ppermute(own_core, "dp", partner))
        weight_sets = [weight_mine] * ring.cores + weight_theirs
    else:
        weight_sets = [weight_mine[:, : col_width // 2]] * ring.cores
        weight_sets += [weight_mine[:, col_width // 2 :]] * ring.cores
    head_out = exchange_rows(output_weight.reshape(rows, col_width // rows, row_width))
    head_out = head_out.transpose(0, 2, 1).reshape(D, HD)
    at = [col_rank, row_rank]
    table = []
    for half in range(2):
        for k in range(ring.cores):
            for chip_group in range(ring.groups):
                col = chip_group * ring.cores + (ring.core + k) % ring.cores
                for row in range(rows):
                    whole_plane = half == 0 or not paired
                    table.append(col * rows + row if whole_plane else chip_group * rows + row)
    for chip_group in range(ring.groups):
        for half in range(2):
            for k in range(ring.cores):
                col = chip_group * ring.cores + (ring.core + k) % ring.cores
                at.append((col * 2 + (half_rank + half) % 2) * (rows // 2))
    at = jnp.stack([jnp.asarray(value, jnp.int32) for value in at])
    table = jnp.stack([jnp.asarray(value, jnp.int32) for value in table])

    x_steps = ring.gather_steps(layer_input)
    x_arrivals = [next(x_steps), next(x_steps)]
    pieces, head_half = together([piece for piece, _ in x_arrivals[-1]], head_half)
    x_arrivals[-1] = list(zip(pieces, [distance for _, distance in x_arrivals[-1]]))
    x_arrivals.append(x_steps.send(pieces))
    if paired:
        other_half = lax.ppermute(head_half, "dp", partner)
        pieces, other_half, head_out = together(
            [piece for piece, _ in x_arrivals[-1]], other_half, head_out
        )
        x_arrivals[-1] = list(zip(pieces, [distance for _, distance in x_arrivals[-1]]))
        head_weight = jnp.where(
            half_rank == 0,
            jnp.stack([head_half, other_half], axis=1),
            jnp.stack([other_half, head_half], axis=1),
        )
    else:
        head_weight = head_half
    x_arrivals += [x_steps.send(pieces), *x_steps]
    head_weight = head_weight.reshape(D, 3 * HD)
    weight_flip = head_weight.T
    x_blocks = unwritten((group,) + layer_input.shape, bf16)
    for arrival in x_arrivals:
        x_blocks = ring.place_blocks(x_blocks, ring.with_siblings(arrival))
    x_blocks, cosine, sine_part, dispatch, combine = together(
        x_blocks, cosine, sine_part, dispatch, combine
    )
    projected, inv_first, square_terms = project(x_blocks, gain_rows[0:1], head_weight, rows)
    squares = ring.small_sum(square_terms)

    head_first = block_rank * HD
    gain_pair = lax.dynamic_slice(gain_rows, (1, head_first), (2, HD))
    query_low, key_low, value_low, key_flip, value_flip = turn(
        projected, squares, gain_pair, cosine, sine_part
    )

    upstream_blocks = lax.all_gather(after(cotangent, x_blocks), BLOCKS, axis=0)
    query_rows = max(seq_len // 6, 128)
    attn_head, lse = attention(query_low, key_low, value_flip, prefix_len, query_rows)
    attn_tokens = exchange(attn_head.reshape(group, tok_rows, HD), BLOCKS)
    upstream_slots = dispatch_blocks(dispatch, upstream_blocks, rows, local_experts)
    residual, second_low = output_branch(
        at, table, attn_tokens, weight_sets, x_blocks, gain_rows[3:4], rows, ring.groups
    )
    feat_steps = ring.gather_steps(second_low)
    arrivals = [next(feat_steps), next(feat_steps)]
    grad_raw = einsum(
        "end,efd->enf", upstream_slots.reshape(local_experts, group * capacity, D), reduce_weight
    ).reshape(local_experts, group, capacity, F)
    pieces, upstream_slots = together([piece for piece, _ in arrivals[-1]], upstream_slots)
    arrivals[-1] = list(zip(pieces, [distance for _, distance in arrivals[-1]]))
    arrivals.append(feat_steps.send(pieces))
    pieces, grad_raw = together([piece for piece, _ in arrivals[-1]], grad_raw)
    arrivals[-1] = list(zip(pieces, [distance for _, distance in arrivals[-1]]))
    arrivals.append(feat_steps.send(pieces))

    carried = None
    waiting, feat_parts, places = [], {}, {}
    calls = {1: 0, ring.size // 2 - 2: 3, ring.size // 2: 1}
    start = {0: 0, 3: group - 2 * ring.cores, 1: 3 * ring.cores}
    for step in range(ring.size // 2 + 1):
        if step == len(arrivals):
            pieces, *carried = together([piece for piece, _ in arrivals[-1]], *carried)
            arrivals.append(feat_steps.send(pieces))
        arrival = arrivals[step]
        pairs = ring.with_siblings(arrival)
        for k, (_, distance) in enumerate(arrival):
            waiting.append((distance, pairs[k * ring.cores : (k + 1) * ring.cores]))
        if step not in calls:
            continue
        taken = [pair for _, chip in waiting for pair in chip]
        carried, feat_sums = run_experts(
            [block for block, _ in taken],
            [ident for _, ident in taken],
            first_expert,
            grad_raw,
            dispatch,
            combine,
            router_flip,
            expand_weight,
            carried,
            calls[step],
        )
        for k, (distance, chip) in enumerate(waiting):
            feat_parts[distance] = ring.chip_sum(*feat_sums[k * ring.cores : (k + 1) * ring.cores])
            for j, (_, ident) in enumerate(chip):
                places[start[calls[step]] + k * ring.cores + j] = (distance, ident)
        waiting.clear()
    slot_rows, hidden, grad_gate_pre, grad_up_pre, slot_gate = carried

    far = ring.size // 2
    feat_parts[far], slot_rows = together(feat_parts[far], slot_rows)
    grad_steps = ring.scatter_steps(lambda distance: feat_parts[distance])
    grad_terms = next(grad_steps)
    expand_sides = [grad_gate_pre, grad_up_pre]
    expand_sent, expand_arrived = weight_grad_sends(slot_rows, expand_sides, D // dp_count)
    grad_terms, expand_sent, hidden = together(grad_terms, expand_sent, hidden)
    grad_terms = grad_steps.send(grad_terms)
    expert_out = einsum("enf,efd->end", hidden, reduce_weight).astype(bf16)
    arriving, arrived = list(expand_arrived), []

    def taking(count, *values):
        taken, arriving[:count] = arriving[:count], []
        *values, taken = together(*values, taken)
        arrived.extend(taken)
        return values

    grad_terms, expert_out = taking(1, grad_terms, expert_out)
    grad_terms = grad_steps.send(grad_terms)
    ids = jnp.stack([places[k][1] for k in range(group)]).astype(jnp.int32)
    gate_tokens, grad_out_slots, moe_sums = combine_experts(
        ids, expert_out, upstream_slots, dispatch, combine, slot_gate
    )
    grad_out_slots = grad_out_slots.reshape(local_experts, group * capacity, D)
    grad_probs = exchange(gate_tokens, BLOCKS)
    grad_terms, grad_out_slots, moe_sums = taking(1, grad_terms, grad_out_slots, moe_sums)
    grad_terms = grad_steps.send(grad_terms)
    reduce_sent, reduce_arrived = weight_grad_sends(hidden, [grad_out_slots], F // dp_count)
    arriving += reduce_arrived
    grad_probs = grad_probs.reshape(cols, rows, local_experts, tok_rows)
    grad_probs = grad_probs.transpose(1, 0, 2, 3).reshape(expert_count, tok_rows)
    logits = dot_nt(router_flip, second_low)
    probs = jax.nn.softmax(logits, axis=0)
    grad_logits = probs * (grad_probs - jnp.sum(probs * grad_probs, axis=0, keepdims=True))
    grad_logits = grad_logits.T.astype(bf16)
    router_term = einsum("te,td->ed", grad_logits, second_low)
    while len(grad_terms) == 2:
        grad_terms = grad_steps.send(grad_terms)

    grad_branch, gain_second_term = residual_back(
        at[:2], grad_terms, grad_logits, router_flip, residual, upstream_blocks, gain_rows[3:4], rows
    )
    grad_branch, reduce_sent, router_term = taking(1, grad_branch, reduce_sent, router_term)
    branch_steps = ring.gather_steps(grad_branch)
    branch_arrivals = [next(branch_steps)]
    router_total = lax.psum(router_term, ("dp", "row", "col"))
    pieces = None
    for arrival in iter(lambda: branch_steps.send(pieces), None):
        pieces, = taking(1, [piece for piece, _ in arrival])
        branch_arrivals.append(list(zip(pieces, [distance for _, distance in arrival])))
        if len(branch_arrivals) == ring.size // 2 + 1:
            break
    branch_all = unwritten((group, tok_rows, D), bf16)
    for arrival in branch_arrivals:
        branch_all = ring.place_blocks(branch_all, ring.with_siblings(arrival))

    moe_tokens = lax.psum_scatter(
        after(moe_sums, branch_all), BLOCKS, scatter_dimension=0, tiled=False
    )
    grad_attn = dot(branch_all.reshape(seq_len, D), head_out).astype(bf16)
    centre = jnp.sum(attn_head.astype(f32) * grad_attn.astype(f32), axis=1)[None]
    *head_grads, dot_query, dot_key, dot_value = attention_back(
        query_low, key_low, key_flip, value_low, grad_attn, lse, centre, prefix_len, query_rows
    )
    dots = jnp.concatenate([dot_query, dot_key, dot_value], axis=0)
    dots, = taking(1, dots)
    dots = ring.small_sum(dots)

    grad_qkv, gain_pair_terms, grad_first_blocks = unproject(
        head_grads, projected, squares, dots, gain_pair, cosine, sine_part, weight_flip, rows, cols
    )
    grad_first_blocks, = taking(2, grad_first_blocks)

    def blocks_sum(blocks, distance):
        return ring.chip_sum(
            *[lax.dynamic_index_in_dim(blocks, ident, 0, False) for ident in ring.block_ids(distance)]
        )

    first_far = blocks_sum(grad_first_blocks, ring.size // 2)
    first_far, grad_first_blocks = together(first_far, grad_first_blocks)

    def first_part(distance):
        return first_far if distance == ring.size // 2 else blocks_sum(grad_first_blocks, distance)

    first_steps = ring.scatter_steps(first_part)
    grad_first = next(first_steps)
    grad_first, grad_qkv = together(grad_first, grad_qkv)
    grad_first = first_steps.send(grad_first)
    qkv_term = project_weight(x_blocks, gain_rows[0:1], inv_first, grad_qkv, rows)
    grad_first, qkv_term = taking(1, grad_first, qkv_term)
    grad_first = first_steps.send(grad_first)
    rank = lax.axis_index("dp")
    expand_grad = weight_grad(
        slot_rows, expand_sides, rank, D // dp_count, more=arrived[: len(expand_arrived)]
    )
    layer_tokens = (residual + moe_tokens.astype(f32)).astype(bf16)
    layer_output = lax.all_to_all(layer_tokens, "row", split_axis=1, concat_axis=0, tiled=True)
    grad_first, expand_grad, layer_output = taking(
        len(arriving), grad_first, expand_grad, layer_output
    )
    grad_first = first_steps.send(grad_first)
    output_term = dot(attn_head.T, branch_all.reshape(seq_len, D))
    output_term = output_term.astype(bf16).reshape(HD, rows, row_width).transpose(1, 0, 2)
    output_sum = exchange_rows(output_term).reshape(col_width, row_width)
    reduce_grad = weight_grad(
        hidden, [grad_out_slots], rank, F // dp_count, more=arrived[len(expand_arrived) :]
    )
    grad_first, output_sum, reduce_grad = together(grad_first, output_sum, reduce_grad)
    grad_first = first_steps.send(grad_first)
    grad_first = sum(term.astype(f32) for term in grad_first)
    grad_block = lax.dynamic_slice(
        branch_all, (col_rank * rows, 0, row_rank * row_width), (rows, tok_rows, row_width)
    ).reshape(res_rows, row_width)
    inverse = lax.rsqrt(squares / D + norm_epsilon)
    dot_first = dots[2] + norm_epsilon * jnp.sum(dots[:2] * inverse, axis=0)
    dot_first = dot_first / inv_first[0]
    own_first = col_rank * res_rows
    dot_first = lax.dynamic_slice_in_dim(dot_first, own_first, res_rows)
    inv_block = lax.dynamic_slice_in_dim(inv_first[0], own_first, res_rows)
    gain_block = lax.dynamic_slice_in_dim(gain_rows[0], row_rank * row_width, row_width)
    input_grad = grad_block.astype(f32) + norm_back(
        layer_input.astype(f32), inv_block, gain_block, grad_first, dot_first
    )

    output_rows = col_width // dp_count
    output_grad = dp_sum(
        lambda rank: lax.dynamic_slice_in_dim(
            output_sum, rank * output_rows, output_rows, 0
        ).astype(f32)
    )
    gain_first_term = jnp.sum(qkv_term * head_weight.astype(f32), axis=1) / gain_rows[0]
    qkv_rows = row_width // dp_count
    qkv_shaped = qkv_term.reshape(rows, row_width, 3 * HD)
    qkv_sum = dp_sum(
        lambda rank: lax.dynamic_slice_in_dim(qkv_shaped, rank * qkv_rows, qkv_rows, 1)
    )
    qkv_grad = exchange_rows(qkv_sum.astype(bf16)).reshape(rows, qkv_rows, 3, HD)
    qkv_grad = qkv_grad.transpose(1, 2, 0, 3).reshape(1, qkv_rows, 3, col_width).astype(f32)

    def placed(term):
        return lax.dynamic_update_slice(jnp.zeros((D,), f32), term, (head_first,))

    gain_total = dp_all_sum(
        ring.small_sum(
            jnp.concatenate(
                [
                    jnp.stack(
                        [gain_first_term, placed(gain_pair_terms[0]), placed(gain_pair_terms[1])]
                    ),
                    gain_second_term,
                ],
                axis=0,
            )
        )
    )
    router_total = router_total.T
    return (
        layer_output,
        input_grad.astype(bf16),
        gain_total,
        qkv_grad,
        output_grad[None],
        router_total,
        expand_grad,
        reduce_grad,
    )


def solution(mesh):
    return jax.shard_map(
        on_device,
        mesh=mesh,
        in_specs=(
            P(("dp", "col"), "row"),
            P(),
            P("row", None, "col"),
            P("col", "row"),
            P(),
            P(("row", "col"), None, None),
            P(("row", "col"), None, None),
            P(("dp", "col"), None),
            P(("dp", "col")),
            P("dp"),
            P(("dp", "col"), "row"),
        ),
        out_specs=(
            P(("dp", "col"), "row"),
            P(("dp", "col"), "row"),
            P(),
            P("row", "dp", None, "col"),
            P("col", "dp", "row"),
            P(),
            P(("row", "col"), "dp", None),
            P(("row", "col"), "dp", None),
        ),
        check_vma=False,
    )
```

time: 1440 us -> 927 us (0.64)
  waiting for transfers between devices: 539 us -> 300 us
  Pallas kernels: 34.7 us -> 261 us
  local copies, waits for them, and re-layouts: 328 us -> 112 us
  matrix products: 210 us -> 42.6 us
  blocking collectives: 78.9 us -> 0 us
  other arithmetic: 102 us -> 48 us
  starting transfers between devices: 119 us -> 135 us
    pallas_call x0 -> x23, Pallas kernels: none -> 219 us  [the longest x3 72.1 us: run_experts(): pl.pallas_call(functools.partial(experts_kernel, count, first), grid_spec...]
    ppermute x4 -> x2, waiting for transfers between devices: 179 us -> 1.9 us  [dp_sum(): arrived = lax.ppermute(total.astype(bf16), 'dp', onward)]
    dot_general x17 -> x3, matrix products: 191 us -> 25.8 us  [einsum(): return jnp.einsum(spec, a, b, preferred_element_type=f32)]
    dynamic_update_slice x31 -> x49, local copies, waits for them, and re-layouts: 156 us -> 50.2 us  [the longest x32 39.8 us: place_blocks(): box = lax.dynamic_update_slice(box, piece[None], start)]
    ppermute x92 -> x123, waiting for transfers between devices: 329 us -> 258 us  [the longest x12 83.8 us: weight_grad_sends(): more = [lax.ppermute(part, 'dp', onward) for part in parts]]
    reshape x10 -> x6, local copies, waits for them, and re-layouts: 46.3 us -> 2.49 us  [the longest x1 2.25 us: on_device(): output_term.astype(bf16).reshape(HD, rows, row_width).transpose(1, 0, 2)]
    psum x1 -> x0, blocking collectives: 39.6 us -> none  [on_device(): lax.psum((gain_terms, router_term), ('dp', 'row', 'col'))]
    ppermute x92 -> x123, starting transfers between devices: 87.5 us -> 120 us  [the longest x12 35.7 us: exchange_rows(): lax.ppermute(sent, 'row', [(r, (r + step) % rows) for r in range(rows)])]
  transfers between devices with their start and end apart: 106 -> 132, of which waited for: 43 -> 58; matrix products, arithmetic and copies ran while one was open for 34% -> 20% of each run, Pallas kernels for 2% -> 26%
where the time goes in v2:
time: 927 us; the launch traced here: 915 us
  waiting for transfers between devices  300 us (32%)
  Pallas kernels  261 us (28%)
  starting transfers between devices  135 us (15%)
  local copies, waits for them, and re-layouts  112 us (12%)
  other arithmetic  48 us (5%)
  matrix products  42.6 us (5%)
  between operations  16.9 us (2%)
    ppermute x12, waiting for transfers between devices, weight_grad_sends(): more = [lax.ppermute(part, 'dp', onward) for part in parts]  83.8 us
    pallas_call x3, Pallas kernels, run_experts(): pl.pallas_call(functools.partial(experts_kernel, count, first), grid_spec...  72.1 us
    pallas_call x6, Pallas kernels, weight_grad(): pl.pallas_call(functools.partial(weight_grad_kernel, sides, len(more), pi...  56.2 us
    dynamic_update_slice x32, local copies, waits for them, and re-layouts, place_blocks(): box = lax.dynamic_update_slice(box, piece[None], start)  39.8 us
    ppermute x12, waiting for transfers between devices, exchange_rows(): lax.ppermute(sent, 'row', [(r, (r + step) % rows) for r in range(rows)])  37 us
    ppermute x12, starting transfers between devices, exchange_rows(): lax.ppermute(sent, 'row', [(r, (r + step) % rows) for r in range(rows)])  35.7 us
    all_to_all x2, waiting for transfers between devices, exchange(): return lax.all_to_all(pieces, axes, split_axis=0, concat_axis=0, tiled=True)  34.1 us
    unnamed x197, local copies, waits for them, and re-layouts  28.7 us
  transfers between devices with their start and end apart: 132, of which 58 were waited for; matrix products, arithmetic and copies ran while one was open for 20% of the time, Pallas kernels for 26%

profile of v2, /device:TPU:0, one launch (start us, length us, event | category | flops | bytes accessed | tf_op | source)
XLA Modules:
  0.0 915.5 jit_solution(7820411521468684861)
XLA Ops:
  113.0 10.7 %collective-permute-done.16 = bf16[768,512]{1,0:T(8,128)(2,1)S(1)} collective-permute-done((bf16[768,512]{1,0:T(8,128)(2,1)}, bf16[768,512]{1,0:T(8,128)(2,1)S(1)}, u32[]{:S(2)}, u32[]{:S(2)}) %collective-permute-start.16) | collective-permute-done | bytes 786464 | tf_op jit(solution)/shard_map/ppermute | solution.py:279
  146.4 13.6 %norm_and_project.1 = (f32[3072,384]{1,0:T(8,128)}, f32[1,3072]{1,0:T(1,128)S(1)}, f32[2,3072]{1,0:T(2,128)S(1)}) custom-call(bf16[16,768,512]{2,1,0:T(8,128)(2,1)} %bitcast_dynamic-update-slice_fusion.16.x_ref.refs_1_, f32[1,2048]{1,0:T(1,128)S(1)} %get-tuple-element.368.gain_ref, bf16[2048,384]{1,0:T(8,128)(2,1)S(1)} %bitcast.268), custom_call_target="tpu_custom_call" | custom-call | flops 15399999488 | tf_op jit(solution)/shard_map/norm_and_project/pallas_call | solution.py:444
  183.9 9.6 %collective-permute-done.30.refs_5_.refs_9_ = bf16[8,256,512]{2,1,0:T(8,128)(2,1)} collective-permute-done((bf16[8,256,512]{2,1,0:T(8,128)(2,1)}, bf16[8,256,512]{2,1,0:T(8,128)(2,1)}, u32[]{:S(2)}, u32[]{:S(2)}) %collective-permute-start.30) | collective-permute-done | bytes 2097184 | tf_op jit(solution)/shard_map/ppermute | solution.py:1091
  196.9 17.2 %attention_forward.1 = (bf16[3072,128]{1,0:T(8,128)(2,1)}, f32[1,3072]{1,0:T(1,128)S(1)}) custom-call(s32[1]{0:T(128)S(6)} %copy.301.prefix_ref, bf16[3072,128]{1,0:T(8,128)(2,1)S(1)} %copy-done.39, bf16[3072,128]{1,0:T(8,128)(2,1)S(1)} %copy-done.41, bf16[128,3072]{1,0:T(8,128)(2,1)S(1)} %copy-done.45), custom_call_target="tpu_custom_call" | custom-call | flops 18699999232 | tf_op jit(solution)/shard_map/attention_forward/pallas_call | solution.py:102
  220.6 34.1 %all-to-all-done.refs_0_ = bf16[16,192,128]{2,1,0:T(8,128)(2,1)S(1)} async-done(((bf16[16,192,128]{2,1,0:T(8,128)(2,1)}), bf16[16,192,128]{2,1,0:T(8,128)(2,1)S(1)}, u32[]{:S(2)}, u32[]{:S(2)}) %all-to-all-start) | async-done | bytes 786464 | tf_op jit(solution)/shard_map/all_to_all | solution.py:417
  264.7 14.3 %cotangent_to_slots.1.up_ref = bf16[2,16,48,2048]{3,2,1,0:T(8,128)(2,1)} custom-call(bf16[16,96,192]{2,1,0:T(8,128)(2,1)} %copy.184.hits_ref.refs_12_.refs_8_, bf16[16,768,512]{2,1,0:T(8,128)(2,1)} %bitcast.286), custom_call_target="tpu_custom_call" | custom-call | flops 15399999488 | tf_op jit(solution)/shard_map/cotangent_to_slots/pallas_call | solution.py:667
  285.3 12.9 %fusion.25 = f32[2,768,1024]{2,1,0:T(8,128)} fusion(bf16[2,768,2048]{2,1,0:T(8,128)(2,1)} %bitcast.312, bf16[2,1024,2048]{2,1,0:T(8,128)(2,1)} %param.17), kind=kOutput, calls=%fused_computation.190 | convolution fusion | flops 6442450944 | bytes 20971520 | tf_op jit(solution)/shard_map/end,efd->enf/dot_general | solution.py:1008
  307.1 25.6 %experts.3 = (bf16[2,768,2048]{2,1,0:T(8,128)(2,1)}, bf16[2,768,1024]{2,1,0:T(8,128)(2,1)}, bf16[2,768,1024]{2,1,0:T(8,128)(2,1)}, bf16[2,768,1024]{2,1,0:T(8,12...) custom-call(s32[7]{0:T(128)} %stack.200.ids_ref, ...), custom_call_target="tpu_custom_call" | custom-call | flops 27499999232 | tf_op jit(solution)/shard_map/experts/pallas_call | solution.py:780
  333.9 21.0 %experts.4 = (bf16[2,768,2048]{2,1,0:T(8,128)(2,1)}, bf16[2,768,1024]{2,1,0:T(8,128)(2,1)}, bf16[2,768,1024]{2,1,0:T(8,128)(2,1)}, bf16[2,768,1024]{2,1,0:T(8,12...) custom-call(s32[5]{0:T(128)} %stack.231.ids_ref, ...), custom_call_target="tpu_custom_call", output_to_operand_aliasing={{0}: (14, {}), {1}: (15, {}), {2}: (16, {}), {3}: (17, {}),... | custom-call | flops 23100000256 | tf_op jit(solution)/shard_map/experts/pallas_call | solution.py:780
  373.4 25.5 %experts.5 = (bf16[2,768,2048]{2,1,0:T(8,128)(2,1)}, bf16[2,768,1024]{2,1,0:T(8,128)(2,1)}, bf16[2,768,1024]{2,1,0:T(8,128)(2,1)}, bf16[2,768,1024]{2,1,0:T(8,12...) custom-call(s32[7]{0:T(128)} %stack.238.ids_ref, ...), custom_call_target="tpu_custom_call", output_to_operand_aliasing={{0}: (18, {}), {1}: (19, {}), {2}: (20, {}), {3}: (21, {}),... | custom-call | flops 27499999232 | tf_op jit(solution)/shard_map/experts/pallas_call | solution.py:780
  428.0 11.9 %convolution_convert_fusion = bf16[2,768,2048]{2,1,0:T(8,128)(2,1)} fusion(bf16[2,768,1024]{2,1,0:T(8,128)(2,1)S(1)} %copy-done.6, bf16[2,1024,2048]{2,1,0:T(8,128)(2,1)} %param.17), kind=kOutput, calls=%fused_computation.1 | convolution fusion | flops 6445596672 | bytes 17825792 | tf_op jit(solution)/shard_map/enf,efd->end/dot_general | solution.py:1008
  446.0 17.1 %experts_combine.1 = (f32[16,2,192]{2,1,0:T(2,128)}, bf16[2,16,48,2048]{3,2,1,0:T(8,128)(2,1)S(1)}, bf16[16,192,2048]{2,1,0:T(8,128)(2,1)}) custom-call(s32[16]{0:T(128)S(1)} %stack.239.ids_ref, bf16[2,16,48,2048]{3,2,1,0:T(8,128)(2,1)} %bitcast.329, bf16[2,16,48,2048]{3,2,1,0:T(8,128)(2,1)} %cotangent_to_slots.1.up_ref, ...), custom_call_target="tpu_custom_call" | custom-call | flops 19800000512 | tf_op jit(solution)/shard_map/experts_combine/pallas_call | solution.py:825
  480.4 14.7 %collective-permute-done.62.refs_3_ = bf16[512,1024]{1,0:T(8,128)(2,1)S(1)} collective-permute-done((bf16[512,1024]{1,0:T(8,128)(2,1)}, bf16[512,1024]{1,0:T(8,128)(2,1)S(1)}, u32[]{:S(2)}, u32[]{:S(2)}) %collective-permute-start.62) | collective-permute-done | bytes 1048608 | tf_op jit(solution)/shard_map/ppermute | solution.py:933
  528.3 16.6 %collective-permute-done.70.refs_5_ = bf16[512,1024]{1,0:T(8,128)(2,1)} collective-permute-done((bf16[512,1024]{1,0:T(8,128)(2,1)}, bf16[512,1024]{1,0:T(8,128)(2,1)}, u32[]{:S(2)}, u32[]{:S(2)}) %collective-permute-start.70) | collective-permute-done | bytes 1048608 | tf_op jit(solution)/shard_map/ppermute | solution.py:933
  550.7 16.6 %collective-permute-done.75.refs_6_ = bf16[512,1024]{1,0:T(8,128)(2,1)S(1)} collective-permute-done((bf16[512,1024]{1,0:T(8,128)(2,1)}, bf16[512,1024]{1,0:T(8,128)(2,1)S(1)}, u32[]{:S(2)}, u32[]{:S(2)}) %collective-permute-start.75) | collective-permute-done | bytes 1048608 | tf_op jit(solution)/shard_map/ppermute | solution.py:933
  575.2 14.6 %collective-permute-done.80.refs_7_ = bf16[512,1024]{1,0:T(8,128)(2,1)S(1)} collective-permute-done((bf16[512,1024]{1,0:T(8,128)(2,1)S(1)}, bf16[512,1024]{1,0:T(8,128)(2,1)S(1)}, u32[]{:S(2)}, u32[]{:S(2)}) %collective-permute-start.80) | collective-permute-done | bytes 1048608 | tf_op jit(solution)/shard_map/ppermute | solution.py:933
  625.9 24.1 %attention_backward.1 = (f32[3072,128]{1,0:T(8,128)S(1)}, f32[3072,128]{1,0:T(8,128)S(1)}, f32[3072,128]{1,0:T(8,128)S(1)}, f32[1,3072]{1,0:T(1,128)S(1)}, f32[1,3072]{1,0:T(1,128)S(1)}, /*index=5*/f32[1,3072]{1,0:T(1,128)S(1)}) custom-call(s32[1]{0:T(128)S(6)} %copy.301.prefix_ref, bf16[3072,128]{1,0:T(8,128)(2,1)S(1)} %copy-done.40, ...), custom_call_target="tpu_custom_call" | custom-call | flops 26400000000 | tf_op jit(solution)/shard_map/attention_backward/pallas_call | solution.py:187
  678.2 15.7 %projection_backward.1 = (bf16[3072,384]{1,0:T(8,128)(2,1)}, f32[2,128]{1,0:T(2,128)S(1)}, bf16[16,768,512]{2,1,0:T(8,128)(2,1)}) custom-call(f32[3072,128]{1,0:T(8,128)S(1)} %get-tuple-element.258.grad_q_ref, f32[3072,128]{1,0:T(8,128)} %copy-done.47, f32[3072,128]{1,0:T(8,128)} %copy-done.48, f32[3072,384]{1,0:T(8,128)} %get-tuple-element.162.raw_ref, ...), custom_call_target="tpu_custom_call" | custom-call | flops 17050000384 | tf_op jit(solution)/shard_map/projection_backward/pallas_call | solution.py:977
  693.9 17.0 %collective-permute-done.93.refs_3_ = bf16[512,1024]{1,0:T(8,128)(2,1)} collective-permute-done((bf16[512,1024]{1,0:T(8,128)(2,1)}, bf16[512,1024]{1,0:T(8,128)(2,1)}, u32[]{:S(2)}, u32[]{:S(2)}) %collective-permute-start.93) | collective-permute-done | bytes 1048608 | tf_op jit(solution)/shard_map/ppermute | solution.py:933
  712.3 18.9 %weight_gradient.10 = f32[2,1024,2048]{2,1,0:T(8,128)} custom-call(s32[1]{0:T(128)} %bitcast.122.rank_ref, bf16[2,768,2048]{2,1,0:T(8,128)(2,1)} %get-tuple-element.208.left_ref, bf16[2,768,1024]{2,1,0:T(8,128)(2,1)} %get-tuple-element.209.refs_0_, bf16[2,768,1024]{2,1,0:T(8,128)(2,1)} %get-tuple-element.210.refs_1_, bf16[512,1024]{1,0:T(8,128)(2,1)S(1)} %copy-done.25, ...), custom_call_target="tpu_custom_call" | custom-call | flops 16091428864 | tf_op jit(solution)/shard_map/weight_gradient/pallas_call | solution.py:900
  741.7 15.1 %collective-permute-done.97 = bf16[384,512]{1,0:T(8,128)(2,1)S(1)} collective-permute-done((bf16[384,512]{1,0:T(8,128)(2,1)S(1)}, bf16[384,512]{1,0:T(8,128)(2,1)S(1)}, u32[]{:S(2)}, u32[]{:S(2)}) %collective-permute-start.97) | collective-permute-done | bytes 393248 | tf_op jit(solution)/shard_map/ppermute | solution.py:320
  765.8 14.7 %projection_weight_gradient.1 = f32[2048,384]{1,0:T(8,128)S(1)} custom-call(bf16[16,768,512]{2,1,0:T(8,128)(2,1)} %bitcast_dynamic-update-slice_fusion.16.x_ref.refs_1_, f32[1,2048]{1,0:T(1,128)S(1)} %copy-done.22, f32[1,3072]{1,0:T(1,128)S(1)} %get-tuple-element.272.inverse_ref, bf16[3072,384]{1,0:T(8,128)(2,1)S(1)} %copy-done.46), custom_call_target="tpu_custom_call" | custom-call | flops 16499999744 | tf_op jit(solution)/shard_map/projection_weight_gradient/pallas_call | solution.py:490
  825.3 13.1 %collective-permute-done.121 = bf16[1,256,384]{2,1,0:T(8,128)(2,1)S(1)} collective-permute-done((bf16[1,256,384]{2,1,0:T(8,128)(2,1)S(1)}, bf16[1,256,384]{2,1,0:T(8,128)(2,1)S(1)}, u32[]{:S(2)}, u32[]{:S(2)}) %collective-permute-start.121) | collective-permute-done | bytes 196640 | tf_op jit(solution)/shard_map/ppermute | solution.py:411
  879.7 12.4 %weight_gradient.11 = f32[2,512,2048]{2,1,0:T(8,128)} custom-call(s32[1]{0:T(128)} %bitcast.122.rank_ref, bf16[2,768,1024]{2,1,0:T(8,128)(2,1)} %get-tuple-element.224.left_ref, bf16[2,768,2048]{2,1,0:T(8,128)(2,1)} %bitcast.261, bf16[2,768,2048]{2,1,0:T(8,128)(2,1)} %bitcast.262, bf16[512,1024]{1,0:T(8,128)(2,1)} %collective-permute-done.92.refs_2_, ...), custom_call_target="tpu_custom_call" | custom-call | flops 8045714432 | tf_op jit(solution)/shard_map/weight_gradient/pallas_call | solution.py:900
  (651 shorter events, 491.5 us)
Async XLA Ops:
  7.2 134.4 %all-gather.5.cloned.1.call-start = ((), (), s32[]{:S(2)}) async-start(), calls=%async_computation.6 | async-start | bytes 4456448 | tf_op jit(solution)/shard_map/all_gather | solution.py:1084
  7.2 75.5 %collective-permute-start = (bf16[768,512]{1,0:T(8,128)(2,1)}, bf16[768,512]{1,0:T(8,128)(2,1)}, u32[]{:S(2)}, u32[]{:S(2)}) collective-permute-start(bf16[768,512]{1,0:T(8,128)(2,1)} %param.11), channel_id=1, source_target_pairs={{0,1},{1,0},{2,3},{3,2},{4,5},{5,4},{6,7},{7,6},{8,9},{9,8},{10,11... | collective-permute-start | bytes 2359304 | tf_op jit(solution)/shard_map/ppermute | solution.py:273
  7.7 54.5 %collective-permute-start.1 = (bf16[768,512]{1,0:T(8,128)(2,1)}, bf16[768,512]{1,0:T(8,128)(2,1)}, u32[]{:S(2)}, u32[]{:S(2)}) collective-permute-start(bf16[768,512]{1,0:T(8,128)(2,1)} %param.11), channel_id=1, source_target_pairs={{0,4},{1,5},{4,8},{5,9},{8,12},{9,13},{12,14},{13,15},{14,10},{15,... | collective-permute-start | bytes 2359304 | tf_op jit(solution)/shard_map/ppermute | solution.py:279
  10.4 56.8 %collective-permute-start.2 = (bf16[768,512]{1,0:T(8,128)(2,1)}, bf16[768,512]{1,0:T(8,128)(2,1)}, u32[]{:S(2)}, u32[]{:S(2)}) collective-permute-start(bf16[768,512]{1,0:T(8,128)(2,1)} %param.11), channel_id=1, source_target_pairs={{0,2},{1,3},{4,0},{5,1},{8,4},{9,5},{12,8},{13,9},{14,12},{15,13},... | collective-permute-start | bytes 2359304 | tf_op jit(solution)/shard_map/ppermute | solution.py:280
  15.6 249.1 %all-gather.7.cloned.1.call-start = ((), (), s32[]{:S(2)}) async-start(), calls=%async_computation.7 | async-start | bytes 13369344 | tf_op jit(solution)/shard_map/all_gather | solution.py:1151
  145.2 48.3 %collective-permute-start.30 = (bf16[8,256,512]{2,1,0:T(8,128)(2,1)}, bf16[8,256,512]{2,1,0:T(8,128)(2,1)}, u32[]{:S(2)}, u32[]{:S(2)}) collective-permute-start(bf16[8,256,512]{2,1,0:T(8,128)(2,1)} %bitcast.70), channel_id=1, source_target_pairs={{0,16},{16,0},{1,17},{17,1},{2,18},{18,2},{3,19},{19,3},{4,20},{20... | collective-permute-start | bytes 6291464 | tf_op jit(solution)/shard_map/ppermute | solution.py:1091
  193.5 61.2 %collective-permute-start.31 = (bf16[8,256,512]{2,1,0:T(8,128)(2,1)}, bf16[8,256,512]{2,1,0:T(8,128)(2,1)}, u32[]{:S(2)}, u32[]{:S(2)}) collective-permute-start(bf16[8,256,512]{2,1,0:T(8,128)(2,1)} %collective-permute-done.30.refs_5_.refs_9_), channel_id=1, source_target_pairs={{0,1},{1,0},{2,3},{3,2},{4,5},{5,4},{6,7},{7,6},{8,9},{9,8},{10,11... | collective-permute-start | bytes 6291464 | tf_op jit(solution)/shard_map/ppermute | solution.py:273
  303.5 51.3 %collective-permute-start.44 = (bf16[192,2048]{1,0:T(8,128)(2,1)S(1)}, bf16[192,2048]{1,0:T(8,128)(2,1)}, u32[]{:S(2)}, u32[]{:S(2)}) collective-permute-start(bf16[192,2048]{1,0:T(8,128)(2,1)S(1)} %collective-permute-done.37.refs_0_), channel_id=1, source_target_pairs={{0,4},{1,5},{4,8},{5,9},{8,12},{9,13},{12,14},{13,15},{14,10},{15,... | collective-permute-start | bytes 2359304 | tf_op jit(solution)/shard_map/ppermute | solution.py:279
  305.1 49.8 %collective-permute-start.46 = (bf16[192,2048]{1,0:T(8,128)(2,1)S(1)}, bf16[192,2048]{1,0:T(8,128)(2,1)}, u32[]{:S(2)}, u32[]{:S(2)}) collective-permute-start(bf16[192,2048]{1,0:T(8,128)(2,1)S(1)} %collective-permute-done.38.refs_2_), channel_id=1, source_target_pairs={{0,2},{1,3},{4,0},{5,1},{8,4},{9,5},{12,8},{13,9},{14,12},{15,13},... | collective-permute-start | bytes 2359304 | tf_op jit(solution)/shard_map/ppermute | solution.py:280
  400.0 98.2 %collective-permute-start.64 = (bf16[192,2048]{1,0:T(8,128)(2,1)}, bf16[192,2048]{1,0:T(8,128)(2,1)}, u32[]{:S(2)}, u32[]{:S(2)}) collective-permute-start(bf16[192,2048]{1,0:T(8,128)(2,1)} %get-tuple-element.236), channel_id=1, source_target_pairs={{0,1},{1,0},{2,3},{3,2},{4,5},{5,4},{6,7},{7,6},{8,9},{9,8},{10,11... | collective-permute-start | bytes 2359304 | tf_op jit(solution)/shard_map/ppermute | solution.py:311
  400.4 101.5 %collective-permute-start.40 = (bf16[192,2048]{1,0:T(8,128)(2,1)}, bf16[192,2048]{1,0:T(8,128)(2,1)}, u32[]{:S(2)}, u32[]{:S(2)}) collective-permute-start(bf16[192,2048]{1,0:T(8,128)(2,1)} %get-tuple-element.180), channel_id=1, source_target_pairs={{0,1},{1,0},{2,3},{3,2},{4,5},{5,4},{6,7},{7,6},{8,9},{9,8},{10,11... | collective-permute-start | bytes 2359304 | tf_op jit(solution)/shard_map/ppermute | solution.py:311
  469.3 338.5 %reduce-scatter.2.cloned.1.call-start = ((), (), s32[]{:S(2)}) async-start(), calls=%async_computation.4 | async-start | bytes 13369344 | tf_op jit(solution)/shard_map/reduce_scatter | solution.py:1261
  496.7 48.3 %collective-permute-start.70 = (bf16[512,1024]{1,0:T(8,128)(2,1)}, bf16[512,1024]{1,0:T(8,128)(2,1)}, u32[]{:S(2)}, u32[]{:S(2)}) collective-permute-start(bf16[512,1024]{1,0:T(8,128)(2,1)} %copy-done.35), channel_id=1, source_target_pairs={{0,16},{16,0},{1,17},{17,1},{2,18},{18,2},{3,19},{19,3},{4,20},{20... | collective-permute-start | bytes 3145736 | tf_op jit(solution)/shard_map/ppermute | solution.py:933
  526.8 40.6 %collective-permute-start.75 = (bf16[512,1024]{1,0:T(8,128)(2,1)}, bf16[512,1024]{1,0:T(8,128)(2,1)S(1)}, u32[]{:S(2)}, u32[]{:S(2)}) collective-permute-start(bf16[512,1024]{1,0:T(8,128)(2,1)} %copy-done.34), channel_id=1, source_target_pairs={{0,16},{16,0},{1,17},{17,1},{2,18},{18,2},{3,19},{19,3},{4,20},{20... | collective-permute-start | bytes 3145736 | tf_op jit(solution)/shard_map/ppermute | solution.py:933
  545.0 44.8 %collective-permute-start.80 = (bf16[512,1024]{1,0:T(8,128)(2,1)S(1)}, bf16[512,1024]{1,0:T(8,128)(2,1)S(1)}, u32[]{:S(2)}, u32[]{:S(2)}) collective-permute-start(bf16[512,1024]{1,0:T(8,128)(2,1)S(1)} %copy-done.33), channel_id=1, source_target_pairs={{0,16},{16,0},{1,17},{17,1},{2,18},{18,2},{3,19},{19,3},{4,20},{20... | collective-permute-start | bytes 3145736 | tf_op jit(solution)/shard_map/ppermute | solution.py:933
  567.3 43.7 %collective-permute-start.85 = (bf16[512,1024]{1,0:T(8,128)(2,1)S(1)}, bf16[512,1024]{1,0:T(8,128)(2,1)S(1)}, u32[]{:S(2)}, u32[]{:S(2)}) collective-permute-start(bf16[512,1024]{1,0:T(8,128)(2,1)S(1)} %copy-done.31), channel_id=1, source_target_pairs={{0,16},{16,0},{1,17},{17,1},{2,18},{18,2},{3,19},{19,3},{4,20},{20... | collective-permute-start | bytes 3145736 | tf_op jit(solution)/shard_map/ppermute | solution.py:933
  615.9 290.1 %all-reduce.2.cloned.1.call-start = ((), (), s32[]{:S(2)}) async-start(), calls=%async_computation.5 | async-start | bytes 524288 | tf_op jit(solution)/shard_map/psum | solution.py:1250
  662.9 48.1 %collective-permute-start.93 = (bf16[512,1024]{1,0:T(8,128)(2,1)}, bf16[512,1024]{1,0:T(8,128)(2,1)}, u32[]{:S(2)}, u32[]{:S(2)}) collective-permute-start(bf16[512,1024]{1,0:T(8,128)(2,1)} %get-tuple-element.243), channel_id=1, source_target_pairs={{0,16},{16,0},{1,17},{17,1},{2,18},{18,2},{3,19},{19,3},{4,20},{20... | collective-permute-start | bytes 3145736 | tf_op jit(solution)/shard_map/ppermute | solution.py:933
  664.1 116.4 %collective-permute-start.102 = (bf16[512,1024]{1,0:T(8,128)(2,1)}, bf16[512,1024]{1,0:T(8,128)(2,1)}, u32[]{:S(2)}, u32[]{:S(2)}) collective-permute-start(bf16[512,1024]{1,0:T(8,128)(2,1)} %get-tuple-element.244), channel_id=1, source_target_pairs={{0,16},{16,0},{1,17},{17,1},{2,18},{18,2},{3,19},{19,3},{4,20},{20... | collective-permute-start | bytes 3145736 | tf_op jit(solution)/shard_map/ppermute | solution.py:933
  756.9 99.4 %collective-permute-start.106 = (bf16[512,1024]{1,0:T(8,128)(2,1)}, bf16[512,1024]{1,0:T(8,128)(2,1)}, u32[]{:S(2)}, u32[]{:S(2)}) collective-permute-start(bf16[512,1024]{1,0:T(8,128)(2,1)} %get-tuple-element.245), channel_id=1, source_target_pairs={{0,16},{16,0},{1,17},{17,1},{2,18},{18,2},{3,19},{19,3},{4,20},{20... | collective-permute-start | bytes 3145736 | tf_op jit(solution)/shard_map/ppermute | solution.py:933
  759.0 41.7 %collective-permute-start.112 = (bf16[1,128,512]{2,1,0:T(8,128)(2,1)S(1)}, bf16[1,128,512]{2,1,0:T(8,128)(2,1)S(1)}, u32[]{:S(2)}, u32[]{:S(2)}) collective-permute-start(bf16[1,128,512]{2,1,0:T(8,128)(2,1)S(1)} %bitcast.303), channel_id=1, source_target_pairs={{0,4},{4,8},{8,12},{12,0},{1,5},{5,9},{9,13},{13,1},{2,6},{6,10},{... | collective-permute-start | bytes 393224 | tf_op jit(solution)/shard_map/ppermute | solution.py:411
  810.2 60.0 %all-to-all-start.2 = ((bf16[192,4,512]{2,0,1:T(8,128)(2,1)}), bf16[192,4,512]{2,0,1:T(8,128)(2,1)S(1)}, u32[]{:S(2)}, u32[]{:S(2)}) async-start(bf16[192,4,512]{2,0,1:T(8,128)(2,1)} %bitcast.251), calls=%async_computation.3 | async-start | bytes 1572864 | tf_op jit(solution)/shard_map/all_to_all | solution.py:1301
  824.7 45.5 %collective-permute-start.108 = (bf16[768,512]{1,0:T(8,128)(2,1)S(1)}, bf16[768,512]{1,0:T(8,128)(2,1)}, u32[]{:S(2)}, u32[]{:S(2)}) collective-permute-start(bf16[768,512]{1,0:T(8,128)(2,1)S(1)} %copy-done.63), channel_id=1, source_target_pairs={{0,1},{1,0},{2,3},{3,2},{4,5},{5,4},{6,7},{7,6},{8,9},{9,8},{10,11... | collective-permute-start | bytes 2359304 | tf_op jit(solution)/shard_map/ppermute | solution.py:311
  824.8 45.4 %collective-permute-start.110 = (bf16[768,512]{1,0:T(8,128)(2,1)S(1)}, bf16[768,512]{1,0:T(8,128)(2,1)}, u32[]{:S(2)}, u32[]{:S(2)}) collective-permute-start(bf16[768,512]{1,0:T(8,128)(2,1)S(1)} %copy-done.62), channel_id=1, source_target_pairs={{0,1},{1,0},{2,3},{3,2},{4,5},{5,4},{6,7},{7,6},{8,9},{9,8},{10,11... | collective-permute-start | bytes 2359304 | tf_op jit(solution)/shard_map/ppermute | solution.py:311
  (200 other events, 3386.8 us)
Sparse Core Ops, SparseCore 0:
  15.7 71.9 all-gather.4
  141.1 115.7 all-gather.6
  616.0 140.6 reduce-scatter.1
  762.6 143.3 all-reduce.1

commit v3 on v2

--- a/solution.py
+++ b/solution.py
@@ -17,6 +17,7 @@
 BLOCKS = ("col", "row")
 LOG2E = math.log2(math.e)
 MASKED = -1e30
+COST_SHARE = 0.2
 
 norm_epsilon = 1e-05
 rope_base = 10000.0
@@ -33,7 +34,9 @@
 
 
 def cost(microseconds):
-    return pl.CostEstimate(flops=int(microseconds * 1.1e9), bytes_accessed=0, transcendentals=0)
+    return pl.CostEstimate(
+        flops=int(microseconds * 1.1e9 * COST_SHARE), bytes_accessed=0, transcendentals=0
+    )
 
 
 def as_row(column):
@@ -124,7 +127,7 @@
 
 def attention_back_kernel(
     scale, prefix_ref, q_ref, grad_ref, lse_ref, centre_ref, k_ref, k_flip_ref, v_ref,
-    grad_q_ref, grad_k_ref, grad_v_ref, dot_q_ref, dot_k_ref, dot_v_ref,
+    grad_q_ref, dot_q_ref, grad_k_ref, grad_v_ref, dot_k_ref, dot_v_ref,
 ):
     query_rows = q_ref.shape[0]
     key_rows = min(512, k_ref.shape[0])
@@ -183,16 +186,18 @@
     flipped = pl.BlockSpec((width, length), lambda i, p: (0, 0))
     query_block = pl.BlockSpec((query_rows, width), lambda i, p: (i, 0))
     query_row = pl.BlockSpec((1, query_rows), lambda i, p: (0, i))
+    key_row = pl.BlockSpec((1, length), lambda i, p: (0, 0))
     result = jax.ShapeDtypeStruct((length, width), f32)
+    line = jax.ShapeDtypeStruct((1, length), f32)
     return pl.pallas_call(
         functools.partial(attention_back_kernel, width**-0.5),
         grid_spec=pltpu.PrefetchScalarGridSpec(
             num_scalar_prefetch=1,
             grid=(length // query_rows,),
             in_specs=[query_block, query_block, query_row, query_row, whole, flipped, whole],
-            out_specs=[query_block, whole, whole, query_row] + [pl.BlockSpec((1, length), lambda i, p: (0, 0))] * 2,
+            out_specs=[query_block, query_row, whole, whole] + [key_row] * 2,
         ),
-        out_shape=[result, result, result] + [jax.ShapeDtypeStruct((1, length), f32)] * 3,
+        out_shape=[result, line, result, result] + [line] * 2,
         compiler_params=pltpu.CompilerParams(vmem_limit_bytes=40 * 2**20),
         cost_estimate=cost(24),
         name="attention_backward",
@@ -210,6 +215,62 @@
 
 def add_low(one, two):
     return (one.astype(f32) + two.astype(f32)).astype(bf16)
+
+
+def step_sum_kernel(counts, halved, ids_ref, *refs):
+    half = pl.program_id(0)
+    parts, (forth_ref, back_ref, ahead_ref, behind_ref) = refs[:-4], refs[-4:]
+    for start, came_ref, out_ref, at in (
+        (0, forth_ref, ahead_ref, 0),
+        (counts[0], back_ref, behind_ref, 1),
+    ):
+        count = counts[at]
+        total = sum(ref[0].astype(f32) for ref in parts[start : start + count])
+        if not halved:
+            out_ref[...] = (total + came_ref[...].astype(f32)).astype(bf16)
+            continue
+
+        @pl.when(half == at)
+        def _():
+            out_ref[...] = (total + came_ref[...].astype(f32)).astype(bf16)
+
+        @pl.when(half != at)
+        def _():
+            out_ref[...] = total.astype(bf16)
+
+
+def step_sum(ahead, behind, forth, back):
+    parts = [(array if array.ndim == 3 else array[None], place) for array, place in ahead + behind]
+    ids = jnp.stack([jnp.asarray(place, jnp.int32) for _, place in parts])
+    _, rows, width = parts[0][0].shape
+    tile = rows // 2
+    halved = forth.shape[0] != rows
+    came = pl.BlockSpec((tile, width), (lambda i, ids: (0, 0)) if halved else (lambda i, ids: (i, 0)))
+    whole = pl.BlockSpec((tile, width), lambda i, ids: (i, 0))
+    return pl.pallas_call(
+        functools.partial(step_sum_kernel, (len(ahead), len(behind)), halved),
+        grid_spec=pltpu.PrefetchScalarGridSpec(
+            num_scalar_prefetch=1,
+            grid=(2,),
+            in_specs=[
+                pl.BlockSpec((1, tile, width), lambda i, ids, k=k: (ids[k], i, 0))
+                for k in range(len(parts))
+            ]
+            + [came, came],
+            out_specs=[whole, whole],
+        ),
+        out_shape=[jax.ShapeDtypeStruct((rows, width), bf16)] * 2,
+        cost_estimate=cost(3),
+        name="step_sum",
+    )(ids, *[array for array, _ in parts], forth, back)
+
+
+def block_sum(parts):
+    total = 0.0
+    for array, place in parts:
+        block = array if array.ndim == 2 else lax.dynamic_index_in_dim(array, place, 0, False)
+        total = total + block.astype(f32)
+    return total.astype(bf16)
 
 
 def after(value, earlier):
@@ -295,10 +356,33 @@
         ]
 
     def place_blocks(self, box, pairs):
-        for piece, ident in pairs:
-            start = (ident,) + (0,) * piece.ndim
-            box = lax.dynamic_update_slice(box, piece[None], start)
-        return box
+        blocks, ids = zip(*pairs)
+        count = len(blocks)
+
+        def kernel(ids_ref, *refs):
+            step = pl.program_id(0)
+            for k in range(count):
+
+                @pl.when(step == k)
+                def _():
+                    refs[-1][0] = refs[k][...]
+
+        whole = pl.BlockSpec(blocks[0].shape, lambda i, ids: (0,) * blocks[0].ndim)
+        return pl.pallas_call(
+            kernel,
+            grid_spec=pltpu.PrefetchScalarGridSpec(
+                num_scalar_prefetch=1,
+                grid=(count,),
+                in_specs=[whole] * count + [pl.BlockSpec(memory_space=pl.ANY)],
+                out_specs=pl.BlockSpec(
+                    (1,) + blocks[0].shape, lambda i, ids: (ids[i],) + (0,) * blocks[0].ndim
+                ),
+            ),
+            out_shape=jax.ShapeDtypeStruct(box.shape, box.dtype),
+            input_output_aliases={count + 1: 0},
+            cost_estimate=cost(count),
+            name="place_blocks",
+        )(jnp.stack(ids).astype(jnp.int32), *blocks, box)
 
     def gather_array(self, block):
         box = unwritten((self.rows * self.cols,) + block.shape, block.dtype)
@@ -306,47 +390,13 @@
             box = self.place_blocks(box, self.with_siblings(arrival))
         return box
 
-    def chip_sum(self, mine, *others):
-        for other in others:
-            mine = add_low(mine, lax.ppermute(other, PLANE, self.sibling))
-        return mine
-
-    def scatter_steps(self, parts):
-        forth = back = None
-        half = 0
-        if self.size % 2 == 0:
-            far = parts(self.size // 2)
-            half = far.shape[0] // 2
-            forth = lax.ppermute(far[:half], PLANE, self.clockwise)
-            back = lax.ppermute(far[half:], PLANE, self.counter)
-            forth, back = yield forth, back
-        for step in range((self.size - 1) // 2, 0, -1):
-            ahead, behind = parts(step), parts(-step)
-            if forth is None:
-                forth, back = ahead, behind
-            elif forth.shape[0] == half:
-                forth = jnp.concatenate([add_low(ahead[:half], forth), ahead[half:]], axis=0)
-                back = jnp.concatenate([behind[:half], add_low(behind[half:], back)], axis=0)
-            else:
-                forth, back = add_low(ahead, forth), add_low(behind, back)
-            forth = lax.ppermute(forth, PLANE, self.clockwise)
-            back = lax.ppermute(back, PLANE, self.counter)
-            forth, back = yield forth, back
-        yield parts(0), forth, back
-
-    def scatter_parts(self, parts):
-        steps = self.scatter_steps(parts)
-        terms = next(steps)
-        while len(terms) == 2:
-            terms = steps.send(terms)
-        return terms
-
-    def distances(self):
-        half = (self.size - 1) // 2
-        far = [self.size // 2] if self.size % 2 == 0 else []
-        return [0] + [d for step in range(1, half + 1) for d in (-step, step)] + far
-
-    def sum_steps(self, values):
+    def for_siblings(self, *others):
+        return [lax.ppermute(other, PLANE, self.sibling) for other in others]
+
+    def scatter(self, parts):
+        return Scatter(self, parts)
+
+    def sum_steps(self, values, kind=f32):
         rows, cols = self.rows, self.cols
         if rows & (rows - 1) or cols & (cols - 1):
             yield lax.psum(values, PLANE)
@@ -366,13 +416,50 @@
                 for col in range(cols):
                     to_row, to_col = swap(row, col)
                     pairs.append((row * cols + col, to_row * cols + to_col))
-            values = values + lax.ppermute(values, PLANE, pairs)
-            sent = yield values
-            values = values if sent is None else sent
+            sent = values.astype(kind)
+            values = sent.astype(f32) + lax.ppermute(sent, PLANE, pairs).astype(f32)
+            yield values
 
     def small_sum(self, values):
         *_, last = self.sum_steps(values)
         return last
+
+
+class Scatter:
+    def __init__(self, ring, parts):
+        self.ring, self.parts = ring, parts
+        self.step = ring.size // 2
+        self.going = None
+
+    def ready(self):
+        ring, step = self.ring, self.step
+        if 2 * step == ring.size:
+            far = block_sum(self.parts(step))
+            half = far.shape[0] // 2
+            self.going = far[:half], far[half:]
+        elif self.going is None:
+            self.going = block_sum(self.parts(step)), block_sum(self.parts(-step))
+        else:
+            self.going = tuple(step_sum(self.parts(step), self.parts(-step), *self.going))
+
+    def move(self):
+        forth, back = self.going
+        self.going = (
+            lax.ppermute(forth, PLANE, self.ring.clockwise),
+            lax.ppermute(back, PLANE, self.ring.counter),
+        )
+        self.step -= 1
+
+    def tie(self, *values):
+        self.going, *values = together(self.going, *values)
+        return values
+
+    def total(self):
+        own = [
+            array if array.ndim == 2 else lax.dynamic_index_in_dim(array, place, 0, False)
+            for array, place in self.parts(0)
+        ]
+        return *own, *self.going
 
 
 def dp_sum(part):
@@ -388,13 +475,15 @@
     return total
 
 
-def dp_all_sum(values):
+def dp_all_sum(values, kind=f32):
     count = lax.axis_size("dp")
     if count & (count - 1):
         return lax.psum(values, "dp")
     bit = 1
     while bit < count:
-        values = values + lax.ppermute(values, "dp", [(d, d ^ bit) for d in range(count)])
+        sent = values.astype(kind)
+        swapped = lax.ppermute(sent, "dp", [(d, d ^ bit) for d in range(count)])
+        values = sent.astype(f32) + swapped.astype(f32)
         bit *= 2
     return values
 
@@ -435,8 +524,8 @@
         squares_ref[pl.ds(j, 1), :] = as_row(jnp.sum(part * part, axis=1, keepdims=True))
 
 
-def project(x_blocks, gain_row, weight, rows):
-    count, block_rows, width = x_blocks.shape
+def project(x_blocks, block_rows, gain_row, weight, rows):
+    count, _, width = x_blocks.shape
     cols = count // rows
     tile = block_rows
     per = block_rows // tile
@@ -466,7 +555,7 @@
     )(x_blocks, gain_row, weight)
 
 
-def project_weight_kernel(x_ref, gain_ref, inverse_ref, grad_ref, out_ref, low_ref):
+def project_weight_kernel(x_ref, gain_ref, inverse_ref, grad_ref, weight_ref, out_ref, term_ref, low_ref):
     blocks, _, width = x_ref.shape
     inverse = as_column(inverse_ref[...])
 
@@ -479,11 +568,23 @@
         low_ref[:, at] = (x_ref[block].astype(f32) * inverse * gain_ref[:, at]).astype(bf16)
     for block in range(blocks):
         at = pl.ds(block * width, width)
-        out_ref[at, :] += dot_nn(low_ref[:, at].T, grad_ref[...])
-
-
-def project_weight(x_blocks, gain_row, inverse, grads, rows):
-    count, block_rows, width = x_blocks.shape
+        total = dot_nn(low_ref[:, at].T, grad_ref[...])
+        for j in range(3):
+            out_ref[block, j] += total[:, j * HD : (j + 1) * HD]
+
+    @pl.when(pl.program_id(0) == pl.num_programs(0) - 1)
+    def _():
+        for block in range(blocks):
+            at = pl.ds(block * width, width)
+            total = 0.0
+            for j in range(3):
+                total = total + out_ref[block, j] * weight_ref[at, j * HD : (j + 1) * HD].astype(f32)
+            total = as_row(jnp.sum(total, axis=1, keepdims=True))
+            term_ref[:, at] = total / gain_ref[:, at]
+
+
+def project_weight(x_blocks, block_rows, gain_row, inverse, grads, weight, rows):
+    count, _, width = x_blocks.shape
     cols = count // rows
     tile = block_rows // 3 if block_rows % 384 == 0 else block_rows
     per = block_rows // tile
@@ -495,14 +596,21 @@
             pl.BlockSpec((1, D), lambda i: (0, 0)),
             pl.BlockSpec((1, tile), lambda i: (0, i)),
             pl.BlockSpec((tile, 3 * HD), lambda i: (i, 0)),
+            pl.BlockSpec(weight.shape, lambda i: (0, 0)),
         ],
-        out_specs=pl.BlockSpec((D, 3 * HD), lambda i: (0, 0)),
+        out_specs=[
+            pl.BlockSpec((rows, 3, width, HD), lambda i: (0, 0, 0, 0)),
+            pl.BlockSpec((1, D), lambda i: (0, 0)),
+        ],
         scratch_shapes=[pltpu.VMEM((tile, D), bf16)],
-        out_shape=jax.ShapeDtypeStruct((D, 3 * HD), f32),
+        out_shape=[
+            jax.ShapeDtypeStruct((rows, 3, width, HD), f32),
+            jax.ShapeDtypeStruct((1, D), f32),
+        ],
         compiler_params=pltpu.CompilerParams(vmem_limit_bytes=40 * 2**20),
         cost_estimate=cost(15),
         name="projection_weight_gradient",
-    )(x_blocks, gain_row, inverse, grads)
+    )(x_blocks, gain_row, inverse, grads, weight)
 
 
 def turn_kernel(raw_ref, squares_ref, gain_ref, cosine_ref, sine_ref, q_ref, k_ref, v_ref, k_flip_ref, v_flip_ref):
@@ -568,7 +676,8 @@
 def output_branch(at, table, heads, weight_sets, x_blocks, gain_row, rows, groups):
     tok_rows = heads.shape[1]
     sets = len(weight_sets)
-    _, height, width = weight_sets[0].shape
+    width = x_blocks.shape[2]
+    height = D // (2 * rows)
     fixed = lambda shape: pl.BlockSpec(shape, lambda i, a, t: (0,) * len(shape))
     return pl.pallas_call(
         lambda at_ref, table_ref, *refs: branch_kernel(groups, sets, at_ref, *refs),
@@ -582,10 +691,11 @@
             ]
             + [
                 pl.BlockSpec(
-                    (1, height, width), lambda i, a, t, g=g, k=k: (t[(k * groups + g) * rows + i], 0, 0)
+                    (1, height, width),
+                    lambda i, a, t, g=g, k=k, half=half: (t[(k * groups + g) * rows + i], half, 0),
                 )
                 for g in range(groups)
-                for k in range(sets)
+                for k, (_, half) in enumerate(weight_sets)
             ],
             out_specs=[fixed((tok_rows, D)), fixed((tok_rows, D))],
         ),
@@ -596,15 +706,15 @@
         compiler_params=pltpu.CompilerParams(vmem_limit_bytes=40 * 2**20),
         cost_estimate=cost(6),
         name="output_projection",
-    )(at, table, heads, x_blocks, gain_row, *[w for _ in range(groups) for w in weight_sets])
+    )(at, table, heads, x_blocks, gain_row, *[w for _ in range(groups) for w, _ in weight_sets])
 
 
 def resid_kernel(
-    at_ref, own_ref, forth_ref, back_ref, logit_ref, router_ref, residual_ref, up_ref, gain_ref,
-    grad_low_ref, gain_term_ref,
+    at_ref, logit_ref, router_ref, residual_ref, up_ref, gain_ref, *refs,
 ):
+    terms, (grad_low_ref, gain_term_ref) = refs[:-2], refs[-2:]
     rows, width = up_ref.shape[0], up_ref.shape[2]
-    grad = own_ref[...].astype(f32) + forth_ref[...].astype(f32) + back_ref[...].astype(f32)
+    grad = sum(ref[...].astype(f32) for ref in terms)
     grad = grad + dot_nn(logit_ref[...], router_ref[...])
     residual = residual_ref[...]
     inverse = lax.rsqrt(jnp.sum(residual * residual, axis=1, keepdims=True) / D + norm_epsilon)
@@ -630,15 +740,13 @@
             num_scalar_prefetch=1,
             grid=(1,),
             in_specs=[
-                whole,
-                whole,
-                whole,
                 fixed(grad_logits.shape),
                 fixed(router_flip.shape),
                 whole,
                 pl.BlockSpec((rows, tok_rows, width), lambda i, a: (a[0], a[1], 0)),
                 line,
-            ],
+            ]
+            + [whole] * len(terms),
             out_specs=[whole, line],
         ),
         out_shape=[
@@ -648,7 +756,7 @@
         compiler_params=pltpu.CompilerParams(vmem_limit_bytes=40 * 2**20),
         cost_estimate=cost(3),
         name="residual_backward",
-    )(at, *terms, grad_logits, router_flip, residual, up_blocks, gain_row)
+    )(at, grad_logits, router_flip, residual, up_blocks, gain_row, *terms)
 
 
 def dispatch_kernel(hits_ref, x_ref, out_ref):
@@ -755,15 +863,18 @@
     tiles = F // tile
     first = carried is None
     whole = lambda shape: pl.BlockSpec(shape, lambda e, f, ids: (0,) * len(shape))
-    in_specs = [whole((tok_rows, D))] * count
+    once = lambda shape: pl.BlockSpec(
+        shape, lambda e, f, ids: (0,) * len(shape), pipeline_mode=pl.Buffered(1)
+    )
+    in_specs = [once((tok_rows, D))] * count
     in_specs += [
         pl.BlockSpec((1, 1, capacity, tile), lambda e, f, ids, k=k: (e, ids[k], 0, f))
         for k in range(count)
     ]
     in_specs += [
-        whole(hits.shape),
-        whole(flip.shape),
-        whole(router_flip.shape),
+        once(hits.shape),
+        once(flip.shape),
+        once(router_flip.shape),
         pl.BlockSpec((1, D, tile), lambda e, f, ids: (e, 0, f)),
         pl.BlockSpec((1, D, tile), lambda e, f, ids: (e, 0, f + tiles)),
     ]
@@ -795,14 +906,14 @@
         + [jax.ShapeDtypeStruct((experts, group * capacity, 1), f32)]
         + [jax.ShapeDtypeStruct((tok_rows, D), bf16)] * count,
         input_output_aliases=aliases,
-        compiler_params=pltpu.CompilerParams(vmem_limit_bytes=56 * 2**20),
+        compiler_params=pltpu.CompilerParams(vmem_limit_bytes=58 * 2**20),
         cost_estimate=cost(13 + 2 * count),
         name="experts",
     )(jnp.stack([*ids, first_expert]).astype(jnp.int32), *operands)
     return out[:5], out[5:]
 
 
-def combine_kernel(ids_ref, out_ref, up_ref, hits_ref, flip_ref, scale_ref, gates_ref, grad_out_ref, moe_ref):
+def combine_kernel(cores, ids_ref, slot_ref, out_ref, up_ref, hits_ref, flip_ref, scale_ref, gates_ref, grad_out_ref, *moe_refs):
     experts, _, capacity, _ = out_ref.shape
     scaled = []
     for e in range(experts):
@@ -814,49 +925,77 @@
         gates_ref[0, pl.ds(e, 1), :] = jnp.sum(hits * dots, axis=0, keepdims=True)
         grad_out_ref[e, 0] = (upstream * scale).astype(bf16)
         scaled.append((expert_out * scale).astype(bf16))
-    moe_ref[0] = dot_nn(flip_ref[0], jnp.concatenate(scaled, axis=0)).astype(bf16)
-
-
-def combine_experts(ids, expert_out, upstream_slots, hits, flip, scale):
+    total = dot_nn(flip_ref[0], jnp.concatenate(scaled, axis=0)).astype(bf16)
+    for k in range(cores):
+
+        @pl.when(slot_ref[2 * pl.program_id(0)] == k)
+        def _():
+            moe_refs[k][0] = total
+
+
+def combine_experts(ids, chips, expert_out, upstream_slots, hits, flip, scale, cores):
     experts, group, capacity, _ = upstream_slots.shape
     tok_rows = hits.shape[2]
-    by_place = pl.BlockSpec((experts, 1, capacity, D), lambda j, ids: (0, j, 0, 0))
-    by_id = lambda shape: pl.BlockSpec((1,) + shape, lambda j, ids: (ids[j], 0, 0))
-    return pl.pallas_call(
-        combine_kernel,
+    by_place = pl.BlockSpec((experts, 1, capacity, D), lambda j, ids, at: (0, j, 0, 0))
+    by_id = lambda shape: pl.BlockSpec((1,) + shape, lambda j, ids, at: (ids[j], 0, 0))
+    order = []
+    for distance, _ in chips:
+        if distance not in order:
+            order.append(distance)
+    slots = []
+    for j, (_, k) in enumerate(chips):
+        slots += [k, 0]
+    places = []
+    for core in range(cores):
+        mine = [(j, order.index(distance)) for j, (distance, k) in enumerate(chips) if k == core]
+        for j in range(group):
+            later = [place for at, place in mine if at >= j]
+            places.append(later[0] if later else mine[-1][1])
+    table = jnp.array(slots + places, jnp.int32)
+    gates, grad_out, *sums = pl.pallas_call(
+        functools.partial(combine_kernel, cores),
         grid_spec=pltpu.PrefetchScalarGridSpec(
-            num_scalar_prefetch=1,
+            num_scalar_prefetch=2,
             grid=(group,),
             in_specs=[
                 by_place,
-                pl.BlockSpec((experts, 1, capacity, D), lambda j, ids: (0, ids[j], 0, 0)),
+                pl.BlockSpec((experts, 1, capacity, D), lambda j, ids, at: (0, ids[j], 0, 0)),
                 by_id(hits.shape[1:]),
                 by_id(flip.shape[1:]),
-                pl.BlockSpec((experts, 1, capacity, 1), lambda j, ids: (0, j, 0, 0)),
+                pl.BlockSpec((experts, 1, capacity, 1), lambda j, ids, at: (0, j, 0, 0)),
             ],
-            out_specs=[by_id((experts, tok_rows)), by_place, by_id((tok_rows, D))],
+            out_specs=[by_id((experts, tok_rows)), by_place]
+            + [
+                pl.BlockSpec(
+                    (1, tok_rows, D),
+                    lambda j, ids, at, k=k: (at[2 * group + k * group + j], 0, 0),
+                )
+                for k in range(cores)
+            ],
         ),
         out_shape=[
             jax.ShapeDtypeStruct((group, experts, tok_rows), f32),
             jax.ShapeDtypeStruct((experts, group, capacity, D), bf16),
-            jax.ShapeDtypeStruct((group, tok_rows, D), bf16),
-        ],
+        ]
+        + [jax.ShapeDtypeStruct((group // cores, tok_rows, D), bf16)] * cores,
         compiler_params=pltpu.CompilerParams(vmem_limit_bytes=40 * 2**20),
         cost_estimate=cost(18),
         name="experts_combine",
     )(
         ids,
+        table,
         expert_out.reshape(experts, group, capacity, D),
         upstream_slots,
         hits,
         flip,
         scale.reshape(experts, group, capacity, 1),
     )
-
-
-def weight_grad_kernel(sides, added, pieces, rank_ref, left_ref, *refs):
+    return gates, grad_out, sums, order
+
+
+def weight_grad_kernel(sides, added, pieces, filled, rank_ref, left_ref, *refs):
     rights, refs = refs[:sides], refs[sides:]
-    more, refs = refs[:added], refs[added:]
+    more, refs = refs[:added], refs[added + filled :]
     outs, flip_ref = refs[:-1], refs[-1]
     e, m, n = pl.program_id(0), pl.program_id(1), pl.program_id(2)
 
@@ -882,7 +1021,7 @@
                         outs[0][0] = grown
 
 
-def weight_grad(left, rights, rank, rows, first=0, experts=None, more=(), pieces=False):
+def weight_grad(left, rights, rank, rows, first=0, experts=None, more=(), pieces=False, into=None):
     experts = left.shape[0] if experts is None else experts
     slots = left.shape[1]
     tile = min(512, rows)
@@ -895,10 +1034,10 @@
         out_specs = [piece] * (experts * per * sides)
         out_shape = [jax.ShapeDtypeStruct((tile, width), bf16)] * (experts * per * sides)
     else:
-        out_specs = [pl.BlockSpec((1, tile, width), lambda e, m, n, p: (e, m, n))]
-        out_shape = [jax.ShapeDtypeStruct((experts, rows, sides * width), f32)]
+        out_specs = [pl.BlockSpec((1, tile, width), lambda e, m, n, p: (e + first, m, n))]
+        out_shape = [jax.ShapeDtypeStruct((left.shape[0], rows, sides * width), f32)]
     out = pl.pallas_call(
-        functools.partial(weight_grad_kernel, sides, len(more), pieces),
+        functools.partial(weight_grad_kernel, sides, len(more), pieces, into is not None),
         grid_spec=pltpu.PrefetchScalarGridSpec(
             num_scalar_prefetch=1,
             grid=(experts, per, sides),
@@ -909,24 +1048,29 @@
                 pl.BlockSpec((1, slots, width), lambda e, m, n, p, j=j: (e + first, 0, j))
                 for _, j in shares
             ]
-            + [piece] * len(more),
+            + [piece] * len(more)
+            + [pl.BlockSpec(memory_space=pl.ANY)] * (into is not None),
             out_specs=out_specs,
             scratch_shapes=[pltpu.VMEM((tile, slots), bf16)],
         ),
         out_shape=out_shape,
+        input_output_aliases={} if into is None else {2 + sides + len(more): 0},
         compiler_params=pltpu.CompilerParams(vmem_limit_bytes=48 * 2**20),
         cost_estimate=cost(experts * rows * sides / 560 * (2 if more else 1.7)),
         name="weight_gradient",
-    )(rank.reshape(1).astype(jnp.int32), left, *[right for right, _ in shares], *more)
+    )(
+        rank.reshape(1).astype(jnp.int32), left, *[right for right, _ in shares], *more,
+        *([] if into is None else [into]),
+    )
     return out if pieces else out[0]
 
 
-def weight_grad_sends(left, rights, rows):
+def weight_grad_sends(left, rights, rows, first, experts):
     count = lax.axis_size("dp")
     rank = lax.axis_index("dp")
     onward = [(d, (d + 1) % count) for d in range(count)]
     sent, arrived = [], []
-    for e in range(left.shape[0]):
+    for e in range(first, first + experts):
         more = []
         for step in range(1, count):
             parts = weight_grad(left, rights, (rank + count - step) % count, rows, e, 1, more, True)
@@ -1044,8 +1188,16 @@
     halves = 2 if paired else 1
     half_rows = row_width // halves
     head_half = lax.dynamic_slice_in_dim(qkv_weight, half_rank * half_rows, half_rows, 0)
-    head_half = head_half.reshape(half_rows, 3, rows, HD).transpose(2, 0, 1, 3)
-    head_half = exchange_rows(head_half.reshape(rows, half_rows, 3 * HD))
+    head_half = head_half.reshape(half_rows, 3, rows, HD).transpose(2, 1, 0, 3)
+    head_out = output_weight.reshape(rows, HD, row_width // HD, HD).transpose(0, 2, 1, 3)
+    head_half = jnp.concatenate(
+        [head_half.reshape(rows, 3 * half_rows, HD), head_out.reshape(rows, row_width, HD)], axis=1
+    )
+    head_half = exchange(head_half, "row")
+    head_out = head_half[:, 3 * half_rows :].reshape(D, HD).reshape(D // HD, HD, HD)
+    head_out = head_out.transpose(0, 2, 1).reshape(D, HD)
+    head_half = head_half[:, : 3 * half_rows].reshape(rows, 3, half_rows, HD)
+    head_half = head_half.transpose(0, 2, 1, 3).reshape(rows, half_rows, 3 * HD)
     half_width = HD // 2
     frequency = rope_base ** (-2.0 * jnp.arange(half_width, dtype=f32) / HD)
     angles = jnp.arange(seq_len).astype(f32)[:, None] * frequency[None, :]
@@ -1081,21 +1233,45 @@
     weight_half = lax.dynamic_slice_in_dim(
         output_weight, half_rank * (col_width // 2), col_width // halves, 0
     )
-    weight_mine = lax.all_gather(weight_half, BLOCKS, axis=0)
-    by_core = weight_mine.reshape(
-        ring.groups, ring.cores, rows, weight_half.shape[0], row_width
-    )
+    at = [col_rank, row_rank]
+    for chip_group in range(ring.groups):
+        for half in range(2):
+            for k in range(ring.cores):
+                col = chip_group * ring.cores + (ring.core + k) % ring.cores
+                at.append((col * 2 + (half_rank + half) % 2) * (rows // 2))
+    at = jnp.stack([jnp.asarray(value, jnp.int32) for value in at])
+
+    x_steps = ring.gather_steps(jnp.concatenate([layer_input, weight_half], axis=0))
+    x_blocks = unwritten((group, res_rows + weight_half.shape[0], row_width), bf16)
+    x_blocks = ring.place_blocks(x_blocks, ring.with_siblings(next(x_steps)))
+    pieces = other_half = None
+    for step in range(ring.size // 2):
+        arrival = x_steps.send(pieces)
+        pieces = [piece for piece, _ in arrival]
+        if step == 0:
+            pieces, cosine, sine_part = together(pieces, cosine, sine_part)
+        elif step == 1:
+            pieces, head_half, x_blocks, dispatch, combine = together(
+                pieces, head_half, x_blocks, dispatch, combine
+            )
+            other_half = lax.ppermute(head_half, "dp", partner) if paired else None
+        elif step == 2:
+            pieces, x_blocks = together(pieces, x_blocks)
+        else:
+            pieces, x_blocks, other_half = together(pieces, x_blocks, other_half)
+        arrival = list(zip(pieces, [distance for _, distance in arrival]))
+        x_blocks = ring.place_blocks(x_blocks, ring.with_siblings(arrival))
     if paired:
-        own_core = lax.dynamic_index_in_dim(by_core, ring.core, 1, False)
-        own_core = own_core.reshape(ring.size, weight_half.shape[0], row_width)
-        weight_theirs = ring.from_siblings(lax.ppermute(own_core, "dp", partner))
-        weight_sets = [weight_mine] * ring.cores + weight_theirs
+        head_weight = jnp.where(
+            half_rank == 0,
+            jnp.stack([head_half, other_half], axis=1),
+            jnp.stack([other_half, head_half], axis=1),
+        )
     else:
-        weight_sets = [weight_mine[:, : col_width // 2]] * ring.cores
-        weight_sets += [weight_mine[:, col_width // 2 :]] * ring.cores
-    head_out = exchange_rows(output_weight.reshape(rows, col_width // rows, row_width))
-    head_out = head_out.transpose(0, 2, 1).reshape(D, HD)
-    at = [col_rank, row_rank]
+        head_weight = head_half
+    head_weight = head_weight.reshape(D, 3 * HD)
+    weight_flip = head_weight.T
+    half_place = res_rows // (col_width // 2)
     table = []
     for half in range(2):
         for k in range(ring.cores):
@@ -1104,42 +1280,16 @@
                 for row in range(rows):
                     whole_plane = half == 0 or not paired
                     table.append(col * rows + row if whole_plane else chip_group * rows + row)
-    for chip_group in range(ring.groups):
-        for half in range(2):
-            for k in range(ring.cores):
-                col = chip_group * ring.cores + (ring.core + k) % ring.cores
-                at.append((col * 2 + (half_rank + half) % 2) * (rows // 2))
-    at = jnp.stack([jnp.asarray(value, jnp.int32) for value in at])
     table = jnp.stack([jnp.asarray(value, jnp.int32) for value in table])
-
-    x_steps = ring.gather_steps(layer_input)
-    x_arrivals = [next(x_steps), next(x_steps)]
-    pieces, head_half = together([piece for piece, _ in x_arrivals[-1]], head_half)
-    x_arrivals[-1] = list(zip(pieces, [distance for _, distance in x_arrivals[-1]]))
-    x_arrivals.append(x_steps.send(pieces))
     if paired:
-        other_half = lax.ppermute(head_half, "dp", partner)
-        pieces, other_half, head_out = together(
-            [piece for piece, _ in x_arrivals[-1]], other_half, head_out
+        own_core = x_blocks[:, res_rows:].reshape(
+            ring.groups, ring.cores, rows, weight_half.shape[0], row_width
         )
-        x_arrivals[-1] = list(zip(pieces, [distance for _, distance in x_arrivals[-1]]))
-        head_weight = jnp.where(
-            half_rank == 0,
-            jnp.stack([head_half, other_half], axis=1),
-            jnp.stack([other_half, head_half], axis=1),
-        )
-    else:
-        head_weight = head_half
-    x_arrivals += [x_steps.send(pieces), *x_steps]
-    head_weight = head_weight.reshape(D, 3 * HD)
-    weight_flip = head_weight.T
-    x_blocks = unwritten((group,) + layer_input.shape, bf16)
-    for arrival in x_arrivals:
-        x_blocks = ring.place_blocks(x_blocks, ring.with_siblings(arrival))
-    x_blocks, cosine, sine_part, dispatch, combine = together(
-        x_blocks, cosine, sine_part, dispatch, combine
-    )
-    projected, inv_first, square_terms = project(x_blocks, gain_rows[0:1], head_weight, rows)
+        own_core = lax.dynamic_index_in_dim(own_core, ring.core, 1, False)
+        own_core = own_core.reshape(ring.size, weight_half.shape[0], row_width)
+        theirs = lax.ppermute(own_core, "dp", partner)
+    upstream_blocks = lax.all_gather(after(cotangent, pieces), BLOCKS, axis=0)
+    projected, inv_first, square_terms = project(x_blocks, res_rows, gain_rows[0:1], head_weight, rows)
     squares = ring.small_sum(square_terms)
 
     head_first = block_rank * HD
@@ -1148,44 +1298,53 @@
         projected, squares, gain_pair, cosine, sine_part
     )
 
-    upstream_blocks = lax.all_gather(after(cotangent, x_blocks), BLOCKS, axis=0)
     query_rows = max(seq_len // 6, 128)
     attn_head, lse = attention(query_low, key_low, value_flip, prefix_len, query_rows)
     attn_tokens = exchange(attn_head.reshape(group, tok_rows, HD), BLOCKS)
+    weight_sets = [(x_blocks, half_place)] * ring.cores
+    if paired:
+        attn_tokens, theirs = together(attn_tokens, theirs)
+        weight_sets += [(block, 0) for block in ring.from_siblings(theirs)]
+    else:
+        weight_sets += [(x_blocks, half_place + 1)] * ring.cores
     upstream_slots = dispatch_blocks(dispatch, upstream_blocks, rows, local_experts)
     residual, second_low = output_branch(
         at, table, attn_tokens, weight_sets, x_blocks, gain_rows[3:4], rows, ring.groups
     )
     feat_steps = ring.gather_steps(second_low)
-    arrivals = [next(feat_steps), next(feat_steps)]
     grad_raw = einsum(
         "end,efd->enf", upstream_slots.reshape(local_experts, group * capacity, D), reduce_weight
     ).reshape(local_experts, group, capacity, F)
-    pieces, upstream_slots = together([piece for piece, _ in arrivals[-1]], upstream_slots)
-    arrivals[-1] = list(zip(pieces, [distance for _, distance in arrivals[-1]]))
-    arrivals.append(feat_steps.send(pieces))
-    pieces, grad_raw = together([piece for piece, _ in arrivals[-1]], grad_raw)
-    arrivals[-1] = list(zip(pieces, [distance for _, distance in arrivals[-1]]))
-    arrivals.append(feat_steps.send(pieces))
 
     carried = None
-    waiting, feat_parts, places = [], {}, {}
-    calls = {1: 0, ring.size // 2 - 2: 3, ring.size // 2: 1}
-    start = {0: 0, 3: group - 2 * ring.cores, 1: 3 * ring.cores}
-    for step in range(ring.size // 2 + 1):
-        if step == len(arrivals):
-            pieces, *carried = together([piece for piece, _ in arrivals[-1]], *carried)
-            arrivals.append(feat_steps.send(pieces))
-        arrival = arrivals[step]
-        pairs = ring.with_siblings(arrival)
-        for k, (_, distance) in enumerate(arrival):
-            waiting.append((distance, pairs[k * ring.cores : (k + 1) * ring.cores]))
+    waiting = [
+        (block, ident, 0, k)
+        for k, (block, ident) in enumerate(ring.with_siblings(next(feat_steps)))
+    ]
+    calls = {1: 0, ring.size // 2 - 1: 1}
+    feat_sums, taken_by = {}, {}
+    pieces = None
+    for step in range(ring.size // 2):
+        arrival = feat_steps.send(pieces)
+        pieces = [piece for piece, _ in arrival]
+        if step == 0:
+            pieces, upstream_slots = together(pieces, upstream_slots)
+        elif step == 1:
+            pieces, grad_raw = together(pieces, grad_raw)
+        elif step == 2:
+            pieces, *carried = together(pieces, *carried)
+        direct, later = [], []
+        for piece, (_, distance) in zip(pieces, arrival):
+            for k, (block, ident) in enumerate(ring.with_siblings([(piece, distance)])):
+                (later if k else direct).append((block, ident, distance, k))
+        waiting += direct
         if step not in calls:
+            waiting += later
             continue
-        taken = [pair for _, chip in waiting for pair in chip]
-        carried, feat_sums = run_experts(
-            [block for block, _ in taken],
-            [ident for _, ident in taken],
+        taken, waiting = (waiting, later) if step == 1 else (waiting + later, [])
+        carried, sums = run_experts(
+            [block for block, *_ in taken],
+            [ident for _, ident, *_ in taken],
             first_expert,
             grad_raw,
             dispatch,
@@ -1195,23 +1354,23 @@
             carried,
             calls[step],
         )
-        for k, (distance, chip) in enumerate(waiting):
-            feat_parts[distance] = ring.chip_sum(*feat_sums[k * ring.cores : (k + 1) * ring.cores])
-            for j, (_, ident) in enumerate(chip):
-                places[start[calls[step]] + k * ring.cores + j] = (distance, ident)
-        waiting.clear()
+        for (_, ident, distance, k), total in zip(taken, sums):
+            feat_sums[distance, k] = total
+        taken_by[calls[step] * len(taken)] = [item[1:] for item in taken]
+    by_slot = [item for start in sorted(taken_by) for item in taken_by[start]]
+    places = [ident for ident, _, _ in by_slot]
+    chips = [(distance, k) for _, distance, k in by_slot]
+    feat_parts = {}
+
+    def feat_part(distance):
+        if distance not in feat_parts:
+            others = ring.for_siblings(*[feat_sums[distance, k] for k in range(1, ring.cores)])
+            feat_parts[distance] = [(block, 0) for block in (feat_sums[distance, 0], *others)]
+        return feat_parts[distance]
+
     slot_rows, hidden, grad_gate_pre, grad_up_pre, slot_gate = carried
 
-    far = ring.size // 2
-    feat_parts[far], slot_rows = together(feat_parts[far], slot_rows)
-    grad_steps = ring.scatter_steps(lambda distance: feat_parts[distance])
-    grad_terms = next(grad_steps)
-    expand_sides = [grad_gate_pre, grad_up_pre]
-    expand_sent, expand_arrived = weight_grad_sends(slot_rows, expand_sides, D // dp_count)
-    grad_terms, expand_sent, hidden = together(grad_terms, expand_sent, hidden)
-    grad_terms = grad_steps.send(grad_terms)
-    expert_out = einsum("enf,efd->end", hidden, reduce_weight).astype(bf16)
-    arriving, arrived = list(expand_arrived), []
+    arriving, arrived = [], []
 
     def taking(count, *values):
         taken, arriving[:count] = arriving[:count], []
@@ -1219,18 +1378,59 @@
         arrived.extend(taken)
         return values
 
-    grad_terms, expert_out = taking(1, grad_terms, expert_out)
-    grad_terms = grad_steps.send(grad_terms)
-    ids = jnp.stack([places[k][1] for k in range(group)]).astype(jnp.int32)
-    gate_tokens, grad_out_slots, moe_sums = combine_experts(
-        ids, expert_out, upstream_slots, dispatch, combine, slot_gate
+    def ahead_tie(scatter, parts, *values):
+        steps = [scatter.step, -scatter.step] if scatter.step else []
+        terms = {step: scatter.parts(step) for step in steps}
+        blocks = [[block for block, _ in terms[step] if block.ndim == 2] for step in steps]
+        *values, blocks = scatter.tie(*values, blocks)
+        for step, given in zip(steps, blocks):
+            given = iter(given)
+            parts[step] = [
+                (next(given), 0) if block.ndim == 2 else (block, place) for block, place in terms[step]
+            ]
+        return values
+
+    grads = ring.scatter(feat_part)
+    grads.ready()
+    expand_sides = [grad_gate_pre, grad_up_pre]
+    expand_rows, reduce_rows = D // dp_count, F // dp_count
+    half = local_experts // 2
+    slot_rows, = grads.tie(slot_rows)
+    grads.move()
+    sent, pieces = weight_grad_sends(slot_rows, expand_sides, expand_rows, 0, half)
+    arriving += pieces
+    sent, = ahead_tie(grads, feat_parts, sent)
+    grads.ready()
+    slot_rows, hidden = grads.tie(slot_rows, hidden)
+    grads.move()
+    expert_out = einsum("enf,efd->end", hidden, reduce_weight).astype(bf16)
+    expert_out, = taking(1, *ahead_tie(grads, feat_parts, expert_out))
+    grads.ready()
+    expert_out, = grads.tie(expert_out)
+    grads.move()
+    ids = jnp.stack(places).astype(jnp.int32)
+    gate_tokens, grad_out_slots, moe_sums, moe_order = combine_experts(
+        ids, chips, expert_out, upstream_slots, dispatch, combine, slot_gate, ring.cores
     )
     grad_out_slots = grad_out_slots.reshape(local_experts, group * capacity, D)
+    grad_out_slots, moe_sums, gate_tokens = taking(
+        1, *ahead_tie(grads, feat_parts, grad_out_slots, moe_sums, gate_tokens)
+    )
+    grads.ready()
+    moe_sums, gate_tokens, slot_rows = grads.tie(moe_sums, gate_tokens, slot_rows)
+    grads.move()
     grad_probs = exchange(gate_tokens, BLOCKS)
-    grad_terms, grad_out_slots, moe_sums = taking(1, grad_terms, grad_out_slots, moe_sums)
-    grad_terms = grad_steps.send(grad_terms)
-    reduce_sent, reduce_arrived = weight_grad_sends(hidden, [grad_out_slots], F // dp_count)
-    arriving += reduce_arrived
+    sent, pieces = weight_grad_sends(
+        slot_rows, expand_sides, expand_rows, half, local_experts - half
+    )
+    arriving += pieces
+    expand_count = len(arrived) + len(arriving)
+    moe_others = [lax.ppermute(other, PLANE, ring.sibling) for other in moe_sums[1:]]
+
+    def moe_part(distance):
+        place = moe_order.index(distance)
+        return [(array, place) for array in (moe_sums[0], *moe_others)]
+
     grad_probs = grad_probs.reshape(cols, rows, local_experts, tok_rows)
     grad_probs = grad_probs.transpose(1, 0, 2, 3).reshape(expert_count, tok_rows)
     logits = dot_nt(router_flip, second_low)
@@ -1238,79 +1438,132 @@
     grad_logits = probs * (grad_probs - jnp.sum(probs * grad_probs, axis=0, keepdims=True))
     grad_logits = grad_logits.T.astype(bf16)
     router_term = einsum("te,td->ed", grad_logits, second_low)
-    while len(grad_terms) == 2:
-        grad_terms = grad_steps.send(grad_terms)
+    grad_logits, router_term, moe_others, sent = taking(
+        1, *grads.tie(grad_logits, router_term, moe_others, sent)
+    )
+    moes = ring.scatter(moe_part)
+    moes.ready()
+    grad_terms = grads.total()
 
     grad_branch, gain_second_term = residual_back(
         at[:2], grad_terms, grad_logits, router_flip, residual, upstream_blocks, gain_rows[3:4], rows
     )
-    grad_branch, reduce_sent, router_term = taking(1, grad_branch, reduce_sent, router_term)
     branch_steps = ring.gather_steps(grad_branch)
-    branch_arrivals = [next(branch_steps)]
-    router_total = lax.psum(router_term, ("dp", "row", "col"))
+    branch_all = unwritten((group, tok_rows, D), bf16)
+    branch_all = ring.place_blocks(branch_all, ring.with_siblings(next(branch_steps)))
+    rank = lax.axis_index("dp")
+    expand_grad = None
+    extra = []
     pieces = None
-    for arrival in iter(lambda: branch_steps.send(pieces), None):
-        pieces, = taking(1, [piece for piece, _ in arrival])
-        branch_arrivals.append(list(zip(pieces, [distance for _, distance in arrival])))
-        if len(branch_arrivals) == ring.size // 2 + 1:
-            break
-    branch_all = unwritten((group, tok_rows, D), bf16)
-    for arrival in branch_arrivals:
+    for step in range(ring.size // 2):
+        arrival = branch_steps.send(pieces)
+        if step == ring.size // 2 - 1:
+            moes.move()
+        pieces, branch_all, extra, moes.going = taking(
+            1,
+            [piece for piece, _ in arrival],
+            branch_all,
+            extra,
+            moes.going,
+        )
+        if step == 0:
+            left, = together(hidden, pieces)[:1]
+            extra, parts = weight_grad_sends(
+                left, [grad_out_slots], reduce_rows, 0, local_experts
+            )
+            arriving += parts
+        elif step == 2:
+            expand_grad, = extra
+        elif step == 1:
+            left, = together(slot_rows, pieces)[:1]
+            expand_grad = weight_grad(
+                left, expand_sides, rank, expand_rows, 0, half, arrived[: expand_count // 2]
+            )
+            extra = [expand_grad]
+        else:
+            expand_grad, = extra
+        arrival = list(zip(pieces, [distance for _, distance in arrival]))
         branch_all = ring.place_blocks(branch_all, ring.with_siblings(arrival))
 
-    moe_tokens = lax.psum_scatter(
-        after(moe_sums, branch_all), BLOCKS, scatter_dimension=0, tiled=False
-    )
+    moes.ready()
+    branch_all, = moes.tie(branch_all)
+    moes.move()
     grad_attn = dot(branch_all.reshape(seq_len, D), head_out).astype(bf16)
     centre = jnp.sum(attn_head.astype(f32) * grad_attn.astype(f32), axis=1)[None]
-    *head_grads, dot_query, dot_key, dot_value = attention_back(
+    grad_query, dot_query, grad_key, grad_value, dot_key, dot_value = attention_back(
         query_low, key_low, key_flip, value_low, grad_attn, lse, centre, prefix_len, query_rows
     )
+    head_grads = [grad_query, grad_key, grad_value]
     dots = jnp.concatenate([dot_query, dot_key, dot_value], axis=0)
-    dots, = taking(1, dots)
+    dots, = taking(2, *moes.tie(dots))
+    moes.ready()
+    dots, = moes.tie(dots)
     dots = ring.small_sum(dots)
+    dots, = moes.tie(dots)
+    moes.move()
 
     grad_qkv, gain_pair_terms, grad_first_blocks = unproject(
         head_grads, projected, squares, dots, gain_pair, cosine, sine_part, weight_flip, rows, cols
     )
-    grad_first_blocks, = taking(2, grad_first_blocks)
-
-    def blocks_sum(blocks, distance):
-        return ring.chip_sum(
-            *[lax.dynamic_index_in_dim(blocks, ident, 0, False) for ident in ring.block_ids(distance)]
-        )
-
-    first_far = blocks_sum(grad_first_blocks, ring.size // 2)
-    first_far, grad_first_blocks = together(first_far, grad_first_blocks)
 
     def first_part(distance):
-        return first_far if distance == ring.size // 2 else blocks_sum(grad_first_blocks, distance)
-
-    first_steps = ring.scatter_steps(first_part)
-    grad_first = next(first_steps)
-    grad_first, grad_qkv = together(grad_first, grad_qkv)
-    grad_first = first_steps.send(grad_first)
-    qkv_term = project_weight(x_blocks, gain_rows[0:1], inv_first, grad_qkv, rows)
-    grad_first, qkv_term = taking(1, grad_first, qkv_term)
-    grad_first = first_steps.send(grad_first)
-    rank = lax.axis_index("dp")
-    expand_grad = weight_grad(
-        slot_rows, expand_sides, rank, D // dp_count, more=arrived[: len(expand_arrived)]
-    )
-    layer_tokens = (residual + moe_tokens.astype(f32)).astype(bf16)
-    layer_output = lax.all_to_all(layer_tokens, "row", split_axis=1, concat_axis=0, tiled=True)
-    grad_first, expand_grad, layer_output = taking(
-        len(arriving), grad_first, expand_grad, layer_output
-    )
-    grad_first = first_steps.send(grad_first)
+        if distance not in first_parts:
+            mine, *others = ring.block_ids(distance)
+            others = ring.for_siblings(
+                *[lax.dynamic_index_in_dim(grad_first_blocks, k, 0, False) for k in others]
+            )
+            first_parts[distance] = [(grad_first_blocks, mine)] + [(block, 0) for block in others]
+        return first_parts[distance]
+
+    first_parts = {}
+    grad_first_blocks, grad_qkv = taking(1, *moes.tie(grad_first_blocks, grad_qkv))
+    first_far = block_sum(first_part(ring.size // 2))
+    moes.ready()
+    first_far, grad_first_blocks = moes.tie(first_far, grad_first_blocks)
+    first_parts = {ring.size // 2: [(first_far, 0)]}
+    firsts = ring.scatter(first_part)
+    firsts.ready()
+    firsts.move()
+    moes.move()
     output_term = dot(attn_head.T, branch_all.reshape(seq_len, D))
     output_term = output_term.astype(bf16).reshape(HD, rows, row_width).transpose(1, 0, 2)
-    output_sum = exchange_rows(output_term).reshape(col_width, row_width)
+    output_term, = taking(1, *moes.tie(*ahead_tie(firsts, first_parts, output_term)))
+    moe_terms = moes.total()
+    firsts.ready()
+    grad_qkv, slot_rows = firsts.tie(grad_qkv, slot_rows)
+    firsts.move()
+    qkv_term, gain_first_term = project_weight(
+        x_blocks, res_rows, gain_rows[0:1], inv_first, grad_qkv, head_weight, rows
+    )
+    qkv_rows = row_width // dp_count
+    qkv_sum = dp_sum(
+        lambda rank: lax.dynamic_slice_in_dim(qkv_term, rank * qkv_rows, qkv_rows, 2)
+    )
+    output_sum = exchange(output_term, "row").reshape(col_width, row_width)
+    qkv_term, = taking(1, *ahead_tie(firsts, first_parts, qkv_term))
+    firsts.ready()
+    slot_rows, = firsts.tie(slot_rows)
+    firsts.move()
+    expand_grad = weight_grad(
+        slot_rows, expand_sides, rank, expand_rows, half, local_experts - half,
+        arrived[expand_count // 2 : expand_count], into=expand_grad,
+    )
+    layer_tokens = residual
+    for term in moe_terms:
+        layer_tokens = layer_tokens + term.astype(f32)
+    layer_tokens = layer_tokens.astype(bf16)
+    layer_output = lax.all_to_all(layer_tokens, "row", split_axis=1, concat_axis=0, tiled=True)
+    expand_grad, output_sum = taking(
+        len(arriving), *ahead_tie(firsts, first_parts, expand_grad, output_sum)
+    )
+    firsts.ready()
+    hidden, qkv_sum = firsts.tie(hidden, qkv_sum)
+    firsts.move()
     reduce_grad = weight_grad(
-        hidden, [grad_out_slots], rank, F // dp_count, more=arrived[len(expand_arrived) :]
-    )
-    grad_first, output_sum, reduce_grad = together(grad_first, output_sum, reduce_grad)
-    grad_first = first_steps.send(grad_first)
+        hidden, [grad_out_slots], rank, reduce_rows, more=arrived[expand_count:]
+    )
+    reduce_grad, layer_output = firsts.tie(reduce_grad, layer_output)
+    grad_first = firsts.total()
     grad_first = sum(term.astype(f32) for term in grad_first)
     grad_block = lax.dynamic_slice(
         branch_all, (col_rank * rows, 0, row_rank * row_width), (rows, tok_rows, row_width)
@@ -1332,32 +1585,23 @@
             output_sum, rank * output_rows, output_rows, 0
         ).astype(f32)
     )
-    gain_first_term = jnp.sum(qkv_term * head_weight.astype(f32), axis=1) / gain_rows[0]
-    qkv_rows = row_width // dp_count
-    qkv_shaped = qkv_term.reshape(rows, row_width, 3 * HD)
-    qkv_sum = dp_sum(
-        lambda rank: lax.dynamic_slice_in_dim(qkv_shaped, rank * qkv_rows, qkv_rows, 1)
-    )
-    qkv_grad = exchange_rows(qkv_sum.astype(bf16)).reshape(rows, qkv_rows, 3, HD)
-    qkv_grad = qkv_grad.transpose(1, 2, 0, 3).reshape(1, qkv_rows, 3, col_width).astype(f32)
+    qkv_grad = exchange(qkv_sum.astype(bf16), "row").transpose(2, 1, 0, 3)
+    qkv_grad = qkv_grad.reshape(1, qkv_rows, 3, col_width).astype(f32)
 
     def placed(term):
         return lax.dynamic_update_slice(jnp.zeros((D,), f32), term, (head_first,))
 
-    gain_total = dp_all_sum(
-        ring.small_sum(
-            jnp.concatenate(
-                [
-                    jnp.stack(
-                        [gain_first_term, placed(gain_pair_terms[0]), placed(gain_pair_terms[1])]
-                    ),
-                    gain_second_term,
-                ],
-                axis=0,
-            )
-        )
-    )
-    router_total = router_total.T
+    gain_terms = jnp.concatenate(
+        [
+            gain_first_term,
+            jnp.stack([placed(gain_pair_terms[0]), placed(gain_pair_terms[1])]),
+            gain_second_term,
+        ],
+        axis=0,
+    )
+    gain_total = jnp.sum(lax.all_gather(gain_terms, ("dp", "row", "col"), axis=0), axis=0)
+    router_all = lax.all_gather(router_term.astype(bf16), ("dp", "row", "col"), axis=0)
+    router_total = jnp.sum(router_all.astype(f32), axis=0).T
     return (
         layer_output,
         input_grad.astype(bf16),

time: 927 us -> 877 us (0.946)
  waiting for transfers between devices: 300 us -> 178 us
  Pallas kernels: 261 us -> 341 us
  blocking collectives: 0 us -> 43.3 us
  local copies, waits for them, and re-layouts: 112 us -> 77.2 us
  starting transfers between devices: 135 us -> 116 us
    pallas_call x1 -> x20, Pallas kernels: 17.1 us -> 102 us  [the longest x10 44.8 us: place_blocks(): pl.pallas_call(kernel, grid_spec=pltpu.PrefetchScalarGridSpec(num_scalar_...]
    ppermute x59 -> x51, waiting for transfers between devices: 119 us -> 49.7 us  [the longest x8 20.5 us: sum_steps(): values = sent.astype(f32) + lax.ppermute(sent, PLANE, pairs).astype(f32)]
    ppermute x12, waiting for transfers between devices: 83.8 us -> 20.9 us  [weight_grad_sends(): more = [lax.ppermute(part, 'dp', onward) for part in parts]]
    dynamic_update_slice x46 -> x0, local copies, waits for them, and re-layouts: 50.2 us -> none  [the longest x32 39.8 us: place_blocks(): box = lax.dynamic_update_slice(box, piece[None], start)]
    ppermute x59 -> x51, starting transfers between devices: 78.5 us -> 33.5 us  [the longest x12 14 us: move(): lax.ppermute(back, PLANE, self.ring.counter)]
    all_to_all x0 -> x1, blocking collectives: none -> 43.3 us  [exchange(): return lax.all_to_all(pieces, axes, split_axis=0, concat_axis=0, tiled=True)]
    convert_element_type x18 -> x5, other arithmetic: 27.4 us -> 8.43 us  [the longest x3 4.61 us: block_sum(): return total.astype(bf16)]
    ppermute x3, waiting for transfers between devices: 6.2 us -> 19.4 us  [gather_steps(): back = lax.ppermute(back[half:], PLANE, self.counter)]
  transfers between devices with their start and end apart: 132 -> 125, of which waited for: 58 -> 50; matrix products, arithmetic and copies ran while one was open for 20% -> 15% of each run, Pallas kernels for 26% -> 35%
where the time goes in v3:
time: 877 us; the launch traced here: 864 us
  Pallas kernels  341 us (39%)
  waiting for transfers between devices  178 us (20%)
  starting transfers between devices  116 us (13%)
  local copies, waits for them, and re-layouts  77.2 us (9%)
  other arithmetic  49.2 us (6%)
  blocking collectives  43.3 us (5%)
  matrix products  43 us (5%)
  between operations  16.5 us (2%)
    pallas_call x2, Pallas kernels, run_experts(): pl.pallas_call(functools.partial(experts_kernel, count, first), grid_spec...  64.3 us
    pallas_call x7, Pallas kernels, weight_grad(): pl.pallas_call(functools.partial(weight_grad_kernel, sides, len(more), pi...  56.4 us
    pallas_call x10, Pallas kernels, place_blocks(): pl.pallas_call(kernel, grid_spec=pltpu.PrefetchScalarGridSpec(num_scalar_...  44.8 us
    all_to_all x1, blocking collectives, exchange(): return lax.all_to_all(pieces, axes, split_axis=0, concat_axis=0, tiled=True)  43.3 us
    pallas_call x9, Pallas kernels, step_sum(): pl.pallas_call(functools.partial(step_sum_kernel, (len(ahead), len(behind...  38.5 us
    unnamed x168, local copies, waits for them, and re-layouts  36.1 us
    ppermute x9, waiting for transfers between devices, gather_steps(): forth = lax.ppermute(forth, PLANE, self.clockwise)  27.8 us
    all_to_all x4, waiting for transfers between devices, exchange(): return lax.all_to_all(pieces, axes, split_axis=0, concat_axis=0, tiled=True)  27.7 us
  transfers between devices with their start and end apart: 125, of which 50 were waited for; matrix products, arithmetic and copies ran while one was open for 15% of the time, Pallas kernels for 35%

profile of v3, /device:TPU:0, one launch (start us, length us, event | category | flops | bytes accessed | tf_op | source)
XLA Modules:
  0.0 864.4 jit_solution(4320910971475589493)
XLA Ops:
  56.2 12.9 %all-to-all-done = bf16[4,1280,128]{2,1,0:T(8,128)(2,1)} async-done(((bf16[4,1280,128]{2,1,0:T(8,128)(2,1)}), bf16[4,1280,128]{2,1,0:T(8,128)(2,1)}, u32[]{:S(2)}, u32[]{:S(2)}) %all-to-all-start) | async-done | bytes 1310752 | tf_op jit(solution)/shard_map/all_to_all | solution.py:506
  82.5 8.6 collective-permute-start.10
  97.6 16.5 %collective-permute-done.10.refs_0_ = bf16[1024,512]{1,0:T(8,128)(2,1)S(1)} collective-permute-done((bf16[1024,512]{1,0:T(8,128)(2,1)}, bf16[1024,512]{1,0:T(8,128)(2,1)S(1)}, u32[]{:S(2)}, u32[]{:S(2)}) %collective-permute-start.10) | collective-permute-done | bytes 1048608 | tf_op jit(solution)/shard_map/ppermute | solution.py:340
  123.8 11.2 %collective-permute-done.15 = bf16[512,512]{1,0:T(8,128)(2,1)} collective-permute-done((bf16[512,512]{1,0:T(8,128)(2,1)}, bf16[512,512]{1,0:T(8,128)(2,1)}, u32[]{:S(2)}, u32[]{:S(2)}) %collective-permute-start.15) | collective-permute-done | bytes 524320 | tf_op jit(solution)/shard_map/ppermute | solution.py:348
  150.6 13.3 %norm_and_project.1 = (f32[3072,384]{1,0:T(8,128)}, f32[1,3072]{1,0:T(1,128)S(1)}, f32[2,3072]{1,0:T(2,128)S(1)}) custom-call(bf16[16,1024,512]{2,1,0:T(8,128)(2,1)} %place_blocks.14.x_ref.refs_1_.refs_3_.refs_4_.refs_7_.refs_8_, f32[1,2048]{1,0:T(1,128)S(1)} %get-tuple-element.594.gain_ref, bf16[2048,384]{1,0:T(8,128)(2,1)S(1)} %bitcast.206), custom_call_target="tpu_custom_call" | custom-call | flops 3080000000 | tf_op jit(solution)/shard_map/norm_and_project/pallas_call | solution.py:533
  180.7 8.3 query_key_value.1
  192.4 16.4 %attention_forward.1 = (bf16[3072,128]{1,0:T(8,128)(2,1)S(1)}, f32[1,3072]{1,0:T(1,128)S(1)}) custom-call(s32[1]{0:T(128)S(6)} %copy.234.prefix_ref, bf16[3072,128]{1,0:T(8,128)(2,1)S(1)} %copy-done.46, bf16[3072,128]{1,0:T(8,128)(2,1)S(1)} %copy-done.48, bf16[128,3072]{1,0:T(8,128)(2,1)S(1)} %copy-done.52), custom_call_target="tpu_custom_call" | custom-call | flops 3740000000 | tf_op jit(solution)/shard_map/attention_forward/pallas_call | solution.py:105
  209.8 43.3 %all_to_all.44.refs_0_ = bf16[16,192,128]{2,1,0:T(8,128)(2,1)S(1)} all-to-all(bf16[16,192,128]{2,1,0:T(8,128)(2,1)S(1)} %bitcast.212), channel_id=1, replica_groups=mesh['dp'=2,'row'=4,'col'=4] {'col','row'}, dimensions={0} | all-to-all | bytes 1572864 | tf_op jit(solution)/shard_map/all_to_all | solution.py:506
  269.9 14.3 %cotangent_to_slots.1.up_ref = bf16[2,16,48,2048]{3,2,1,0:T(8,128)(2,1)} custom-call(bf16[16,96,192]{2,1,0:T(8,128)(2,1)} %copy.178.hits_ref.refs_16_, bf16[16,768,512]{2,1,0:T(8,128)(2,1)} %bitcast.238), custom_call_target="tpu_custom_call" | custom-call | flops 3080000000 | tf_op jit(solution)/shard_map/cotangent_to_slots/pallas_call | solution.py:775
  289.0 12.9 %fusion.26 = f32[2,768,1024]{2,1,0:T(8,128)} fusion(bf16[2,768,2048]{2,1,0:T(8,128)(2,1)} %bitcast.240, bf16[2,1024,2048]{2,1,0:T(8,128)(2,1)} %param.18), kind=kOutput, calls=%fused_computation.113 | convolution fusion | flops 6442450944 | bytes 20971520 | tf_op jit(solution)/shard_map/end,efd->enf/dot_general | solution.py:1152
  309.8 32.0 %experts.2 = (bf16[2,768,2048]{2,1,0:T(8,128)(2,1)}, bf16[2,768,1024]{2,1,0:T(8,128)(2,1)}, bf16[2,768,1024]{2,1,0:T(8,128)(2,1)}, bf16[2,768,1024]{2,1,0:T(8,12...) custom-call(s32[9]{0:T(128)} %stack.304.ids_ref, ...), custom_call_target="tpu_custom_call" | custom-call | flops 6380000256 | tf_op jit(solution)/shard_map/experts/pallas_call | solution.py:891
  355.8 32.3 %experts.3 = (bf16[2,768,2048]{2,1,0:T(8,128)(2,1)}, bf16[2,768,1024]{2,1,0:T(8,128)(2,1)}, bf16[2,768,1024]{2,1,0:T(8,128)(2,1)}, bf16[2,768,1024]{2,1,0:T(8,12...) custom-call(s32[9]{0:T(128)} %stack.260.ids_ref, ...), custom_call_target="tpu_custom_call", output_to_operand_aliasing={{0}: (22, {}), {1}: (23, {}), {2}: (24, {}), {3}: (25, {}),... | custom-call | flops 6380000256 | tf_op jit(solution)/shard_map/experts/pallas_call | solution.py:891
  413.2 11.9 %convolution_convert_fusion = bf16[2,768,2048]{2,1,0:T(8,128)(2,1)} fusion(bf16[2,768,1024]{2,1,0:T(8,128)(2,1)S(1)} %copy-done.3, bf16[2,1024,2048]{2,1,0:T(8,128)(2,1)} %param.18), kind=kOutput, calls=%fused_computation.2 | convolution fusion | flops 6445596672 | bytes 17825792 | tf_op jit(solution)/shard_map/enf,efd->end/dot_general | solution.py:1152
  441.8 18.3 %experts_combine.1 = (f32[16,2,192]{2,1,0:T(2,128)}, bf16[2,16,48,2048]{3,2,1,0:T(8,128)(2,1)S(1)}, bf16[8,192,2048]{2,1,0:T(8,128)(2,1)}, bf16[8,192,2048]{2,1,0:T(8,128)(2,1)}) custom-call(s32[16]{0:T(128)S(1)} %stack.305.ids_ref, s32[64]{0:T(128)S(1)} %copy-done.37, bf16[2,16,48,2048]{3,2,1,0:T(8,128)(2,1)} %bitcast.244, ...), custom_call_target="tpu_custom_call" | custom-call | flops 3960000000 | tf_op jit(solution)/shard_map/experts_combine/pallas_call | solution.py:955
  477.6 8.0 weight_gradient.8
  515.4 9.2 %collective-permute-done.65.refs_5_ = bf16[512,1024]{1,0:T(8,128)(2,1)} collective-permute-done((bf16[512,1024]{1,0:T(8,128)(2,1)}, bf16[512,1024]{1,0:T(8,128)(2,1)}, u32[]{:S(2)}, u32[]{:S(2)}) %collective-permute-start.65) | collective-permute-done | bytes 1048608 | tf_op jit(solution)/shard_map/ppermute | solution.py:1077
  552.2 10.0 %weight_gradient.11.refs_6_ = f32[2,1024,2048]{2,1,0:T(8,128)} custom-call(s32[1]{0:T(128)} %bitcast.92.rank_ref, bf16[2,768,2048]{2,1,0:T(8,128)(2,1)} %get-tuple-element.494.left_ref, bf16[2,768,1024]{2,1,0:T(8,128)(2,1)} %get-tuple-element.319.refs_0_, bf16[2,768,1024]{2,1,0:T(8,128)(2,1)} %get-tuple-element.320.refs_1_, ...), custom_call_target="tpu_custom_call" | custom-call | flops 1609142912 | tf_op jit(solution)/shard_map/weight_gradient/pallas_call | solution.py:1039
  609.7 8.3 multiply_reduce_fusion
  618.0 24.2 %attention_backward.1 = (f32[3072,128]{1,0:T(8,128)S(1)}, f32[1,3072]{1,0:T(1,128)S(1)}, f32[3072,128]{1,0:T(8,128)S(1)}, f32[3072,128]{1,0:T(8,128)S(1)}, f32[1,3072]{1,0:T(1,128)S(1)}, /*index=5*/f32[1,3072]{1,0:T(1,128)S(1)}) custom-call(s32[1]{0:T(128)S(6)} %copy.234.prefix_ref, bf16[3072,128]{1,0:T(8,128)(2,1)S(1)} %copy-done.47, ...), custom_call_target="tpu_custom_call" | custom-call | flops 5280000000 | tf_op jit(solution)/shard_map/attention_backward/pallas_call | solution.py:192
  648.0 9.2 %collective-permute-done.87.refs_2_ = bf16[512,1024]{1,0:T(8,128)(2,1)S(1)} collective-permute-done((bf16[512,1024]{1,0:T(8,128)(2,1)}, bf16[512,1024]{1,0:T(8,128)(2,1)S(1)}, u32[]{:S(2)}, u32[]{:S(2)}) %collective-permute-start.87) | collective-permute-done | bytes 1048608 | tf_op jit(solution)/shard_map/ppermute | solution.py:1077
  682.0 15.6 %projection_backward.1 = (bf16[3072,384]{1,0:T(8,128)(2,1)}, f32[2,128]{1,0:T(2,128)S(1)}, bf16[16,768,512]{2,1,0:T(8,128)(2,1)}) custom-call(f32[3072,128]{1,0:T(8,128)S(1)} %copy-done.21, f32[3072,128]{1,0:T(8,128)} %copy-done.22, f32[3072,128]{1,0:T(8,128)} %copy-done.23, f32[3072,384]{1,0:T(8,128)} %get-tuple-element.282.raw_ref, ...), custom_call_target="tpu_custom_call" | custom-call | flops 3409999872 | tf_op jit(solution)/shard_map/projection_backward/pallas_call | solution.py:1121
  749.3 15.7 %projection_weight_gradient.1 = (f32[4,3,512,128]{3,2,1,0:T(8,128)S(1)}, f32[1,2048]{1,0:T(1,128)S(1)}) custom-call(bf16[16,1024,512]{2,1,0:T(8,128)(2,1)} %place_blocks.14.x_ref.refs_1_.refs_3_.refs_4_.refs_7_.refs_8_, f32[1,2048]{1,0:T(1,128)S(1)} %copy-done.35, f32[1,3072]{1,0:T(1,128)S(1)} %get-tuple-element.482.inverse_ref, ...), custom_call_target="tpu_custom_call" | custom-call | flops 3300000000 | tf_op jit(solution)/shard_map/projection_weight_gradient/pallas_call | solution.py:591
  786.9 9.3 %weight_gradient.12 = f32[2,1024,2048]{2,1,0:T(8,128)} custom-call(s32[1]{0:T(128)} %bitcast.92.rank_ref, bf16[2,768,2048]{2,1,0:T(8,128)(2,1)} %get-tuple-element.494.left_ref, bf16[2,768,1024]{2,1,0:T(8,128)(2,1)} %get-tuple-element.319.refs_0_, bf16[2,768,1024]{2,1,0:T(8,128)(2,1)} %get-tuple-element.320.refs_1_, ...), custom_call_target="tpu_custom_call", output_to_operand_aliasing={{}: (8, {})} | custom-call | flops 1609142912 | tf_op jit(solution)/shard_map/weight_gradient/pallas_call | solution.py:1039
  826.1 11.6 %weight_gradient.13 = f32[2,512,2048]{2,1,0:T(8,128)} custom-call(s32[1]{0:T(128)} %bitcast.92.rank_ref, bf16[2,768,1024]{2,1,0:T(8,128)(2,1)} %get-tuple-element.513.left_ref, bf16[2,768,2048]{2,1,0:T(8,128)(2,1)} %bitcast.204, bf16[2,768,2048]{2,1,0:T(8,128)(2,1)} %bitcast.205, bf16[512,1024]{1,0:T(8,128)(2,1)S(1)} %copy-done.31, ...), custom_call_target="tpu_custom_call" | custom-call | flops 1609142912 | tf_op jit(solution)/shard_map/weight_gradient/pallas_call | solution.py:1039
  (563 shorter events, 474.5 us)
Async XLA Ops:
  13.5 38.9 %collective-permute-start.6 = (bf16[1024,512]{1,0:T(8,128)(2,1)}, bf16[1024,512]{1,0:T(8,128)(2,1)}, u32[]{:S(2)}, u32[]{:S(2)}) collective-permute-start(bf16[1024,512]{1,0:T(8,128)(2,1)} %pad_maximum_fusion.3.refs_0_), channel_id=1, source_target_pairs={{0,1},{1,0},{2,3},{3,2},{4,5},{5,4},{6,7},{7,6},{8,9},{9,8},{10,11... | collective-permute-start | bytes 3145736 | tf_op jit(solution)/shard_map/ppermute | solution.py:334
  18.2 50.9 %all-to-all-start = ((bf16[4,1280,128]{2,1,0:T(8,128)(2,1)}), bf16[4,1280,128]{2,1,0:T(8,128)(2,1)}, u32[]{:S(2)}, u32[]{:S(2)}) async-start(bf16[4,1280,128]{2,1,0:T(8,128)(2,1)} %pad_maximum_fusion.2), calls=%async_computation | async-start | bytes 2621440 | tf_op jit(solution)/shard_map/all_to_all | solution.py:506
  23.1 246.8 %all-gather.8.cloned.1.call-start = ((), (), s32[]{:S(2)}) async-start(), calls=%async_computation.6 | async-start | bytes 13369344 | tf_op jit(solution)/shard_map/all_gather | solution.py:1291
  42.4 37.5 %collective-permute-start.2 = (bf16[1024,512]{1,0:T(8,128)(2,1)}, bf16[1024,512]{1,0:T(8,128)(2,1)}, u32[]{:S(2)}, u32[]{:S(2)}) collective-permute-start(bf16[1024,512]{1,0:T(8,128)(2,1)} %collective-permute-done.refs_0_), channel_id=1, source_target_pairs={{0,4},{1,5},{4,8},{5,9},{8,12},{9,13},{12,14},{13,15},{14,10},{15,... | collective-permute-start | bytes 3145736 | tf_op jit(solution)/shard_map/ppermute | solution.py:340
  172.5 80.5 %collective-permute-start.24 = (bf16[8,256,512]{2,1,0:T(8,128)(2,1)}, bf16[8,256,512]{2,1,0:T(8,128)(2,1)}, u32[]{:S(2)}, u32[]{:S(2)}) collective-permute-start(bf16[8,256,512]{2,1,0:T(8,128)(2,1)} %bitcast.65), channel_id=1, source_target_pairs={{0,16},{16,0},{1,17},{17,1},{2,18},{18,2},{3,19},{19,3},{4,20},{20... | collective-permute-start | bytes 6291464 | tf_op jit(solution)/shard_map/ppermute | solution.py:1290
  269.9 39.9 %collective-permute-start.34 = (bf16[192,2048]{1,0:T(8,128)(2,1)S(1)}, bf16[192,2048]{1,0:T(8,128)(2,1)}, u32[]{:S(2)}, u32[]{:S(2)}) collective-permute-start(bf16[192,2048]{1,0:T(8,128)(2,1)S(1)} %get-tuple-element.292.refs_0_), channel_id=1, source_target_pairs={{0,1},{1,0},{2,3},{3,2},{4,5},{5,4},{6,7},{7,6},{8,9},{9,8},{10,11... | collective-permute-start | bytes 2359304 | tf_op jit(solution)/shard_map/ppermute | solution.py:334
  404.1 58.8 %collective-permute-start.56 = (bf16[512,1024]{1,0:T(8,128)(2,1)}, bf16[512,1024]{1,0:T(8,128)(2,1)}, u32[]{:S(2)}, u32[]{:S(2)}) collective-permute-start(bf16[512,1024]{1,0:T(8,128)(2,1)} %get-tuple-element.322), channel_id=1, source_target_pairs={{0,16},{16,0},{1,17},{17,1},{2,18},{18,2},{3,19},{19,3},{4,20},{20... | collective-permute-start | bytes 3145736 | tf_op jit(solution)/shard_map/ppermute | solution.py:1077
  425.1 37.7 %collective-permute-start.54 = (bf16[192,2048]{1,0:T(8,128)(2,1)}, bf16[192,2048]{1,0:T(8,128)(2,1)}, u32[]{:S(2)}, u32[]{:S(2)}) collective-permute-start(bf16[192,2048]{1,0:T(8,128)(2,1)} %get-tuple-element.365), channel_id=1, source_target_pairs={{0,1},{1,0},{2,3},{3,2},{4,5},{5,4},{6,7},{7,6},{8,9},{9,8},{10,11... | collective-permute-start | bytes 2359304 | tf_op jit(solution)/shard_map/ppermute | solution.py:394
  477.6 344.7 %all-gather.10.cloned.1.call-start = ((), (), s32[]{:S(2)}) async-start(), calls=%async_computation.7 | async-start | bytes 4325376 | tf_op jit(solution)/shard_map/all_gather | solution.py:1603
  499.5 47.8 %collective-permute-start.70 = (bf16[512,1024]{1,0:T(8,128)(2,1)}, bf16[512,1024]{1,0:T(8,128)(2,1)}, u32[]{:S(2)}, u32[]{:S(2)}) collective-permute-start(bf16[512,1024]{1,0:T(8,128)(2,1)} %copy-done.45), channel_id=1, source_target_pairs={{0,16},{16,0},{1,17},{17,1},{2,18},{18,2},{3,19},{19,3},{4,20},{20... | collective-permute-start | bytes 3145736 | tf_op jit(solution)/shard_map/ppermute | solution.py:1077
  551.0 40.4 %collective-permute-start.82 = (bf16[512,1024]{1,0:T(8,128)(2,1)S(1)}, bf16[512,1024]{1,0:T(8,128)(2,1)S(1)}, u32[]{:S(2)}, u32[]{:S(2)}) collective-permute-start(bf16[512,1024]{1,0:T(8,128)(2,1)S(1)} %copy-done.42), channel_id=1, source_target_pairs={{0,16},{16,0},{1,17},{17,1},{2,18},{18,2},{3,19},{19,3},{4,20},{20... | collective-permute-start | bytes 3145736 | tf_op jit(solution)/shard_map/ppermute | solution.py:1077
  596.4 49.4 %collective-permute-start.86 = (bf16[512,1024]{1,0:T(8,128)(2,1)}, bf16[512,1024]{1,0:T(8,128)(2,1)S(1)}, u32[]{:S(2)}, u32[]{:S(2)}) collective-permute-start(bf16[512,1024]{1,0:T(8,128)(2,1)} %get-tuple-element.393), channel_id=1, source_target_pairs={{0,16},{16,0},{1,17},{17,1},{2,18},{18,2},{3,19},{19,3},{4,20},{20... | collective-permute-start | bytes 3145736 | tf_op jit(solution)/shard_map/ppermute | solution.py:1077
  597.7 59.5 %collective-permute-start.87 = (bf16[512,1024]{1,0:T(8,128)(2,1)}, bf16[512,1024]{1,0:T(8,128)(2,1)S(1)}, u32[]{:S(2)}, u32[]{:S(2)}) collective-permute-start(bf16[512,1024]{1,0:T(8,128)(2,1)} %copy-done.43), channel_id=1, source_target_pairs={{0,16},{16,0},{1,17},{17,1},{2,18},{18,2},{3,19},{19,3},{4,20},{20... | collective-permute-start | bytes 3145736 | tf_op jit(solution)/shard_map/ppermute | solution.py:1077
  598.5 99.2 %collective-permute-start.94 = (bf16[512,1024]{1,0:T(8,128)(2,1)}, bf16[512,1024]{1,0:T(8,128)(2,1)}, u32[]{:S(2)}, u32[]{:S(2)}) collective-permute-start(bf16[512,1024]{1,0:T(8,128)(2,1)} %copy-done.39), channel_id=1, source_target_pairs={{0,16},{16,0},{1,17},{17,1},{2,18},{18,2},{3,19},{19,3},{4,20},{20... | collective-permute-start | bytes 3145736 | tf_op jit(solution)/shard_map/ppermute | solution.py:1077
  607.5 38.3 %collective-permute-start.84 = (bf16[192,2048]{1,0:T(8,128)(2,1)}, bf16[192,2048]{1,0:T(8,128)(2,1)S(1)}, u32[]{:S(2)}, u32[]{:S(2)}) collective-permute-start(bf16[192,2048]{1,0:T(8,128)(2,1)} %get-tuple-element.438), channel_id=1, source_target_pairs={{0,4},{1,5},{4,8},{5,9},{8,12},{9,13},{12,14},{13,15},{14,10},{15,... | collective-permute-start | bytes 2359304 | tf_op jit(solution)/shard_map/ppermute | solution.py:448
  608.6 37.2 %collective-permute-start.85 = (bf16[192,2048]{1,0:T(8,128)(2,1)}, bf16[192,2048]{1,0:T(8,128)(2,1)S(1)}, u32[]{:S(2)}, u32[]{:S(2)}) collective-permute-start(bf16[192,2048]{1,0:T(8,128)(2,1)} %get-tuple-element.439), channel_id=1, source_target_pairs={{0,2},{1,3},{4,0},{5,1},{8,4},{9,5},{12,8},{13,9},{14,12},{15,13},... | collective-permute-start | bytes 2359304 | tf_op jit(solution)/shard_map/ppermute | solution.py:449
  728.7 46.9 %collective-permute-start.114 = (bf16[512,1024]{1,0:T(8,128)(2,1)}, bf16[512,1024]{1,0:T(8,128)(2,1)}, u32[]{:S(2)}, u32[]{:S(2)}) collective-permute-start(bf16[512,1024]{1,0:T(8,128)(2,1)} %get-tuple-element.413), channel_id=1, source_target_pairs={{0,16},{16,0},{1,17},{17,1},{2,18},{18,2},{3,19},{19,3},{4,20},{20... | collective-permute-start | bytes 3145736 | tf_op jit(solution)/shard_map/ppermute | solution.py:1077
  729.4 48.3 %collective-permute-start.102 = (bf16[768,512]{1,0:T(8,128)(2,1)}, bf16[768,512]{1,0:T(8,128)(2,1)}, u32[]{:S(2)}, u32[]{:S(2)}) collective-permute-start(bf16[768,512]{1,0:T(8,128)(2,1)} %get-tuple-element.584), channel_id=1, source_target_pairs={{0,1},{1,0},{2,3},{3,2},{4,5},{5,4},{6,7},{7,6},{8,9},{9,8},{10,11... | collective-permute-start | bytes 2359304 | tf_op jit(solution)/shard_map/ppermute | solution.py:394
  738.2 39.6 %collective-permute-start.103 = (bf16[768,512]{1,0:T(8,128)(2,1)}, bf16[768,512]{1,0:T(8,128)(2,1)}, u32[]{:S(2)}, u32[]{:S(2)}) collective-permute-start(bf16[768,512]{1,0:T(8,128)(2,1)} %get-tuple-element.583), channel_id=1, source_target_pairs={{0,1},{1,0},{2,3},{3,2},{4,5},{5,4},{6,7},{7,6},{8,9},{9,8},{10,11... | collective-permute-start | bytes 2359304 | tf_op jit(solution)/shard_map/ppermute | solution.py:394
  739.5 38.8 %collective-permute-start.100 = (bf16[768,512]{1,0:T(8,128)(2,1)}, bf16[768,512]{1,0:T(8,128)(2,1)}, u32[]{:S(2)}, u32[]{:S(2)}) collective-permute-start(bf16[768,512]{1,0:T(8,128)(2,1)} %get-tuple-element.480), channel_id=1, source_target_pairs={{0,4},{1,5},{4,8},{5,9},{8,12},{9,13},{12,14},{13,15},{14,10},{15,... | collective-permute-start | bytes 2359304 | tf_op jit(solution)/shard_map/ppermute | solution.py:448
  739.8 38.5 %collective-permute-start.101 = (bf16[768,512]{1,0:T(8,128)(2,1)}, bf16[768,512]{1,0:T(8,128)(2,1)}, u32[]{:S(2)}, u32[]{:S(2)}) collective-permute-start(bf16[768,512]{1,0:T(8,128)(2,1)} %get-tuple-element.481), channel_id=1, source_target_pairs={{0,2},{1,3},{4,0},{5,1},{8,4},{9,5},{12,8},{13,9},{14,12},{15,13},... | collective-permute-start | bytes 2359304 | tf_op jit(solution)/shard_map/ppermute | solution.py:449
  745.7 94.0 %all-gather.12.cloned.1.call-start = ((), (), s32[]{:S(2)}) async-start(), calls=%async_computation.8 | async-start | bytes 1081344 | tf_op jit(solution)/shard_map/all_gather | solution.py:1602
  769.6 45.6 %all-to-all-start.4 = ((bf16[192,4,512]{2,0,1:T(8,128)(2,1)}), bf16[192,4,512]{2,0,1:T(8,128)(2,1)S(1)}, u32[]{:S(2)}, u32[]{:S(2)}) async-start(bf16[192,4,512]{2,0,1:T(8,128)(2,1)} %bitcast.247), calls=%async_computation.4 | async-start | bytes 1572864 | tf_op jit(solution)/shard_map/all_to_all | solution.py:1555
  796.2 45.5 %collective-permute-start.115 = (bf16[768,512]{1,0:T(8,128)(2,1)}, bf16[768,512]{1,0:T(8,128)(2,1)}, u32[]{:S(2)}, u32[]{:S(2)}) collective-permute-start(bf16[768,512]{1,0:T(8,128)(2,1)} %get-tuple-element.580), channel_id=1, source_target_pairs={{0,1},{1,0},{2,3},{3,2},{4,5},{5,4},{6,7},{7,6},{8,9},{9,8},{10,11... | collective-permute-start | bytes 2359304 | tf_op jit(solution)/shard_map/ppermute | solution.py:394
  (183 other events, 2409.5 us)
Sparse Core Ops, SparseCore 0:
  142.8 115.8 all-gather.7
  594.5 71.6 all-gather.9
  767.5 57.6 all-gather.11

commit v4 on v3

--- a/solution.py
+++ b/solution.py
@@ -17,7 +17,7 @@
 BLOCKS = ("col", "row")
 LOG2E = math.log2(math.e)
 MASKED = -1e30
-COST_SHARE = 0.2
+COST_SHARE = 0.1
 
 norm_epsilon = 1e-05
 rope_base = 10000.0
@@ -795,7 +795,8 @@
         rest = rest[5:]
     slot_ref, hidden_ref, grad_gate_ref, grad_up_ref, scale_ref = rest[:5]
     feat_sums = rest[5 : 5 + count]
-    probs_ref, in_acc, in_all = rest[5 + count :]
+    probs_ref, later_ref, in_acc, in_all = rest[5 + count :]
+    rows = slot_ref.shape[1]
     e, f = pl.program_id(0), pl.program_id(1)
     last_expert = e == pl.num_programs(0) - 1
     last_tile = f == pl.num_programs(1) - 1
@@ -809,13 +810,21 @@
             logits = dot_nt(router_ref[...], feats[k][...])
             raised = jnp.exp(logits - jnp.max(logits, axis=0, keepdims=True))
             probs_ref[k] = raised / jnp.sum(raised, axis=0, keepdims=True)
+            picked = dot_nn(hits_ref[ids_ref[k]], feats[k][...]).astype(bf16)
+            slot_ref[0, pl.ds(k * capacity, capacity), :] = picked[:capacity]
+            for j in range(1, picked.shape[0] // capacity):
+                at = pl.ds((j - 1) * rows + k * capacity, capacity)
+                later_ref[at, :] = picked[j * capacity : (j + 1) * capacity]
+
+    @pl.when((e > 0) & (f == 0))
+    def _():
+        slot_ref[0] = later_ref[pl.ds(pl.multiple_of((e - 1) * rows, 16), rows), :]
 
     @pl.when(f == 0)
     def _():
         for k in range(count):
             at = pl.ds(k * capacity, capacity)
             hits = hits_ref[ids_ref[k], own_slots, :]
-            slot_ref[0, at, :] = dot_nn(hits, feats[k][...]).astype(bf16)
             probs = probs_ref[k]
             rank = lax.broadcasted_iota(jnp.int32, probs.shape, 0)
             gate = jnp.sum(jnp.where(rank == chosen, probs, 0.0), axis=0, keepdims=True)
@@ -897,6 +906,7 @@
             out_specs=[wide, narrow, narrow, narrow, thin] + [whole((tok_rows, D))] * count,
             scratch_shapes=[
                 pltpu.VMEM((count, router_flip.shape[0], tok_rows), f32),
+                pltpu.VMEM((max(experts - 1, 1) * rows, D), bf16),
                 pltpu.VMEM((rows, D), f32),
                 pltpu.VMEM((count, experts * capacity, D), bf16),
             ],
@@ -1299,7 +1309,7 @@
     )
 
     query_rows = max(seq_len // 6, 128)
-    attn_head, lse = attention(query_low, key_low, value_flip, prefix_len, query_rows)
+    attn_head, lse = attention(query_low, key_low, value_flip, prefix_len, 2 * query_rows)
     attn_tokens = exchange(attn_head.reshape(group, tok_rows, HD), BLOCKS)
     weight_sets = [(x_blocks, half_place)] * ring.cores
     if paired:
@@ -1495,7 +1505,7 @@
     )
     head_grads = [grad_query, grad_key, grad_value]
     dots = jnp.concatenate([dot_query, dot_key, dot_value], axis=0)
-    dots, = taking(2, *moes.tie(dots))
+    dots, = taking(1, *moes.tie(dots))
     moes.ready()
     dots, = moes.tie(dots)
     dots = ring.small_sum(dots)
@@ -1516,7 +1526,7 @@
         return first_parts[distance]
 
     first_parts = {}
-    grad_first_blocks, grad_qkv = taking(1, *moes.tie(grad_first_blocks, grad_qkv))
+    grad_first_blocks, grad_qkv = taking(2, *moes.tie(grad_first_blocks, grad_qkv))
     first_far = block_sum(first_part(ring.size // 2))
     moes.ready()
     first_far, grad_first_blocks = moes.tie(first_far, grad_first_blocks)
@@ -1527,8 +1537,7 @@
     moes.move()
     output_term = dot(attn_head.T, branch_all.reshape(seq_len, D))
     output_term = output_term.astype(bf16).reshape(HD, rows, row_width).transpose(1, 0, 2)
-    output_term, = taking(1, *moes.tie(*ahead_tie(firsts, first_parts, output_term)))
-    moe_terms = moes.total()
+    output_term, = taking(1, *ahead_tie(firsts, first_parts, output_term))
     firsts.ready()
     grad_qkv, slot_rows = firsts.tie(grad_qkv, slot_rows)
     firsts.move()
@@ -1540,7 +1549,8 @@
         lambda rank: lax.dynamic_slice_in_dim(qkv_term, rank * qkv_rows, qkv_rows, 2)
     )
     output_sum = exchange(output_term, "row").reshape(col_width, row_width)
-    qkv_term, = taking(1, *ahead_tie(firsts, first_parts, qkv_term))
+    qkv_term, = taking(1, *moes.tie(*ahead_tie(firsts, first_parts, qkv_term)))
+    moe_terms = moes.total()
     firsts.ready()
     slot_rows, = firsts.tie(slot_rows)
     firsts.move()

time: 877 us -> 865 us (0.986)
  waiting for transfers between devices: 178 us -> 168 us
    ppermute x12, waiting for transfers between devices: 20.9 us -> 8.54 us  [weight_grad_sends(): more = [lax.ppermute(part, 'dp', onward) for part in parts]]
    ppermute x12, starting transfers between devices: 10.2 us -> 21.5 us  [move(): lax.ppermute(forth, PLANE, self.ring.clockwise)]
  transfers between devices with their start and end apart: 125 -> 125, of which waited for: 50 -> 51; matrix products, arithmetic and copies ran while one was open for 15% -> 15% of each run, Pallas kernels for 35% -> 35%
where the time goes in v4:
time: 865 us; the launch traced here: 852 us
  Pallas kernels  333 us (38%)
  waiting for transfers between devices  168 us (19%)
  starting transfers between devices  122 us (14%)
  local copies, waits for them, and re-layouts  76.7 us (9%)
  other arithmetic  51.6 us (6%)
  matrix products  43 us (5%)
  blocking collectives  40.9 us (5%)
  between operations  16.6 us (2%)
    pallas_call x2, Pallas kernels, run_experts(): pl.pallas_call(functools.partial(experts_kernel, count, first), grid_spec...  61.7 us
    pallas_call x7, Pallas kernels, weight_grad(): pl.pallas_call(functools.partial(weight_grad_kernel, sides, len(more), pi...  56.8 us
    pallas_call x10, Pallas kernels, place_blocks(): pl.pallas_call(kernel, grid_spec=pltpu.PrefetchScalarGridSpec(num_scalar_...  44.8 us
    all_to_all x1, blocking collectives, exchange(): return lax.all_to_all(pieces, axes, split_axis=0, concat_axis=0, tiled=True)  40.9 us
    pallas_call x9, Pallas kernels, step_sum(): pl.pallas_call(functools.partial(step_sum_kernel, (len(ahead), len(behind...  38.1 us
    unnamed x168, local copies, waits for them, and re-layouts  36.4 us
    ppermute x9, waiting for transfers between devices, gather_steps(): forth = lax.ppermute(forth, PLANE, self.clockwise)  32.3 us
    dot_general x3, matrix products, einsum(): return jnp.einsum(spec, a, b, preferred_element_type=f32)  26.9 us
  transfers between devices with their start and end apart: 125, of which 51 were waited for; matrix products, arithmetic and copies ran while one was open for 15% of the time, Pallas kernels for 35%

profile of v4, /device:TPU:0, one launch (start us, length us, event | category | flops | bytes accessed | tf_op | source)
XLA Modules:
  0.0 852.1 jit_solution(6678176820351453985)
XLA Ops:
  56.2 12.9 %all-to-all-done = bf16[4,1280,128]{2,1,0:T(8,128)(2,1)} async-done(((bf16[4,1280,128]{2,1,0:T(8,128)(2,1)}), bf16[4,1280,128]{2,1,0:T(8,128)(2,1)}, u32[]{:S(2)}, u32[]{:S(2)}) %all-to-all-start) | async-done | bytes 1310752 | tf_op jit(solution)/shard_map/all_to_all | solution.py:506
  82.5 8.6 %collective-permute-start.10 = (bf16[1024,512]{1,0:T(8,128)(2,1)}, bf16[1024,512]{1,0:T(8,128)(2,1)}, u32[]{:S(2)}, u32[]{:S(2)}) collective-permute-start(bf16[1024,512]{1,0:T(8,128)(2,1)} %collective-permute-done.2.refs_0_), channel_id=1, source_target_pairs={{0,4},{1,5},{4,8},{5,9},{8,12},{9,13},{12,14},{13,15},{14,10},{15,... | collective-permute-start | bytes 3145736 | tf_op jit(solution)/shard_map/ppermute | solution.py:340
  98.5 15.6 %collective-permute-done.10.refs_0_ = bf16[1024,512]{1,0:T(8,128)(2,1)} collective-permute-done((bf16[1024,512]{1,0:T(8,128)(2,1)}, bf16[1024,512]{1,0:T(8,128)(2,1)}, u32[]{:S(2)}, u32[]{:S(2)}) %collective-permute-start.10) | collective-permute-done | bytes 1048608 | tf_op jit(solution)/shard_map/ppermute | solution.py:340
  123.3 10.9 %collective-permute-done.15 = bf16[512,512]{1,0:T(8,128)(2,1)S(1)} collective-permute-done((bf16[512,512]{1,0:T(8,128)(2,1)S(1)}, bf16[512,512]{1,0:T(8,128)(2,1)S(1)}, u32[]{:S(2)}, u32[]{:S(2)}) %collective-permute-start.15) | collective-permute-done | bytes 524320 | tf_op jit(solution)/shard_map/ppermute | solution.py:348
  157.5 13.9 %norm_and_project.1 = (f32[3072,384]{1,0:T(8,128)}, f32[1,3072]{1,0:T(1,128)S(1)}, f32[2,3072]{1,0:T(2,128)S(1)}) custom-call(bf16[16,1024,512]{2,1,0:T(8,128)(2,1)} %place_blocks.14.x_ref.refs_1_.refs_3_.refs_4_.refs_7_.refs_8_, f32[1,2048]{1,0:T(1,128)S(1)} %get-tuple-element.592.gain_ref, bf16[2048,384]{1,0:T(8,128)(2,1)S(1)} %bitcast.206), custom_call_target="tpu_custom_call" | custom-call | flops 1540000000 | tf_op jit(solution)/shard_map/norm_and_project/pallas_call | solution.py:533
  196.9 13.1 %attention_forward.1 = (bf16[3072,128]{1,0:T(8,128)(2,1)S(1)}, f32[1,3072]{1,0:T(1,128)S(1)}) custom-call(s32[1]{0:T(128)S(6)} %copy.234.prefix_ref, bf16[3072,128]{1,0:T(8,128)(2,1)S(1)} %copy-done.45, bf16[3072,128]{1,0:T(8,128)(2,1)S(1)} %copy-done.47, bf16[128,3072]{1,0:T(8,128)(2,1)S(1)} %copy-done.51), custom_call_target="tpu_custom_call" | custom-call | flops 1870000000 | tf_op jit(solution)/shard_map/attention_forward/pallas_call | solution.py:105
  210.9 40.9 %all_to_all.44.refs_0_ = bf16[16,192,128]{2,1,0:T(8,128)(2,1)S(1)} all-to-all(bf16[16,192,128]{2,1,0:T(8,128)(2,1)S(1)} %bitcast.212), channel_id=1, replica_groups=mesh['dp'=2,'row'=4,'col'=4] {'col','row'}, dimensions={0} | all-to-all | bytes 1572864 | tf_op jit(solution)/shard_map/all_to_all | solution.py:506
  267.9 14.3 %cotangent_to_slots.1.up_ref = bf16[2,16,48,2048]{3,2,1,0:T(8,128)(2,1)} custom-call(bf16[16,96,192]{2,1,0:T(8,128)(2,1)} %copy.178.hits_ref.refs_16_, bf16[16,768,512]{2,1,0:T(8,128)(2,1)} %bitcast.238), custom_call_target="tpu_custom_call" | custom-call | flops 1540000000 | tf_op jit(solution)/shard_map/cotangent_to_slots/pallas_call | solution.py:775
  287.2 12.9 %fusion.26 = f32[2,768,1024]{2,1,0:T(8,128)} fusion(bf16[2,768,2048]{2,1,0:T(8,128)(2,1)} %bitcast.240, bf16[2,1024,2048]{2,1,0:T(8,128)(2,1)} %param.18), kind=kOutput, calls=%fused_computation.113 | convolution fusion | flops 6442450944 | bytes 20971520 | tf_op jit(solution)/shard_map/end,efd->enf/dot_general | solution.py:1162
  308.9 30.7 %experts.2 = (bf16[2,768,2048]{2,1,0:T(8,128)(2,1)}, bf16[2,768,1024]{2,1,0:T(8,128)(2,1)}, bf16[2,768,1024]{2,1,0:T(8,128)(2,1)}, bf16[2,768,1024]{2,1,0:T(8,12...) custom-call(s32[9]{0:T(128)} %stack.304.ids_ref, ...), custom_call_target="tpu_custom_call" | custom-call | flops 3190000128 | tf_op jit(solution)/shard_map/experts/pallas_call | solution.py:900
  354.2 31.0 %experts.3 = (bf16[2,768,2048]{2,1,0:T(8,128)(2,1)}, bf16[2,768,1024]{2,1,0:T(8,128)(2,1)}, bf16[2,768,1024]{2,1,0:T(8,128)(2,1)}, bf16[2,768,1024]{2,1,0:T(8,12...) custom-call(s32[9]{0:T(128)} %stack.260.ids_ref, ...), custom_call_target="tpu_custom_call", output_to_operand_aliasing={{0}: (22, {}), {1}: (23, {}), {2}: (24, {}), {3}: (25, {}),... | custom-call | flops 3190000128 | tf_op jit(solution)/shard_map/experts/pallas_call | solution.py:900
  391.3 7.9 weight_gradient.7
  411.9 11.9 %convolution_convert_fusion = bf16[2,768,2048]{2,1,0:T(8,128)(2,1)} fusion(bf16[2,768,1024]{2,1,0:T(8,128)(2,1)S(1)} %copy-done.3, bf16[2,1024,2048]{2,1,0:T(8,128)(2,1)} %param.18), kind=kOutput, calls=%fused_computation.2 | convolution fusion | flops 6445596672 | bytes 17825792 | tf_op jit(solution)/shard_map/enf,efd->end/dot_general | solution.py:1162
  441.1 18.3 %experts_combine.1 = (f32[16,2,192]{2,1,0:T(2,128)}, bf16[2,16,48,2048]{3,2,1,0:T(8,128)(2,1)S(1)}, bf16[8,192,2048]{2,1,0:T(8,128)(2,1)}, bf16[8,192,2048]{2,1,0:T(8,128)(2,1)}) custom-call(s32[16]{0:T(128)S(1)} %stack.305.ids_ref, s32[64]{0:T(128)S(1)} %copy-done.37, bf16[2,16,48,2048]{3,2,1,0:T(8,128)(2,1)} %bitcast.244, ...), custom_call_target="tpu_custom_call" | custom-call | flops 1980000000 | tf_op jit(solution)/shard_map/experts_combine/pallas_call | solution.py:965
  478.0 8.0 weight_gradient.8
  552.1 10.0 %weight_gradient.11.refs_6_ = f32[2,1024,2048]{2,1,0:T(8,128)} custom-call(s32[1]{0:T(128)} %bitcast.92.rank_ref, bf16[2,768,2048]{2,1,0:T(8,128)(2,1)} %get-tuple-element.493.left_ref, bf16[2,768,1024]{2,1,0:T(8,128)(2,1)} %get-tuple-element.318.refs_0_, bf16[2,768,1024]{2,1,0:T(8,128)(2,1)} %get-tuple-element.319.refs_1_, ...), custom_call_target="tpu_custom_call" | custom-call | flops 804571456 | tf_op jit(solution)/shard_map/weight_gradient/pallas_call | solution.py:1049
  575.1 7.9 collective-permute-done.77
  609.8 8.2 multiply_reduce_fusion
  618.1 22.6 %attention_backward.1 = (f32[3072,128]{1,0:T(8,128)S(1)}, f32[1,3072]{1,0:T(1,128)S(1)}, f32[3072,128]{1,0:T(8,128)S(1)}, f32[3072,128]{1,0:T(8,128)S(1)}, f32[1,3072]{1,0:T(1,128)S(1)}, /*index=5*/f32[1,3072]{1,0:T(1,128)S(1)}) custom-call(s32[1]{0:T(128)S(6)} %copy.234.prefix_ref, bf16[3072,128]{1,0:T(8,128)(2,1)S(1)} %copy-done.46, ...), custom_call_target="tpu_custom_call" | custom-call | flops 2640000000 | tf_op jit(solution)/shard_map/attention_backward/pallas_call | solution.py:192
  671.1 15.6 %projection_backward.1 = (bf16[3072,384]{1,0:T(8,128)(2,1)}, f32[2,128]{1,0:T(2,128)S(1)}, bf16[16,768,512]{2,1,0:T(8,128)(2,1)}) custom-call(f32[3072,128]{1,0:T(8,128)S(1)} %copy-done.21, f32[3072,128]{1,0:T(8,128)} %copy-done.22, f32[3072,128]{1,0:T(8,128)} %copy-done.23, f32[3072,384]{1,0:T(8,128)} %get-tuple-element.281.raw_ref, ...), custom_call_target="tpu_custom_call" | custom-call | flops 1704999936 | tf_op jit(solution)/shard_map/projection_backward/pallas_call | solution.py:1131
  734.7 15.6 %projection_weight_gradient.1 = (f32[4,3,512,128]{3,2,1,0:T(8,128)S(1)}, f32[1,2048]{1,0:T(1,128)S(1)}) custom-call(bf16[16,1024,512]{2,1,0:T(8,128)(2,1)} %place_blocks.14.x_ref.refs_1_.refs_3_.refs_4_.refs_7_.refs_8_, f32[1,2048]{1,0:T(1,128)S(1)} %copy-done.35, f32[1,3072]{1,0:T(1,128)S(1)} %get-tuple-element.481.inverse_ref, ...), custom_call_target="tpu_custom_call" | custom-call | flops 1650000000 | tf_op jit(solution)/shard_map/projection_weight_gradient/pallas_call | solution.py:591
  769.3 9.3 %weight_gradient.12 = f32[2,1024,2048]{2,1,0:T(8,128)} custom-call(s32[1]{0:T(128)} %bitcast.92.rank_ref, bf16[2,768,2048]{2,1,0:T(8,128)(2,1)} %get-tuple-element.493.left_ref, bf16[2,768,1024]{2,1,0:T(8,128)(2,1)} %get-tuple-element.318.refs_0_, bf16[2,768,1024]{2,1,0:T(8,128)(2,1)} %get-tuple-element.319.refs_1_, ...), custom_call_target="tpu_custom_call", output_to_operand_aliasing={{}: (8, {})} | custom-call | flops 804571456 | tf_op jit(solution)/shard_map/weight_gradient/pallas_call | solution.py:1049
  780.9 8.3 collective-permute-done.104.refs_4_
  812.3 11.7 %weight_gradient.13 = f32[2,512,2048]{2,1,0:T(8,128)} custom-call(s32[1]{0:T(128)} %bitcast.92.rank_ref, bf16[2,768,1024]{2,1,0:T(8,128)(2,1)} %get-tuple-element.509.left_ref, bf16[2,768,2048]{2,1,0:T(8,128)(2,1)} %bitcast.204, bf16[2,768,2048]{2,1,0:T(8,128)(2,1)} %bitcast.205, bf16[512,1024]{1,0:T(8,128)(2,1)S(1)} %copy-done.31, ...), custom_call_target="tpu_custom_call" | custom-call | flops 804571456 | tf_op jit(solution)/shard_map/weight_gradient/pallas_call | solution.py:1049
  (563 shorter events, 475.2 us)
Async XLA Ops:
  13.5 38.9 %collective-permute-start.6 = (bf16[1024,512]{1,0:T(8,128)(2,1)}, bf16[1024,512]{1,0:T(8,128)(2,1)}, u32[]{:S(2)}, u32[]{:S(2)}) collective-permute-start(bf16[1024,512]{1,0:T(8,128)(2,1)} %pad_maximum_fusion.3.refs_0_), channel_id=1, source_target_pairs={{0,1},{1,0},{2,3},{3,2},{4,5},{5,4},{6,7},{7,6},{8,9},{9,8},{10,11... | collective-permute-start | bytes 3145736 | tf_op jit(solution)/shard_map/ppermute | solution.py:334
  18.2 50.9 %all-to-all-start = ((bf16[4,1280,128]{2,1,0:T(8,128)(2,1)}), bf16[4,1280,128]{2,1,0:T(8,128)(2,1)}, u32[]{:S(2)}, u32[]{:S(2)}) async-start(bf16[4,1280,128]{2,1,0:T(8,128)(2,1)} %pad_maximum_fusion.2), calls=%async_computation | async-start | bytes 2621440 | tf_op jit(solution)/shard_map/all_to_all | solution.py:506
  23.1 244.8 %all-gather.8.cloned.1.call-start = ((), (), s32[]{:S(2)}) async-start(), calls=%async_computation.6 | async-start | bytes 13369344 | tf_op jit(solution)/shard_map/all_gather | solution.py:1301
  40.8 39.0 %collective-permute-start.2 = (bf16[1024,512]{1,0:T(8,128)(2,1)}, bf16[1024,512]{1,0:T(8,128)(2,1)}, u32[]{:S(2)}, u32[]{:S(2)}) collective-permute-start(bf16[1024,512]{1,0:T(8,128)(2,1)} %collective-permute-done.refs_0_), channel_id=1, source_target_pairs={{0,4},{1,5},{4,8},{5,9},{8,12},{9,13},{12,14},{13,15},{14,10},{15,... | collective-permute-start | bytes 3145736 | tf_op jit(solution)/shard_map/ppermute | solution.py:340
  47.5 34.5 %collective-permute-start.3 = (bf16[1024,512]{1,0:T(8,128)(2,1)}, bf16[1024,512]{1,0:T(8,128)(2,1)}, u32[]{:S(2)}, u32[]{:S(2)}) collective-permute-start(bf16[1024,512]{1,0:T(8,128)(2,1)} %collective-permute-done.1.refs_2_), channel_id=1, source_target_pairs={{0,2},{1,3},{4,0},{5,1},{8,4},{9,5},{12,8},{13,9},{14,12},{15,13},... | collective-permute-start | bytes 3145736 | tf_op jit(solution)/shard_map/ppermute | solution.py:341
  152.2 99.7 %collective-permute-start.24 = (bf16[8,256,512]{2,1,0:T(8,128)(2,1)}, bf16[8,256,512]{2,1,0:T(8,128)(2,1)}, u32[]{:S(2)}, u32[]{:S(2)}) collective-permute-start(bf16[8,256,512]{2,1,0:T(8,128)(2,1)} %bitcast.65), channel_id=1, source_target_pairs={{0,16},{16,0},{1,17},{17,1},{2,18},{18,2},{3,19},{19,3},{4,20},{20... | collective-permute-start | bytes 6291464 | tf_op jit(solution)/shard_map/ppermute | solution.py:1300
  267.8 41.1 %collective-permute-start.34 = (bf16[192,2048]{1,0:T(8,128)(2,1)S(1)}, bf16[192,2048]{1,0:T(8,128)(2,1)}, u32[]{:S(2)}, u32[]{:S(2)}) collective-permute-start(bf16[192,2048]{1,0:T(8,128)(2,1)S(1)} %get-tuple-element.291.refs_0_), channel_id=1, source_target_pairs={{0,1},{1,0},{2,3},{3,2},{4,5},{5,4},{6,7},{7,6},{8,9},{9,8},{10,11... | collective-permute-start | bytes 2359304 | tf_op jit(solution)/shard_map/ppermute | solution.py:334
  403.8 58.4 %collective-permute-start.56 = (bf16[512,1024]{1,0:T(8,128)(2,1)}, bf16[512,1024]{1,0:T(8,128)(2,1)}, u32[]{:S(2)}, u32[]{:S(2)}) collective-permute-start(bf16[512,1024]{1,0:T(8,128)(2,1)} %get-tuple-element.321), channel_id=1, source_target_pairs={{0,16},{16,0},{1,17},{17,1},{2,18},{18,2},{3,19},{19,3},{4,20},{20... | collective-permute-start | bytes 3145736 | tf_op jit(solution)/shard_map/ppermute | solution.py:1087
  423.8 38.4 %collective-permute-start.54 = (bf16[192,2048]{1,0:T(8,128)(2,1)}, bf16[192,2048]{1,0:T(8,128)(2,1)}, u32[]{:S(2)}, u32[]{:S(2)}) collective-permute-start(bf16[192,2048]{1,0:T(8,128)(2,1)} %get-tuple-element.364), channel_id=1, source_target_pairs={{0,1},{1,0},{2,3},{3,2},{4,5},{5,4},{6,7},{7,6},{8,9},{9,8},{10,11... | collective-permute-start | bytes 2359304 | tf_op jit(solution)/shard_map/ppermute | solution.py:394
  466.3 34.4 %collective-permute-start.59 = (bf16[8,192,2048]{2,1,0:T(8,128)(2,1)}, bf16[8,192,2048]{2,1,0:T(8,128)(2,1)}, u32[]{:S(2)}, u32[]{:S(2)}) collective-permute-start(bf16[8,192,2048]{2,1,0:T(8,128)(2,1)} %get-tuple-element.387), channel_id=1, source_target_pairs={{0,1},{1,0},{2,3},{3,2},{4,5},{5,4},{6,7},{7,6},{8,9},{9,8},{10,11... | collective-permute-start | bytes 18874376 | tf_op jit(solution)/shard_map/ppermute | solution.py:1438
  477.9 330.6 %all-gather.10.cloned.1.call-start = ((), (), s32[]{:S(2)}) async-start(), calls=%async_computation.7 | async-start | bytes 4325376 | tf_op jit(solution)/shard_map/all_gather | solution.py:1613
  499.0 47.1 %collective-permute-start.70 = (bf16[512,1024]{1,0:T(8,128)(2,1)}, bf16[512,1024]{1,0:T(8,128)(2,1)}, u32[]{:S(2)}, u32[]{:S(2)}) collective-permute-start(bf16[512,1024]{1,0:T(8,128)(2,1)} %copy-done.44), channel_id=1, source_target_pairs={{0,16},{16,0},{1,17},{17,1},{2,18},{18,2},{3,19},{19,3},{4,20},{20... | collective-permute-start | bytes 3145736 | tf_op jit(solution)/shard_map/ppermute | solution.py:1087
  551.7 41.0 %collective-permute-start.82 = (bf16[512,1024]{1,0:T(8,128)(2,1)S(1)}, bf16[512,1024]{1,0:T(8,128)(2,1)S(1)}, u32[]{:S(2)}, u32[]{:S(2)}) collective-permute-start(bf16[512,1024]{1,0:T(8,128)(2,1)S(1)} %copy-done.42), channel_id=1, source_target_pairs={{0,16},{16,0},{1,17},{17,1},{2,18},{18,2},{3,19},{19,3},{4,20},{20... | collective-permute-start | bytes 3145736 | tf_op jit(solution)/shard_map/ppermute | solution.py:1087
  597.5 48.6 %collective-permute-start.86 = (bf16[512,1024]{1,0:T(8,128)(2,1)}, bf16[512,1024]{1,0:T(8,128)(2,1)S(1)}, u32[]{:S(2)}, u32[]{:S(2)}) collective-permute-start(bf16[512,1024]{1,0:T(8,128)(2,1)} %get-tuple-element.392), channel_id=1, source_target_pairs={{0,16},{16,0},{1,17},{17,1},{2,18},{18,2},{3,19},{19,3},{4,20},{20... | collective-permute-start | bytes 3145736 | tf_op jit(solution)/shard_map/ppermute | solution.py:1087
  597.9 88.9 %collective-permute-start.93 = (bf16[512,1024]{1,0:T(8,128)(2,1)}, bf16[512,1024]{1,0:T(8,128)(2,1)S(1)}, u32[]{:S(2)}, u32[]{:S(2)}) collective-permute-start(bf16[512,1024]{1,0:T(8,128)(2,1)} %copy-done.39), channel_id=1, source_target_pairs={{0,16},{16,0},{1,17},{17,1},{2,18},{18,2},{3,19},{19,3},{4,20},{20... | collective-permute-start | bytes 3145736 | tf_op jit(solution)/shard_map/ppermute | solution.py:1087
  599.5 87.3 %collective-permute-start.94 = (bf16[512,1024]{1,0:T(8,128)(2,1)}, bf16[512,1024]{1,0:T(8,128)(2,1)}, u32[]{:S(2)}, u32[]{:S(2)}) collective-permute-start(bf16[512,1024]{1,0:T(8,128)(2,1)} %copy-done.38), channel_id=1, source_target_pairs={{0,16},{16,0},{1,17},{17,1},{2,18},{18,2},{3,19},{19,3},{4,20},{20... | collective-permute-start | bytes 3145736 | tf_op jit(solution)/shard_map/ppermute | solution.py:1087
  607.6 36.7 %collective-permute-start.84 = (bf16[192,2048]{1,0:T(8,128)(2,1)}, bf16[192,2048]{1,0:T(8,128)(2,1)S(1)}, u32[]{:S(2)}, u32[]{:S(2)}) collective-permute-start(bf16[192,2048]{1,0:T(8,128)(2,1)} %get-tuple-element.437), channel_id=1, source_target_pairs={{0,4},{1,5},{4,8},{5,9},{8,12},{9,13},{12,14},{13,15},{14,10},{15,... | collective-permute-start | bytes 2359304 | tf_op jit(solution)/shard_map/ppermute | solution.py:448
  609.0 35.3 %collective-permute-start.85 = (bf16[192,2048]{1,0:T(8,128)(2,1)}, bf16[192,2048]{1,0:T(8,128)(2,1)S(1)}, u32[]{:S(2)}, u32[]{:S(2)}) collective-permute-start(bf16[192,2048]{1,0:T(8,128)(2,1)} %get-tuple-element.438), channel_id=1, source_target_pairs={{0,2},{1,3},{4,0},{5,1},{8,4},{9,5},{12,8},{13,9},{14,12},{15,13},... | collective-permute-start | bytes 2359304 | tf_op jit(solution)/shard_map/ppermute | solution.py:449
  717.9 48.6 %collective-permute-start.112 = (bf16[512,1024]{1,0:T(8,128)(2,1)}, bf16[512,1024]{1,0:T(8,128)(2,1)}, u32[]{:S(2)}, u32[]{:S(2)}) collective-permute-start(bf16[512,1024]{1,0:T(8,128)(2,1)} %get-tuple-element.412), channel_id=1, source_target_pairs={{0,16},{16,0},{1,17},{17,1},{2,18},{18,2},{3,19},{19,3},{4,20},{20... | collective-permute-start | bytes 3145736 | tf_op jit(solution)/shard_map/ppermute | solution.py:1087
  724.9 34.8 %collective-permute-start.103 = (bf16[768,512]{1,0:T(8,128)(2,1)}, bf16[768,512]{1,0:T(8,128)(2,1)}, u32[]{:S(2)}, u32[]{:S(2)}) collective-permute-start(bf16[768,512]{1,0:T(8,128)(2,1)} %get-tuple-element.581), channel_id=1, source_target_pairs={{0,1},{1,0},{2,3},{3,2},{4,5},{5,4},{6,7},{7,6},{8,9},{9,8},{10,11... | collective-permute-start | bytes 2359304 | tf_op jit(solution)/shard_map/ppermute | solution.py:394
  753.9 47.9 %all-to-all-start.4 = ((bf16[192,4,512]{2,0,1:T(8,128)(2,1)}), bf16[192,4,512]{2,0,1:T(8,128)(2,1)S(1)}, u32[]{:S(2)}, u32[]{:S(2)}) async-start(bf16[192,4,512]{2,0,1:T(8,128)(2,1)} %bitcast.195), calls=%async_computation.4 | async-start | bytes 1572864 | tf_op jit(solution)/shard_map/all_to_all | solution.py:1565
  758.9 67.0 %all-gather.12.cloned.1.call-start = ((), (), s32[]{:S(2)}) async-start(), calls=%async_computation.8 | async-start | bytes 1081344 | tf_op jit(solution)/shard_map/all_gather | solution.py:1612
  778.6 50.7 %collective-permute-start.115 = (bf16[768,512]{1,0:T(8,128)(2,1)}, bf16[768,512]{1,0:T(8,128)(2,1)}, u32[]{:S(2)}, u32[]{:S(2)}) collective-permute-start(bf16[768,512]{1,0:T(8,128)(2,1)} %get-tuple-element.578), channel_id=1, source_target_pairs={{0,1},{1,0},{2,3},{3,2},{4,5},{5,4},{6,7},{7,6},{8,9},{9,8},{10,11... | collective-permute-start | bytes 2359304 | tf_op jit(solution)/shard_map/ppermute | solution.py:394
  801.8 37.8 %all-to-all-start.5 = ((bf16[4,3,256,128]{3,2,1,0:T(8,128)(2,1)}), bf16[4,3,256,128]{3,2,1,0:T(8,128)(2,1)}, u32[]{:S(2)}, u32[]{:S(2)}) async-start(bf16[4,3,256,128]{3,2,1,0:T(8,128)(2,1)} %convert_add_fusion.4), calls=%async_computation.5 | async-start | bytes 1572864 | tf_op jit(solution)/shard_map/all_to_all | solution.py:506
  (183 other events, 2401.0 us)
Sparse Core Ops, SparseCore 0:
  141.2 116.4 all-gather.7
  586.0 71.5 all-gather.9
  763.2 56.2 all-gather.11

commit v5 on v4

--- a/solution.py
+++ b/solution.py
@@ -1567,12 +1567,13 @@
         len(arriving), *ahead_tie(firsts, first_parts, expand_grad, output_sum)
     )
     firsts.ready()
-    hidden, qkv_sum = firsts.tie(hidden, qkv_sum)
+    hidden, = firsts.tie(hidden)
     firsts.move()
     reduce_grad = weight_grad(
         hidden, [grad_out_slots], rank, reduce_rows, more=arrived[expand_count:]
     )
-    reduce_grad, layer_output = firsts.tie(reduce_grad, layer_output)
+    qkv_grad = exchange(qkv_sum.astype(bf16), "row")
+    reduce_grad, layer_output, qkv_grad = firsts.tie(reduce_grad, layer_output, qkv_grad)
     grad_first = firsts.total()
     grad_first = sum(term.astype(f32) for term in grad_first)
     grad_block = lax.dynamic_slice(
@@ -1595,8 +1596,7 @@
             output_sum, rank * output_rows, output_rows, 0
         ).astype(f32)
     )
-    qkv_grad = exchange(qkv_sum.astype(bf16), "row").transpose(2, 1, 0, 3)
-    qkv_grad = qkv_grad.reshape(1, qkv_rows, 3, col_width).astype(f32)
+    qkv_grad = qkv_grad.transpose(2, 1, 0, 3).reshape(1, qkv_rows, 3, col_width).astype(f32)
 
     def placed(term):
         return lax.dynamic_update_slice(jnp.zeros((D,), f32), term, (head_first,))

time: 865 us -> 864 us (level)
  waiting for transfers between devices: 168 us -> 154 us
  starting transfers between devices: 122 us -> 133 us
    ppermute x12, waiting for transfers between devices: 18 us -> 7.31 us  [move(): lax.ppermute(forth, PLANE, self.ring.clockwise)]
    unnamed x168 -> x166, local copies, waits for them, and re-layouts: 36.4 us -> 39.2 us
  transfers between devices with their start and end apart: 125 -> 125, of which waited for: 51 -> 50; matrix products, arithmetic and copies ran while one was open for 15% -> 15% of each run, Pallas kernels for 35% -> 35%
where the time goes in v5:
time: 864 us; the launch traced here: 852 us
  Pallas kernels  333 us (39%)
  waiting for transfers between devices  154 us (18%)
  starting transfers between devices  133 us (15%)
  local copies, waits for them, and re-layouts  79.6 us (9%)
  other arithmetic  50.8 us (6%)
  matrix products  43 us (5%)
  blocking collectives  41.3 us (5%)
  between operations  16.6 us (2%)
    pallas_call x2, Pallas kernels, run_experts(): pl.pallas_call(functools.partial(experts_kernel, count, first), grid_spec...  61.8 us
    pallas_call x7, Pallas kernels, weight_grad(): pl.pallas_call(functools.partial(weight_grad_kernel, sides, len(more), pi...  56.5 us
    pallas_call x10, Pallas kernels, place_blocks(): pl.pallas_call(kernel, grid_spec=pltpu.PrefetchScalarGridSpec(num_scalar_...  44.8 us
    all_to_all x1, blocking collectives, exchange(): return lax.all_to_all(pieces, axes, split_axis=0, concat_axis=0, tiled=True)  41.3 us
    unnamed x166, local copies, waits for them, and re-layouts  39.2 us
    pallas_call x9, Pallas kernels, step_sum(): pl.pallas_call(functools.partial(step_sum_kernel, (len(ahead), len(behind...  38.3 us
    ppermute x9, waiting for transfers between devices, gather_steps(): forth = lax.ppermute(forth, PLANE, self.clockwise)  32.4 us
    dot_general x3, matrix products, einsum(): return jnp.einsum(spec, a, b, preferred_element_type=f32)  26.9 us
  transfers between devices with their start and end apart: 125, of which 50 were waited for; matrix products, arithmetic and copies ran while one was open for 15% of the time, Pallas kernels for 35%

profile of v5, /device:TPU:0, one launch (start us, length us, event | category | flops | bytes accessed | tf_op | source)
XLA Modules:
  0.0 851.9 jit_solution(6631916269580110426)
XLA Ops:
  56.2 12.9 %all-to-all-done = bf16[4,1280,128]{2,1,0:T(8,128)(2,1)} async-done(((bf16[4,1280,128]{2,1,0:T(8,128)(2,1)}), bf16[4,1280,128]{2,1,0:T(8,128)(2,1)}, u32[]{:S(2)}, u32[]{:S(2)}) %all-to-all-start) | async-done | bytes 1310752 | tf_op jit(solution)/shard_map/all_to_all | solution.py:506
  82.5 8.6 %collective-permute-start.10 = (bf16[1024,512]{1,0:T(8,128)(2,1)}, bf16[1024,512]{1,0:T(8,128)(2,1)}, u32[]{:S(2)}, u32[]{:S(2)}) collective-permute-start(bf16[1024,512]{1,0:T(8,128)(2,1)} %collective-permute-done.2.refs_0_), channel_id=1, source_target_pairs={{0,4},{1,5},{4,8},{5,9},{8,12},{9,13},{12,14},{13,15},{14,10},{15,... | collective-permute-start | bytes 3145736 | tf_op jit(solution)/shard_map/ppermute | solution.py:340
  98.6 15.5 %collective-permute-done.10.refs_0_ = bf16[1024,512]{1,0:T(8,128)(2,1)} collective-permute-done((bf16[1024,512]{1,0:T(8,128)(2,1)}, bf16[1024,512]{1,0:T(8,128)(2,1)}, u32[]{:S(2)}, u32[]{:S(2)}) %collective-permute-start.10) | collective-permute-done | bytes 1048608 | tf_op jit(solution)/shard_map/ppermute | solution.py:340
  123.3 10.9 %collective-permute-done.15 = bf16[512,512]{1,0:T(8,128)(2,1)S(1)} collective-permute-done((bf16[512,512]{1,0:T(8,128)(2,1)S(1)}, bf16[512,512]{1,0:T(8,128)(2,1)S(1)}, u32[]{:S(2)}, u32[]{:S(2)}) %collective-permute-start.15) | collective-permute-done | bytes 524320 | tf_op jit(solution)/shard_map/ppermute | solution.py:348
  157.5 13.9 %norm_and_project.1 = (f32[3072,384]{1,0:T(8,128)}, f32[1,3072]{1,0:T(1,128)S(1)}, f32[2,3072]{1,0:T(2,128)S(1)}) custom-call(bf16[16,1024,512]{2,1,0:T(8,128)(2,1)} %place_blocks.14.x_ref.refs_1_.refs_3_.refs_4_.refs_7_.refs_8_, f32[1,2048]{1,0:T(1,128)S(1)} %get-tuple-element.592.gain_ref, bf16[2048,384]{1,0:T(8,128)(2,1)S(1)} %bitcast.206), custom_call_target="tpu_custom_call" | custom-call | flops 1540000000 | tf_op jit(solution)/shard_map/norm_and_project/pallas_call | solution.py:533
  196.9 13.1 %attention_forward.1 = (bf16[3072,128]{1,0:T(8,128)(2,1)S(1)}, f32[1,3072]{1,0:T(1,128)S(1)}) custom-call(s32[1]{0:T(128)S(6)} %copy.234.prefix_ref, bf16[3072,128]{1,0:T(8,128)(2,1)S(1)} %copy-done.45, bf16[3072,128]{1,0:T(8,128)(2,1)S(1)} %copy-done.47, bf16[128,3072]{1,0:T(8,128)(2,1)S(1)} %copy-done.51), custom_call_target="tpu_custom_call" | custom-call | flops 1870000000 | tf_op jit(solution)/shard_map/attention_forward/pallas_call | solution.py:105
  210.9 41.3 %all_to_all.44.refs_0_ = bf16[16,192,128]{2,1,0:T(8,128)(2,1)S(1)} all-to-all(bf16[16,192,128]{2,1,0:T(8,128)(2,1)S(1)} %bitcast.212), channel_id=1, replica_groups=mesh['dp'=2,'row'=4,'col'=4] {'col','row'}, dimensions={0} | all-to-all | bytes 1572864 | tf_op jit(solution)/shard_map/all_to_all | solution.py:506
  267.9 14.3 %cotangent_to_slots.1.up_ref = bf16[2,16,48,2048]{3,2,1,0:T(8,128)(2,1)} custom-call(bf16[16,96,192]{2,1,0:T(8,128)(2,1)} %copy.178.hits_ref.refs_16_, bf16[16,768,512]{2,1,0:T(8,128)(2,1)} %bitcast.238), custom_call_target="tpu_custom_call" | custom-call | flops 1540000000 | tf_op jit(solution)/shard_map/cotangent_to_slots/pallas_call | solution.py:775
  287.2 12.9 %fusion.26 = f32[2,768,1024]{2,1,0:T(8,128)} fusion(bf16[2,768,2048]{2,1,0:T(8,128)(2,1)} %bitcast.240, bf16[2,1024,2048]{2,1,0:T(8,128)(2,1)} %param.18), kind=kOutput, calls=%fused_computation.113 | convolution fusion | flops 6442450944 | bytes 20971520 | tf_op jit(solution)/shard_map/end,efd->enf/dot_general | solution.py:1162
  309.3 30.7 %experts.2 = (bf16[2,768,2048]{2,1,0:T(8,128)(2,1)}, bf16[2,768,1024]{2,1,0:T(8,128)(2,1)}, bf16[2,768,1024]{2,1,0:T(8,128)(2,1)}, bf16[2,768,1024]{2,1,0:T(8,12...) custom-call(s32[9]{0:T(128)} %stack.304.ids_ref, ...), custom_call_target="tpu_custom_call" | custom-call | flops 3190000128 | tf_op jit(solution)/shard_map/experts/pallas_call | solution.py:900
  354.6 31.0 %experts.3 = (bf16[2,768,2048]{2,1,0:T(8,128)(2,1)}, bf16[2,768,1024]{2,1,0:T(8,128)(2,1)}, bf16[2,768,1024]{2,1,0:T(8,128)(2,1)}, bf16[2,768,1024]{2,1,0:T(8,12...) custom-call(s32[9]{0:T(128)} %stack.260.ids_ref, ...), custom_call_target="tpu_custom_call", output_to_operand_aliasing={{0}: (22, {}), {1}: (23, {}), {2}: (24, {}), {3}: (25, {}),... | custom-call | flops 3190000128 | tf_op jit(solution)/shard_map/experts/pallas_call | solution.py:900
  391.8 7.9 weight_gradient.7
  412.5 11.9 %convolution_convert_fusion = bf16[2,768,2048]{2,1,0:T(8,128)(2,1)} fusion(bf16[2,768,1024]{2,1,0:T(8,128)(2,1)S(1)} %copy-done.3, bf16[2,1024,2048]{2,1,0:T(8,128)(2,1)} %param.18), kind=kOutput, calls=%fused_computation.2 | convolution fusion | flops 6445596672 | bytes 17825792 | tf_op jit(solution)/shard_map/enf,efd->end/dot_general | solution.py:1162
  441.7 18.3 %experts_combine.1 = (f32[16,2,192]{2,1,0:T(2,128)}, bf16[2,16,48,2048]{3,2,1,0:T(8,128)(2,1)S(1)}, bf16[8,192,2048]{2,1,0:T(8,128)(2,1)}, bf16[8,192,2048]{2,1,0:T(8,128)(2,1)}) custom-call(s32[16]{0:T(128)S(1)} %stack.305.ids_ref, s32[64]{0:T(128)S(1)} %copy-done.37, bf16[2,16,48,2048]{3,2,1,0:T(8,128)(2,1)} %bitcast.244, ...), custom_call_target="tpu_custom_call" | custom-call | flops 1980000000 | tf_op jit(solution)/shard_map/experts_combine/pallas_call | solution.py:965
  478.3 8.0 weight_gradient.8
  552.4 10.0 %weight_gradient.11.refs_6_ = f32[2,1024,2048]{2,1,0:T(8,128)} custom-call(s32[1]{0:T(128)} %bitcast.92.rank_ref, bf16[2,768,2048]{2,1,0:T(8,128)(2,1)} %get-tuple-element.493.left_ref, bf16[2,768,1024]{2,1,0:T(8,128)(2,1)} %get-tuple-element.318.refs_0_, bf16[2,768,1024]{2,1,0:T(8,128)(2,1)} %get-tuple-element.319.refs_1_, ...), custom_call_target="tpu_custom_call" | custom-call | flops 804571456 | tf_op jit(solution)/shard_map/weight_gradient/pallas_call | solution.py:1049
  575.4 7.9 collective-permute-done.77
  610.2 8.2 multiply_reduce_fusion
  618.5 22.6 %attention_backward.1 = (f32[3072,128]{1,0:T(8,128)S(1)}, f32[1,3072]{1,0:T(1,128)S(1)}, f32[3072,128]{1,0:T(8,128)S(1)}, f32[3072,128]{1,0:T(8,128)S(1)}, f32[1,3072]{1,0:T(1,128)S(1)}, /*index=5*/f32[1,3072]{1,0:T(1,128)S(1)}) custom-call(s32[1]{0:T(128)S(6)} %copy.234.prefix_ref, bf16[3072,128]{1,0:T(8,128)(2,1)S(1)} %copy-done.46, ...), custom_call_target="tpu_custom_call" | custom-call | flops 2640000000 | tf_op jit(solution)/shard_map/attention_backward/pallas_call | solution.py:192
  671.6 15.6 %projection_backward.1 = (bf16[3072,384]{1,0:T(8,128)(2,1)}, f32[2,128]{1,0:T(2,128)S(1)}, bf16[16,768,512]{2,1,0:T(8,128)(2,1)}) custom-call(f32[3072,128]{1,0:T(8,128)S(1)} %copy-done.21, f32[3072,128]{1,0:T(8,128)} %copy-done.22, f32[3072,128]{1,0:T(8,128)} %copy-done.23, f32[3072,384]{1,0:T(8,128)} %get-tuple-element.281.raw_ref, ...), custom_call_target="tpu_custom_call" | custom-call | flops 1704999936 | tf_op jit(solution)/shard_map/projection_backward/pallas_call | solution.py:1131
  735.6 15.7 %projection_weight_gradient.1 = (f32[4,3,512,128]{3,2,1,0:T(8,128)S(1)}, f32[1,2048]{1,0:T(1,128)S(1)}) custom-call(bf16[16,1024,512]{2,1,0:T(8,128)(2,1)} %place_blocks.14.x_ref.refs_1_.refs_3_.refs_4_.refs_7_.refs_8_, f32[1,2048]{1,0:T(1,128)S(1)} %copy-done.35, f32[1,3072]{1,0:T(1,128)S(1)} %get-tuple-element.481.inverse_ref, ...), custom_call_target="tpu_custom_call" | custom-call | flops 1650000000 | tf_op jit(solution)/shard_map/projection_weight_gradient/pallas_call | solution.py:591
  788.3 9.1 %weight_gradient.12 = f32[2,1024,2048]{2,1,0:T(8,128)} custom-call(s32[1]{0:T(128)} %bitcast.92.rank_ref, bf16[2,768,2048]{2,1,0:T(8,128)(2,1)} %get-tuple-element.493.left_ref, bf16[2,768,1024]{2,1,0:T(8,128)(2,1)} %get-tuple-element.318.refs_0_, bf16[2,768,1024]{2,1,0:T(8,128)(2,1)} %get-tuple-element.319.refs_1_, ...), custom_call_target="tpu_custom_call", output_to_operand_aliasing={{}: (8, {})} | custom-call | flops 804571456 | tf_op jit(solution)/shard_map/weight_gradient/pallas_call | solution.py:1049
  804.3 8.3 collective-permute-start.109
  819.5 11.6 %weight_gradient.13 = f32[2,512,2048]{2,1,0:T(8,128)} custom-call(s32[1]{0:T(128)} %bitcast.92.rank_ref, bf16[2,768,1024]{2,1,0:T(8,128)(2,1)} %get-tuple-element.509.left_ref, bf16[2,768,2048]{2,1,0:T(8,128)(2,1)} %bitcast.204, bf16[2,768,2048]{2,1,0:T(8,128)(2,1)} %bitcast.205, bf16[512,1024]{1,0:T(8,128)(2,1)S(1)} %copy-done.31, ...), custom_call_target="tpu_custom_call" | custom-call | flops 804571456 | tf_op jit(solution)/shard_map/weight_gradient/pallas_call | solution.py:1049
  (561 shorter events, 474.8 us)
Async XLA Ops:
  13.5 38.9 %collective-permute-start.6 = (bf16[1024,512]{1,0:T(8,128)(2,1)}, bf16[1024,512]{1,0:T(8,128)(2,1)}, u32[]{:S(2)}, u32[]{:S(2)}) collective-permute-start(bf16[1024,512]{1,0:T(8,128)(2,1)} %pad_maximum_fusion.3.refs_0_), channel_id=1, source_target_pairs={{0,1},{1,0},{2,3},{3,2},{4,5},{5,4},{6,7},{7,6},{8,9},{9,8},{10,11... | collective-permute-start | bytes 3145736 | tf_op jit(solution)/shard_map/ppermute | solution.py:334
  18.2 50.9 %all-to-all-start = ((bf16[4,1280,128]{2,1,0:T(8,128)(2,1)}), bf16[4,1280,128]{2,1,0:T(8,128)(2,1)}, u32[]{:S(2)}, u32[]{:S(2)}) async-start(bf16[4,1280,128]{2,1,0:T(8,128)(2,1)} %pad_maximum_fusion.2), calls=%async_computation | async-start | bytes 2621440 | tf_op jit(solution)/shard_map/all_to_all | solution.py:506
  23.1 244.8 %all-gather.8.cloned.1.call-start = ((), (), s32[]{:S(2)}) async-start(), calls=%async_computation.6 | async-start | bytes 13369344 | tf_op jit(solution)/shard_map/all_gather | solution.py:1301
  40.8 39.0 %collective-permute-start.2 = (bf16[1024,512]{1,0:T(8,128)(2,1)}, bf16[1024,512]{1,0:T(8,128)(2,1)}, u32[]{:S(2)}, u32[]{:S(2)}) collective-permute-start(bf16[1024,512]{1,0:T(8,128)(2,1)} %collective-permute-done.refs_0_), channel_id=1, source_target_pairs={{0,4},{1,5},{4,8},{5,9},{8,12},{9,13},{12,14},{13,15},{14,10},{15,... | collective-permute-start | bytes 3145736 | tf_op jit(solution)/shard_map/ppermute | solution.py:340
  47.5 34.5 %collective-permute-start.3 = (bf16[1024,512]{1,0:T(8,128)(2,1)}, bf16[1024,512]{1,0:T(8,128)(2,1)}, u32[]{:S(2)}, u32[]{:S(2)}) collective-permute-start(bf16[1024,512]{1,0:T(8,128)(2,1)} %collective-permute-done.1.refs_2_), channel_id=1, source_target_pairs={{0,2},{1,3},{4,0},{5,1},{8,4},{9,5},{12,8},{13,9},{14,12},{15,13},... | collective-permute-start | bytes 3145736 | tf_op jit(solution)/shard_map/ppermute | solution.py:341
  152.2 100.1 %collective-permute-start.24 = (bf16[8,256,512]{2,1,0:T(8,128)(2,1)}, bf16[8,256,512]{2,1,0:T(8,128)(2,1)}, u32[]{:S(2)}, u32[]{:S(2)}) collective-permute-start(bf16[8,256,512]{2,1,0:T(8,128)(2,1)} %bitcast.65), channel_id=1, source_target_pairs={{0,16},{16,0},{1,17},{17,1},{2,18},{18,2},{3,19},{19,3},{4,20},{20... | collective-permute-start | bytes 6291464 | tf_op jit(solution)/shard_map/ppermute | solution.py:1300
  267.9 41.4 %collective-permute-start.34 = (bf16[192,2048]{1,0:T(8,128)(2,1)S(1)}, bf16[192,2048]{1,0:T(8,128)(2,1)}, u32[]{:S(2)}, u32[]{:S(2)}) collective-permute-start(bf16[192,2048]{1,0:T(8,128)(2,1)S(1)} %get-tuple-element.291.refs_0_), channel_id=1, source_target_pairs={{0,1},{1,0},{2,3},{3,2},{4,5},{5,4},{6,7},{7,6},{8,9},{9,8},{10,11... | collective-permute-start | bytes 2359304 | tf_op jit(solution)/shard_map/ppermute | solution.py:334
  404.4 58.4 %collective-permute-start.56 = (bf16[512,1024]{1,0:T(8,128)(2,1)}, bf16[512,1024]{1,0:T(8,128)(2,1)}, u32[]{:S(2)}, u32[]{:S(2)}) collective-permute-start(bf16[512,1024]{1,0:T(8,128)(2,1)} %get-tuple-element.321), channel_id=1, source_target_pairs={{0,16},{16,0},{1,17},{17,1},{2,18},{18,2},{3,19},{19,3},{4,20},{20... | collective-permute-start | bytes 3145736 | tf_op jit(solution)/shard_map/ppermute | solution.py:1087
  424.4 38.3 %collective-permute-start.54 = (bf16[192,2048]{1,0:T(8,128)(2,1)}, bf16[192,2048]{1,0:T(8,128)(2,1)}, u32[]{:S(2)}, u32[]{:S(2)}) collective-permute-start(bf16[192,2048]{1,0:T(8,128)(2,1)} %get-tuple-element.364), channel_id=1, source_target_pairs={{0,1},{1,0},{2,3},{3,2},{4,5},{5,4},{6,7},{7,6},{8,9},{9,8},{10,11... | collective-permute-start | bytes 2359304 | tf_op jit(solution)/shard_map/ppermute | solution.py:394
  478.3 337.4 %all-gather.10.cloned.1.call-start = ((), (), s32[]{:S(2)}) async-start(), calls=%async_computation.7 | async-start | bytes 4325376 | tf_op jit(solution)/shard_map/all_gather | solution.py:1613
  499.2 47.1 %collective-permute-start.70 = (bf16[512,1024]{1,0:T(8,128)(2,1)}, bf16[512,1024]{1,0:T(8,128)(2,1)}, u32[]{:S(2)}, u32[]{:S(2)}) collective-permute-start(bf16[512,1024]{1,0:T(8,128)(2,1)} %copy-done.44), channel_id=1, source_target_pairs={{0,16},{16,0},{1,17},{17,1},{2,18},{18,2},{3,19},{19,3},{4,20},{20... | collective-permute-start | bytes 3145736 | tf_op jit(solution)/shard_map/ppermute | solution.py:1087
  552.0 41.0 %collective-permute-start.82 = (bf16[512,1024]{1,0:T(8,128)(2,1)S(1)}, bf16[512,1024]{1,0:T(8,128)(2,1)S(1)}, u32[]{:S(2)}, u32[]{:S(2)}) collective-permute-start(bf16[512,1024]{1,0:T(8,128)(2,1)S(1)} %copy-done.42), channel_id=1, source_target_pairs={{0,16},{16,0},{1,17},{17,1},{2,18},{18,2},{3,19},{19,3},{4,20},{20... | collective-permute-start | bytes 3145736 | tf_op jit(solution)/shard_map/ppermute | solution.py:1087
  597.8 48.6 %collective-permute-start.86 = (bf16[512,1024]{1,0:T(8,128)(2,1)}, bf16[512,1024]{1,0:T(8,128)(2,1)S(1)}, u32[]{:S(2)}, u32[]{:S(2)}) collective-permute-start(bf16[512,1024]{1,0:T(8,128)(2,1)} %get-tuple-element.392), channel_id=1, source_target_pairs={{0,16},{16,0},{1,17},{17,1},{2,18},{18,2},{3,19},{19,3},{4,20},{20... | collective-permute-start | bytes 3145736 | tf_op jit(solution)/shard_map/ppermute | solution.py:1087
  598.2 88.9 %collective-permute-start.93 = (bf16[512,1024]{1,0:T(8,128)(2,1)}, bf16[512,1024]{1,0:T(8,128)(2,1)S(1)}, u32[]{:S(2)}, u32[]{:S(2)}) collective-permute-start(bf16[512,1024]{1,0:T(8,128)(2,1)} %copy-done.39), channel_id=1, source_target_pairs={{0,16},{16,0},{1,17},{17,1},{2,18},{18,2},{3,19},{19,3},{4,20},{20... | collective-permute-start | bytes 3145736 | tf_op jit(solution)/shard_map/ppermute | solution.py:1087
  599.8 87.3 %collective-permute-start.94 = (bf16[512,1024]{1,0:T(8,128)(2,1)}, bf16[512,1024]{1,0:T(8,128)(2,1)}, u32[]{:S(2)}, u32[]{:S(2)}) collective-permute-start(bf16[512,1024]{1,0:T(8,128)(2,1)} %copy-done.38), channel_id=1, source_target_pairs={{0,16},{16,0},{1,17},{17,1},{2,18},{18,2},{3,19},{19,3},{4,20},{20... | collective-permute-start | bytes 3145736 | tf_op jit(solution)/shard_map/ppermute | solution.py:1087
  608.0 36.7 %collective-permute-start.84 = (bf16[192,2048]{1,0:T(8,128)(2,1)}, bf16[192,2048]{1,0:T(8,128)(2,1)S(1)}, u32[]{:S(2)}, u32[]{:S(2)}) collective-permute-start(bf16[192,2048]{1,0:T(8,128)(2,1)} %get-tuple-element.437), channel_id=1, source_target_pairs={{0,4},{1,5},{4,8},{5,9},{8,12},{9,13},{12,14},{13,15},{14,10},{15,... | collective-permute-start | bytes 2359304 | tf_op jit(solution)/shard_map/ppermute | solution.py:448
  609.4 35.3 %collective-permute-start.85 = (bf16[192,2048]{1,0:T(8,128)(2,1)}, bf16[192,2048]{1,0:T(8,128)(2,1)S(1)}, u32[]{:S(2)}, u32[]{:S(2)}) collective-permute-start(bf16[192,2048]{1,0:T(8,128)(2,1)} %get-tuple-element.438), channel_id=1, source_target_pairs={{0,2},{1,3},{4,0},{5,1},{8,4},{9,5},{12,8},{13,9},{14,12},{15,13},... | collective-permute-start | bytes 2359304 | tf_op jit(solution)/shard_map/ppermute | solution.py:449
  718.3 53.5 %collective-permute-start.111 = (bf16[512,1024]{1,0:T(8,128)(2,1)}, bf16[512,1024]{1,0:T(8,128)(2,1)}, u32[]{:S(2)}, u32[]{:S(2)}) collective-permute-start(bf16[512,1024]{1,0:T(8,128)(2,1)} %get-tuple-element.412), channel_id=1, source_target_pairs={{0,16},{16,0},{1,17},{17,1},{2,18},{18,2},{3,19},{19,3},{4,20},{20... | collective-permute-start | bytes 3145736 | tf_op jit(solution)/shard_map/ppermute | solution.py:1087
  721.6 37.7 %collective-permute-start.102 = (bf16[768,512]{1,0:T(8,128)(2,1)}, bf16[768,512]{1,0:T(8,128)(2,1)}, u32[]{:S(2)}, u32[]{:S(2)}) collective-permute-start(bf16[768,512]{1,0:T(8,128)(2,1)} %get-tuple-element.582), channel_id=1, source_target_pairs={{0,1},{1,0},{2,3},{3,2},{4,5},{5,4},{6,7},{7,6},{8,9},{9,8},{10,11... | collective-permute-start | bytes 2359304 | tf_op jit(solution)/shard_map/ppermute | solution.py:394
  726.8 34.9 %collective-permute-start.103 = (bf16[768,512]{1,0:T(8,128)(2,1)}, bf16[768,512]{1,0:T(8,128)(2,1)}, u32[]{:S(2)}, u32[]{:S(2)}) collective-permute-start(bf16[768,512]{1,0:T(8,128)(2,1)} %get-tuple-element.581), channel_id=1, source_target_pairs={{0,1},{1,0},{2,3},{3,2},{4,5},{5,4},{6,7},{7,6},{8,9},{9,8},{10,11... | collective-permute-start | bytes 2359304 | tf_op jit(solution)/shard_map/ppermute | solution.py:394
  759.2 73.7 %all-gather.12.cloned.1.call-start = ((), (), s32[]{:S(2)}) async-start(), calls=%async_computation.8 | async-start | bytes 1081344 | tf_op jit(solution)/shard_map/all_gather | solution.py:1612
  761.7 35.7 %collective-permute-start.107 = (bf16[768,512]{1,0:T(8,128)(2,1)}, bf16[768,512]{1,0:T(8,128)(2,1)}, u32[]{:S(2)}, u32[]{:S(2)}) collective-permute-start(bf16[768,512]{1,0:T(8,128)(2,1)} %get-tuple-element.580), channel_id=1, source_target_pairs={{0,1},{1,0},{2,3},{3,2},{4,5},{5,4},{6,7},{7,6},{8,9},{9,8},{10,11... | collective-permute-start | bytes 2359304 | tf_op jit(solution)/shard_map/ppermute | solution.py:394
  761.8 35.6 %collective-permute-start.108 = (bf16[768,512]{1,0:T(8,128)(2,1)}, bf16[768,512]{1,0:T(8,128)(2,1)}, u32[]{:S(2)}, u32[]{:S(2)}) collective-permute-start(bf16[768,512]{1,0:T(8,128)(2,1)} %get-tuple-element.579), channel_id=1, source_target_pairs={{0,1},{1,0},{2,3},{3,2},{4,5},{5,4},{6,7},{7,6},{8,9},{9,8},{10,11... | collective-permute-start | bytes 2359304 | tf_op jit(solution)/shard_map/ppermute | solution.py:394
  781.0 54.0 %all-to-all-start.5 = ((bf16[4,3,256,128]{3,2,1,0:T(8,128)(2,1)}), bf16[4,3,256,128]{3,2,1,0:T(8,128)(2,1)S(1)}, u32[]{:S(2)}, u32[]{:S(2)}) async-start(bf16[4,3,256,128]{3,2,1,0:T(8,128)(2,1)} %add_convert_fusion), calls=%async_computation.5 | async-start | bytes 1572864 | tf_op jit(solution)/shard_map/all_to_all | solution.py:506
  (182 other events, 2391.4 us)
Sparse Core Ops, SparseCore 0:
  141.2 116.4 all-gather.7
  586.3 71.3 all-gather.9
  763.5 65.9 all-gather.11
